TPU v7x, 32 devices: a whole 2x2x4 slice. The times are simulated.
32 devices in a mesh: row: 4 (over y, core), col: 8 (over z, x).
Axes of the slice: x: 2, y: 2, z: 4, core: 2. Of those that a mesh axis runs over, the one named last changes fastest.
Arguments:
- amps: bfloat16 [512, 64, 256], P('row', 'col'), may hold values from -6 to 6
- ints: bfloat16 [2048, 256, 256], P(('row', 'col')), may hold values from -0.046875 to 0.046875
- task_cd: int32 [2048], P(('row', 'col')), may hold values from 0 to 7, as said below
- task_ab: int32 [2048], P(('row', 'col')), may hold values from 0 to 7
- task_count: int32 [32], P(('row', 'col')), may hold values from 8 to 64, as said below
Outputs:
- residual: bfloat16 [512, 32, 256], P('col', 'row')
Inputs may be any that keep to these rules, and one draw needn't show every extreme that they name: On each device the slots name distinct (task_cd, task_ab) pairs. The live slots of a device are its first task_count ones; some device has all 64 slots live in every draw.
All inputs are finite; a program needn't handle non-finite values.
Results may differ from a plain program's by a relative error of at most 0.001.
Values may be sent and summed in bfloat16 or wider, within the bound.
No kernel may reach another device: no remote copies, remote signals or barrier semaphores. Data moves between devices by JAX's collectives and lax.ppermute only.
A program may use at most 128 MiB of HBM per device.

v0:
```python
import jax
import jax.numpy as jnp
from jax import lax
from jax.sharding import PartitionSpec as P

CD_COL = 8
PAIR_TILES_ROW = 8


def dense_tiles(ints, task_cd, task_ab, count):
    slots = ints.shape[0]
    order = jnp.arange(slots, dtype=jnp.int32)
    live = order < count
    wanted = jnp.arange(PAIR_TILES_ROW * CD_COL, dtype=jnp.int32)[:, None]
    slot_key = task_ab * CD_COL + task_cd
    match = (slot_key[None, :] == wanted) & live[None, :]
    found = jnp.sum(jnp.where(match, order[None, :], 0), axis=1)
    present_mask = jnp.any(match, axis=1)
    table = jnp.take(ints, found, axis=0) * present_mask.astype(ints.dtype)[:, None, None]
    return table.reshape(PAIR_TILES_ROW, CD_COL, ints.shape[1], ints.shape[2])


def ladder_term(rows_amps, table):
    return jnp.einsum("nkt,aktu->nau", rows_amps, table, preferred_element_type=jnp.float32)


def shards(amps, ints, task_cd, task_ab, task_count):
    whole = lax.all_gather(amps, "row", axis=0, tiled=True)
    table = dense_tiles(ints, task_cd, task_ab, task_count[0])
    partial_sum = ladder_term(whole, table)
    summed = lax.psum_scatter(partial_sum, "col", scatter_dimension=0, tiled=True)
    return summed.astype(jnp.bfloat16)


def solution(mesh):
    return jax.shard_map(
        shards,
        mesh=mesh,
        in_specs=(
            P("row", "col", None),
            P(("row", "col"), None, None),
            P(("row", "col")),
            P(("row", "col")),
            P(("row", "col")),
        ),
        out_specs=P("col", "row", None),
        check_vma=False,
    )
```

profile of v0, /device:TPU:0, one launch (start us, length us, event | category | flops | bytes accessed | tf_op | source)
XLA Modules:
  0.0 147.1 jit_solution(8629862842809781432)
XLA Ops:
  6.5 0.0 all-gather.2.cloned.1.call-start
  6.5 1.9 %copy.13 = bf16[128,8,256]{2,0,1:T(8,128)(2,1)} copy(bf16[128,8,256]{2,1,0:T(8,128)(2,1)} %param.5) | data formatting | bytes 1048576 | tf_op args[0]
  8.5 0.0 all-gather.2.cloned.1.call-update
  8.5 0.0 reduce-scatter.2.cloned.1.call-start
  9.2 0.7 multiply_add_fusion
  9.9 0.1 select_reduce_fusion
  10.0 0.1 reduce_sum.14
  10.1 9.0 %gather_fusion = bf16[64,256,256]{2,1,0:T(8,128)(2,1)} fusion(bf16[64,256,256]{2,1,0:T(8,128)(2,1)} %param.6, s32[1024]{0:T(1024)S(1)} %pad_clamp_fusion), kind=kCustom, calls=%fused_computation | custom fusion | bytes 16777472 | tf_op jit(solution)/shard_map/jit(_take)/gather | solution.py:19
  19.1 11.5 %copy.12 = bf16[8,8,256,256]{2,3,1,0:T(8,128)(2,1)} copy(bf16[8,8,256,256]{3,2,1,0:T(8,128)(2,1)} %bitcast.15) | data formatting | bytes 16777216 | tf_op jit(solution)/shard_map/jit(_take)/gather | solution.py:19
  30.6 0.1 fusion.11
  30.7 0.1 reshape.35
  30.8 3.4 %all-gather.2.cloned.1.call-done = bf16[512,8,256]{2,0,1:T(8,128)(2,1)} async-done(((bf16[128,8,256]{2,0,1:T(8,128)(2,1)}), bf16[512,8,256]{2,0,1:T(8,128)(2,1)}) %all-gather.2.cloned.1.call-update) | async-done | bytes 2097168 | tf_op jit(solution)/shard_map/all_gather | solution.py:28
  34.2 10.5 %fusion.6 = f32[512,8,256]{0,2,1:T(8,128)} fusion(bf16[8,8,256,256]{2,3,1,0:T(8,128)(2,1)} %copy.12, pred[8,8]{1,0:T(8,128)(4,1)S(1)} %compare_and_fusion, bf16[8,8]{1,0:T(8,128)(2,1)S(1)} %reshape.35, bf16[512,8,256]{2,0,1:T(8,128)(2,1)} %all-gather.2.cloned.1.call-done), kind=kOutput, calls=%fused_computation.7 | convolution fusion | flops 4303355904 | bytes 14680256 | tf_op jit(solution)/shard_map/nkt,aktu->nau/dot_general | solution.py:24
  44.8 5.4 %copy.14 = f32[512,8,256]{2,1,0:T(8,128)} copy(f32[512,8,256]{0,2,1:T(8,128)} %fusion.6) | data formatting | bytes 8388608 | tf_op jit(solution)/shard_map/nkt,aktu->nau/dot_general | solution.py:24
  50.2 0.0 reduce-scatter.2.cloned.1.call-update
  50.2 88.2 %reduce-scatter.2.cloned.1.call-done = f32[64,8,256]{2,1,0:T(8,128)} async-done(((f32[512,8,256]{2,1,0:T(8,128)}), f32[64,8,256]{2,1,0:T(8,128)}) %reduce-scatter.2.cloned.1.call-update) | async-done | bytes 524304 | tf_op jit(solution)/shard_map/reduce_scatter | solution.py:31
  138.5 1.8 %convert_element_type.15 = bf16[64,8,256]{2,1,0:T(8,128)(2,1)} convert(f32[64,8,256]{2,1,0:T(8,128)} %reduce-scatter.2.cloned.1.call-done) | non-fusion elementwise | flops 131072 | bytes 786432 | tf_op jit(solution)/shard_map/convert_element_type | solution.py:32
  (5 shorter events, 0.0 us)
Async XLA Ops:
  6.5 27.7 %all-gather.2.cloned.1.call-start = ((), (), s32[]{:S(2)}) async-start(), calls=%async_computation.1 | async-start | bytes 2621440 | tf_op jit(solution)/shard_map/all_gather | solution.py:28
  8.5 130.0 %reduce-scatter.2.cloned.1.call-start = ((), (), s32[]{:S(2)}) async-start(), calls=%async_computation.2 | async-start | bytes 4718592 | tf_op jit(solution)/shard_map/reduce_scatter | solution.py:31
Sparse Core Ops, SparseCore 0:
  8.9 25.2 all-gather.1
  50.3 88.0 reduce-scatter.1
where the time goes:
time: 148 us; the launch traced here: 147 us
  waiting for transfers between devices  91.7 us (62%)
  local copies, waits for them, and re-layouts  28 us (19%)
  between operations  14.1 us (10%)
  matrix products  10.5 us (7%)
  other arithmetic  2.71 us (2%)
    reduce_scatter x1, waiting for transfers between devices, shards(): lax.psum_scatter(partial_sum, 'col', scatter_dimension=0, tiled=True)  88.2 us
    gather x2, local copies, waits for them, and re-layouts, dense_tiles(): jnp.take(ints, found, axis=0)  20.5 us
    dot_general x1, matrix products, ladder_term(): jnp.einsum('nkt,aktu->nau', rows_amps, table, preferred_element_type=jnp....  10.5 us
    dot_general x1, local copies, waits for them, and re-layouts, ladder_term(): jnp.einsum('nkt,aktu->nau', rows_amps, table, preferred_element_type=jnp....  5.44 us
    all_gather x1, waiting for transfers between devices, shards(): whole = lax.all_gather(amps, 'row', axis=0, tiled=True)  3.42 us
  transfers between devices with their start and end apart: 2, of which 2 were waited for; matrix products, arithmetic and copies ran while one was open for 15% of the time, Pallas kernels for 0%

commit v1 on v0

v1 whole, which is shorter than its diff:
```python
import functools

import jax
import jax.numpy as jnp
from jax import lax
from jax.experimental import pallas as pl
from jax.experimental.pallas import tpu as pltpu
from jax.sharding import PartitionSpec as P

CD_COL = 8
PAIR_TILES_ROW = 8
CHUNKS = 2
LANES = 128
LEVELS = 32000.0
STEPS = 64.0
SMALLEST = 2.0**-110
VMEM_LIMIT = 48 * 1024 * 1024

F32 = jnp.float32
BF16 = jnp.bfloat16
I16 = jnp.int16

IN_VMEM = pl.BlockSpec(memory_space=pltpu.VMEM)
IN_SMEM = pl.BlockSpec(memory_space=pltpu.SMEM)
IN_HBM = pl.BlockSpec(memory_space=pl.ANY)


def held(x):
    return pltpu.with_memory_space_constraint(x, pltpu.VMEM)


def kernel_call(body, outs, ins, scratch=(), flops=0, moved=0, name=None):
    return pl.pallas_call(
        body,
        out_shape=outs,
        in_specs=ins,
        out_specs=jax.tree.map(lambda _: IN_VMEM, outs),
        scratch_shapes=list(scratch),
        compiler_params=pltpu.CompilerParams(vmem_limit_bytes=VMEM_LIMIT),
        cost_estimate=pl.CostEstimate(flops=flops, bytes_accessed=moved, transcendentals=0),
        name=name,
    )


def code(block):
    top = jnp.maximum(jnp.max(jnp.abs(block), axis=0, keepdims=True), SMALLEST)
    exponent = jnp.ceil(jnp.log2(top) * STEPS)
    scaled = block * (LEVELS * jnp.exp2(exponent * (-1.0 / STEPS)))
    return jnp.round(scaled).astype(jnp.int32).astype(I16), exponent


def store_exponents(ref, at, rows):
    tiles = len(rows)
    block = jnp.concatenate(list(rows) + [jnp.zeros_like(rows[0])] * (16 - tiles), axis=0)
    ref[at] = block.astype(jnp.int32).astype(I16)


def scales(exponents):
    return jnp.exp2(exponents.astype(jnp.int32).astype(F32) * (1.0 / STEPS)) * (1.0 / LEVELS)


def decode(block, scale):
    return block.astype(jnp.int32).astype(F32) * scale


def split_kernel(parts, here_ref, amps_ref, *refs):
    outs, flat = refs[:-1], refs[-1]
    rows, tiles, width = amps_ref.shape
    chunks, each = len(outs), outs[0].shape[2]
    lanes = flat.shape[2]
    for half in range(width // lanes):
        columns = pl.ds(half * lanes, lanes)
        flat[half] = amps_ref[:, :, columns].astype(F32).reshape(rows * tiles, lanes)
    for step in range(parts):
        part = lax.rem(here_ref[0] + step, parts)
        for chunk in range(chunks):
            for tile in range(tiles):
                first = (part * (rows // parts) + chunk * each) * tiles + tile
                for half in range(width // lanes):
                    picked = flat[half, pl.ds(first, each, stride=tiles), :]
                    outs[chunk][step, tile, :, pl.ds(half * lanes, lanes)] = picked.astype(BF16)


def table_kernel(cd_ref, ab_ref, count_ref, ints_ref, table_ref, present, sems):
    slots = cd_ref.shape[0]
    pairs = present.shape[0]
    count = count_ref[0]

    def copy(slot):
        place = ab_ref[slot] * CD_COL + cd_ref[slot]
        return pltpu.make_async_copy(ints_ref.at[slot], table_ref.at[place], sems.at[slot])

    def clear(pair, carry):
        present[pair] = 0
        return carry

    def start(slot, carry):
        copy(slot).start()
        present[ab_ref[slot] * CD_COL + cd_ref[slot]] = 1
        return carry

    def fill(pair, carry):
        @pl.when(present[pair] == 0)
        def _():
            table_ref[pair] = jnp.zeros(table_ref.shape[1:], table_ref.dtype)

        return carry

    def finish(slot, carry):
        copy(slot).wait()
        return carry

    lax.fori_loop(0, pairs, clear, 0)
    lax.fori_loop(0, count, start, 0)
    lax.fori_loop(0, pairs, fill, 0)
    lax.fori_loop(0, count, finish, 0)


def product_kernel(blocks, *refs):
    amps_refs, table_ref = refs[:blocks], refs[blocks]
    parts, tiles, each, width = amps_refs[0].shape
    keep_ref = refs[blocks + 1]
    send_refs = refs[blocks + 2 : blocks + 1 + parts]
    left = refs[-1]
    ab_tiles = table_ref.shape[0] // tiles
    for tile in range(tiles):
        for block in range(blocks):
            for part in range(parts):
                at = (block * parts + part) * each
                left[at : at + each, tile * width : (tile + 1) * width] = amps_refs[block][part, tile]
    exponents = {}
    for ab in range(ab_tiles):
        right = table_ref[ab * tiles : (ab + 1) * tiles].reshape(tiles * width, table_ref.shape[2])
        total = jnp.dot(left[...], right, preferred_element_type=F32)
        for block in range(blocks):
            for part in range(parts):
                at = (block * parts + part) * each
                piece = total[at : at + each]
                if part == 0:
                    keep_ref[block, ab] = piece
                else:
                    coded, exponent = code(piece)
                    send_refs[part - 1][block, ab * each : (ab + 1) * each] = coded
                    exponents.setdefault((block, part), []).append(exponent)
    for (block, part), rows in exponents.items():
        store_exponents(send_refs[part - 1].at[block], pl.ds(ab_tiles * each, 16), rows)


def pair_kernel(places_ref, keep_ref, *refs):
    blocks, ab_tiles, each, width = keep_ref.shape
    received = refs[: len(refs) - blocks]
    own_ref, send_refs = refs[len(received)], refs[len(received) + 1 :]
    for step in range(blocks):
        block = places_ref[step]
        factors = [scales(ref[block, pl.ds(ab_tiles * each, 16)]) for ref in received]
        exponents = []
        for ab in range(ab_tiles):
            total = keep_ref[block, ab]
            for ref, factor in zip(received, factors):
                total = total + decode(ref[block, ab * each : (ab + 1) * each], factor[ab : ab + 1])
            if step == 0:
                own_ref[ab] = total
            else:
                coded, exponent = code(total)
                send_refs[step - 1][ab * each : (ab + 1) * each] = coded
                exponents.append(exponent)
        if step:
            store_exponents(send_refs[step - 1], pl.ds(ab_tiles * each, 16), exponents)


def last_kernel(chunks, *refs):
    flat, out_ref = refs[-1], refs[-2]
    per = (len(refs) - 2) // chunks
    rows, ab_tiles, width = out_ref.shape
    lanes = flat.shape[2]
    for chunk in range(chunks):
        own_ref, received = refs[chunk * per], refs[chunk * per + 1 : (chunk + 1) * per]
        each = own_ref.shape[1]
        factors = [scales(ref[pl.ds(ab_tiles * each, 16)]) for ref in received]
        for ab in range(ab_tiles):
            total = own_ref[ab]
            for ref, factor in zip(received, factors):
                total = total + decode(ref[ab * each : (ab + 1) * each], factor[ab : ab + 1])
            for half in range(width // lanes):
                piece = total[:, half * lanes : (half + 1) * lanes]
                flat[half, pl.ds(chunk * each * ab_tiles + ab, each, stride=ab_tiles), :] = piece
    for half in range(width // lanes):
        whole = flat[half].reshape(rows, ab_tiles, lanes)
        out_ref[:, :, pl.ds(half * lanes, lanes)] = whole.astype(out_ref.dtype)


def shards(n_row, n_col, amps, ints, task_cd, task_ab, task_count):
    n_x = n_col // n_row
    n_z = n_row
    n_y = n_row // 2
    rows, tiles, width = amps.shape
    out_rows = rows // n_x
    each = out_rows // CHUNKS
    row, col = lax.axis_index("row"), lax.axis_index("col")
    x, z = lax.rem(col, n_x), lax.div(col, n_x)

    def along_row(array, pairs):
        return lax.ppermute(array, "row", pairs)

    def along_x(array, step):
        pairs = [(c, c - c % n_x + (c % n_x + step) % n_x) for c in range(n_col)]
        return lax.ppermute(array, "col", pairs)

    def along_z(array, step):
        return lax.ppermute(array, "col", [(c, (c + step * n_x) % n_col) for c in range(n_col)])

    swap = [(r, r ^ 1) for r in range(n_row)]

    mine = kernel_call(
        functools.partial(split_kernel, n_x),
        [jax.ShapeDtypeStruct((n_x, tiles, each, width), BF16)] * CHUNKS,
        [IN_SMEM, IN_VMEM],
        [pltpu.VMEM((width // LANES, rows * tiles, LANES), F32)],
        name="split",
    )(x[None], amps)
    others = [
        [along_row(mine[q], [(r, (r + 2 * k) % n_row) for r in range(n_row)]) for k in range(1, n_y)]
        for q in range(CHUNKS)
    ]
    beside = [along_row(mine[q], swap) for q in range(CHUNKS)]
    pairs = PAIR_TILES_ROW * CD_COL
    table = pl.pallas_call(
        table_kernel,
        out_shape=pltpu.VMEM((pairs, width, ints.shape[2]), BF16),
        in_specs=[IN_SMEM, IN_SMEM, IN_SMEM, IN_HBM],
        out_specs=IN_VMEM,
        scratch_shapes=[pltpu.SMEM((pairs,), jnp.int32), pltpu.SemaphoreType.DMA((ints.shape[0],))],
        compiler_params=pltpu.CompilerParams(vmem_limit_bytes=VMEM_LIMIT),
        cost_estimate=pl.CostEstimate(flops=0, bytes_accessed=ints.size * 2, transcendentals=0),
        name="table",
    )(task_cd, task_ab, task_count, ints)

    places = []
    for step in range(n_z):
        wanted = lax.rem(z + step, n_z)
        far = lax.rem(row // 2 - wanted // 2 + n_y, n_y)
        places.append(2 * far + lax.rem(row + wanted, 2))
    places = jnp.stack(places).astype(jnp.int32)

    coded_rows = PAIR_TILES_ROW * each + 16
    last = []
    for q in range(CHUNKS):
        blocks = [mine[q], beside[q]]
        for other in others[q]:
            blocks += [other, along_row(other, swap)]
        keep, *sends = kernel_call(
            functools.partial(product_kernel, n_row),
            [jax.ShapeDtypeStruct((n_row, PAIR_TILES_ROW, each, width), F32)]
            + [jax.ShapeDtypeStruct((n_row, coded_rows, width), I16)] * (n_x - 1),
            [IN_VMEM] * (n_row + 1),
            [pltpu.VMEM((n_row * n_x * each, tiles * width), BF16)],
            flops=2 * n_row * n_x * each * tiles * width * PAIR_TILES_ROW * width,
            moved=0,
            name="product",
        )(*blocks, held(table))
        received = [along_x(send, step) for step, send in zip(range(1, n_x), sends)]
        own, *sends = kernel_call(
            pair_kernel,
            [jax.ShapeDtypeStruct((PAIR_TILES_ROW, each, width), F32)]
            + [jax.ShapeDtypeStruct((coded_rows, width), I16)] * (n_z - 1),
            [IN_SMEM] + [IN_VMEM] * n_x,
            name="pairs",
        )(places, keep, *received)
        last += [own] + [along_z(send, step) for step, send in zip(range(1, n_z), sends)]
    return kernel_call(
        functools.partial(last_kernel, CHUNKS),
        jax.ShapeDtypeStruct((out_rows, PAIR_TILES_ROW, width), BF16),
        [IN_VMEM] * len(last),
        [pltpu.VMEM((width // LANES, out_rows * PAIR_TILES_ROW, LANES), F32)],
        name="last",
    )(*last)


def solution(mesh):
    return jax.shard_map(
        functools.partial(shards, mesh.shape["row"], mesh.shape["col"]),
        mesh=mesh,
        in_specs=(
            P("row", "col", None),
            P(("row", "col"), None, None),
            P(("row", "col")),
            P(("row", "col")),
            P(("row", "col")),
        ),
        out_specs=P("col", "row", None),
        check_vma=False,
    )
```

time: 148 us -> 72.7 us (0.49)
  the two profiles are of different devices: /device:TPU:0 before, /device:TPU:12 now
where the time goes in v1:
time: 72.7 us; the launch traced here: 72.5 us
  waiting for transfers between devices  35 us (48%)
  Pallas kernels  16.4 us (23%)
  starting transfers between devices  15.2 us (21%)
  local copies, waits for them, and re-layouts  5.06 us (7%)
  between operations  0.78 us (1%)
    ppermute x6, waiting for transfers between devices, along_z(): lax.ppermute(array, 'col', [(c, (c + step * n_x) % n_col) for c in range(...  12.2 us
    ppermute x2, waiting for transfers between devices, along_x(): return lax.ppermute(array, 'col', pairs)  11.7 us
    ppermute x6, waiting for transfers between devices, along_row(): return lax.ppermute(array, 'row', pairs)  11.1 us
    ppermute x6, starting transfers between devices, along_z(): lax.ppermute(array, 'col', [(c, (c + step * n_x) % n_col) for c in range(...  10.6 us
    pallas_call x2, Pallas kernels, shards(): kernel_call(functools.partial(product_kernel, n_row), [jax.ShapeDtypeStru...  9.34 us
    unnamed x22, local copies, waits for them, and re-layouts  5.06 us
    pallas_call x1, Pallas kernels, shards(): pl.pallas_call(table_kernel, out_shape=pltpu.VMEM((pairs, width, ints.sha...  3.92 us
    ppermute x6, starting transfers between devices, along_row(): return lax.ppermute(array, 'row', pairs)  2.61 us
  transfers between devices with their start and end apart: 14, of which 7 were waited for; matrix products, arithmetic and copies ran while one was open for 0% of the time, Pallas kernels for 21%

profile of v1, /device:TPU:12, one launch (start us, length us, event | category | flops | bytes accessed | tf_op | source)
XLA Modules:
  0.0 72.5 jit_solution(2809039403101823061)
XLA Ops:
  0.0 1.0 %copy-done.2 = bf16[128,8,256]{2,1,0:T(8,128)(2,1)S(1)} copy-done((bf16[128,8,256]{2,1,0:T(8,128)(2,1)S(1)}, bf16[128,8,256]{2,1,0:T(8,128)(2,1)}, u32[]{:S(2)}) %copy-start.2) | copy-done | bytes 524312
  1.0 0.3 split.1
  1.3 0.0 copy-start.3
  1.3 0.0 copy-start.4
  1.4 0.6 collective-permute-start.8
  1.9 1.5 %collective-permute-start.1 = (bf16[2,8,32,256]{3,2,1,0:T(8,128)(2,1)S(1)}, bf16[2,8,32,256]{3,2,1,0:T(8,128)(2,1)S(1)}, u32[]{:S(2)}, u32[]{:S(2)}) collective-permute-start(bf16[2,8,32,256]{3,2,1,0:T(8,128)(2,1)S(1)} %get-tuple-element.19.refs_0_), channel_id=1, source_target_pairs={{0,16},{8,24},{16,0},{24,8},{1,17},{9,25},{17,1},{25,9},{2,18},{10... | collective-permute-start | bytes 786440 | tf_op jit(solution)/shard_map/ppermute | solution.py:203
  3.4 0.0 collective-permute-start.7
  3.4 7.2 %collective-permute-done.8.refs_2_ = bf16[2,8,32,256]{3,2,1,0:T(8,128)(2,1)S(1)} collective-permute-done((bf16[2,8,32,256]{3,2,1,0:T(8,128)(2,1)S(1)}, bf16[2,8,32,256]{3,2,1,0:T(8,128)(2,1)S(1)}, u32[]{:S(2)}, u32[]{:S(2)}) %collective-permute-start.8) | collective-permute-done | bytes 262176 | tf_op jit(solution)/shard_map/ppermute | solution.py:203
  10.6 0.0 collective-permute-start.9
  10.6 0.5 collective-permute-start
  11.1 4.0 %collective-permute-done.1.refs_2_ = bf16[2,8,32,256]{3,2,1,0:T(8,128)(2,1)S(1)} collective-permute-done((bf16[2,8,32,256]{3,2,1,0:T(8,128)(2,1)S(1)}, bf16[2,8,32,256]{3,2,1,0:T(8,128)(2,1)S(1)}, u32[]{:S(2)}, u32[]{:S(2)}) %collective-permute-start.1) | collective-permute-done | bytes 262176 | tf_op jit(solution)/shard_map/ppermute | solution.py:203
  15.1 0.0 collective-permute-start.2
  15.7 3.9 %table.1.refs_4_ = bf16[64,256,256]{2,1,0:T(8,128)(2,1)S(1)} custom-call(s32[64]{0:T(128)} %cd_ref.1, s32[64]{0:T(128)} %ab_ref.1, s32[1]{0:T(128)S(6)} %copy.6.count_ref, bf16[64,256,256]{2,1,0:T(8,128)(2,1)} %ints_ref.1), custom_call_target="tpu_custom_call" | custom-call | bytes 8388608 | tf_op jit(solution)/shard_map/table/pallas_call | solution.py:227
  19.7 0.0 copy-done.3
  19.7 0.0 copy-done.4
  19.7 0.0 copy-done.6
  19.7 0.0 copy-done.5
  19.7 0.0 collective-permute-done.7.refs_1_
  19.7 0.0 collective-permute-done.9.refs_3_
  19.7 0.7 copy-done.8
  20.4 0.7 copy-done.10
  21.1 4.7 %product.3 = (f32[4,8,32,256]{3,2,1,0:T(8,128)}, s16[4,272,256]{2,1,0:T(8,128)(2,1)}) custom-call(bf16[2,8,32,256]{3,2,1,0:T(8,128)(2,1)} %copy-done.4, bf16[2,8,32,256]{3,2,1,0:T(8,128)(2,1)} %copy-done.8, bf16[2,8,32,256]{3,2,1,0:T(8,128)(2,1)} %copy-done.6, bf16[2,8,32,256]{3,2,1,0:T(8,128)(2,1)} %copy-done.10, bf16[64,256,256]{2,1,0:T(8,128)(2,1)S(1)} %table.1.refs_4_), custom_call_target="tpu_custom_call" | custom-call | flops 2147483648 | tf_op jit(solution)/shard_map/product/pallas_call | solution.py:251
  25.8 0.5 collective-permute-start.10
  26.3 0.0 collective-permute-done.refs_1_
  26.3 0.0 collective-permute-done.2.refs_3_
  26.3 0.7 copy-done.7
  27.0 0.7 copy-done.9
  27.7 4.7 %product.2 = (f32[4,8,32,256]{3,2,1,0:T(8,128)}, s16[4,272,256]{2,1,0:T(8,128)(2,1)}) custom-call(bf16[2,8,32,256]{3,2,1,0:T(8,128)(2,1)} %copy-done.3, bf16[2,8,32,256]{3,2,1,0:T(8,128)(2,1)} %copy-done.7, bf16[2,8,32,256]{3,2,1,0:T(8,128)(2,1)} %copy-done.5, bf16[2,8,32,256]{3,2,1,0:T(8,128)(2,1)} %copy-done.9, bf16[64,256,256]{2,1,0:T(8,128)(2,1)S(1)} %table.1.refs_4_), custom_call_target="tpu_custom_call" | custom-call | flops 2147483648 | tf_op jit(solution)/shard_map/product/pallas_call | solution.py:251
  32.4 1.5 %collective-permute-start.3 = (s16[4,272,256]{2,1,0:T(8,128)(2,1)}, s16[4,272,256]{2,1,0:T(8,128)(2,1)S(1)}, u32[]{:S(2)}, u32[]{:S(2)}) collective-permute-start(s16[4,272,256]{2,1,0:T(8,128)(2,1)} %get-tuple-element.21), channel_id=1, source_target_pairs={{0,1},{1,0},{2,3},{3,2},{4,5},{5,4},{6,7},{7,6},{8,9},{9,8},{10,11... | collective-permute-start | bytes 1671176 | tf_op jit(solution)/shard_map/ppermute | solution.py:207
  33.9 0.1 pad_add_fusion.places_ref
  34.0 7.1 %collective-permute-done.10.refs_0_ = s16[4,272,256]{2,1,0:T(8,128)(2,1)S(1)} collective-permute-done((s16[4,272,256]{2,1,0:T(8,128)(2,1)}, s16[4,272,256]{2,1,0:T(8,128)(2,1)S(1)}, u32[]{:S(2)}, u32[]{:S(2)}) %collective-permute-start.10) | collective-permute-done | bytes 557088 | tf_op jit(solution)/shard_map/ppermute | solution.py:207
  41.0 0.9 %pairs.3 = (f32[8,32,256]{2,1,0:T(8,128)S(1)}, s16[272,256]{1,0:T(8,128)(2,1)S(1)}, s16[272,256]{1,0:T(8,128)(2,1)S(1)}, s16[272,256]{1,0:T(8,128)(2,1)S(1)}) custom-call(s32[4]{0:T(128)S(1)} %pad_add_fusion.places_ref, f32[4,8,32,256]{3,2,1,0:T(8,128)S(1)} %copy-done.1, s16[4,272,256]{2,1,0:T(8,128)(2,1)S(1)} %collective-permute-done.10.refs_0_), custom_call_target="tpu_custom_call" | custom-call | tf_op jit(solution)/shard_map/pairs/pallas_call | solution.py:262
  41.9 1.4 %collective-permute-start.11 = (s16[272,256]{1,0:T(8,128)(2,1)S(1)}, s16[272,256]{1,0:T(8,128)(2,1)S(1)}, u32[]{:S(2)}, u32[]{:S(2)}) collective-permute-start(s16[272,256]{1,0:T(8,128)(2,1)S(1)} %get-tuple-element.30), channel_id=1, source_target_pairs={{0,2},{1,3},{2,4},{3,5},{4,6},{5,7},{6,0},{7,1},{8,10},{9,11},{10,... | collective-permute-start | bytes 417800 | tf_op jit(solution)/shard_map/ppermute | solution.py:210
  43.3 3.1 %collective-permute-start.12 = (s16[272,256]{1,0:T(8,128)(2,1)S(1)}, s16[272,256]{1,0:T(8,128)(2,1)S(1)}, u32[]{:S(2)}, u32[]{:S(2)}) collective-permute-start(s16[272,256]{1,0:T(8,128)(2,1)S(1)} %get-tuple-element.31), channel_id=1, source_target_pairs={{0,4},{1,5},{2,6},{3,7},{4,0},{5,1},{6,2},{7,3},{8,12},{9,13},{10,... | collective-permute-start | bytes 417800 | tf_op jit(solution)/shard_map/ppermute | solution.py:210
  46.5 1.9 %collective-permute-start.13 = (s16[272,256]{1,0:T(8,128)(2,1)S(1)}, s16[272,256]{1,0:T(8,128)(2,1)S(1)}, u32[]{:S(2)}, u32[]{:S(2)}) collective-permute-start(s16[272,256]{1,0:T(8,128)(2,1)S(1)} %get-tuple-element.32), channel_id=1, source_target_pairs={{0,6},{1,7},{2,0},{3,1},{4,2},{5,3},{6,4},{7,5},{8,14},{9,15},{10,... | collective-permute-start | bytes 417800 | tf_op jit(solution)/shard_map/ppermute | solution.py:210
  48.4 4.6 %collective-permute-done.3.refs_0_ = s16[4,272,256]{2,1,0:T(8,128)(2,1)S(1)} collective-permute-done((s16[4,272,256]{2,1,0:T(8,128)(2,1)}, s16[4,272,256]{2,1,0:T(8,128)(2,1)S(1)}, u32[]{:S(2)}, u32[]{:S(2)}) %collective-permute-start.3) | collective-permute-done | bytes 557088 | tf_op jit(solution)/shard_map/ppermute | solution.py:207
  53.0 1.2 %copy-done = f32[4,8,32,256]{3,2,1,0:T(8,128)S(1)} copy-done((f32[4,8,32,256]{3,2,1,0:T(8,128)S(1)}, f32[4,8,32,256]{3,2,1,0:T(8,128)}, u32[]{:S(2)}) %copy-start) | copy-done | bytes 1048600
  54.2 0.9 %pairs.2 = (f32[8,32,256]{2,1,0:T(8,128)S(1)}, s16[272,256]{1,0:T(8,128)(2,1)S(1)}, s16[272,256]{1,0:T(8,128)(2,1)S(1)}, s16[272,256]{1,0:T(8,128)(2,1)S(1)}) custom-call(s32[4]{0:T(128)S(1)} %pad_add_fusion.places_ref, f32[4,8,32,256]{3,2,1,0:T(8,128)S(1)} %copy-done, s16[4,272,256]{2,1,0:T(8,128)(2,1)S(1)} %collective-permute-done.3.refs_0_), custom_call_target="tpu_custom_call" | custom-call | tf_op jit(solution)/shard_map/pairs/pallas_call | solution.py:262
  55.1 1.0 %collective-permute-start.4 = (s16[272,256]{1,0:T(8,128)(2,1)S(1)}, s16[272,256]{1,0:T(8,128)(2,1)S(1)}, u32[]{:S(2)}, u32[]{:S(2)}) collective-permute-start(s16[272,256]{1,0:T(8,128)(2,1)S(1)} %get-tuple-element.23), channel_id=1, source_target_pairs={{0,2},{1,3},{2,4},{3,5},{4,6},{5,7},{6,0},{7,1},{8,10},{9,11},{10,... | collective-permute-start | bytes 417800 | tf_op jit(solution)/shard_map/ppermute | solution.py:210
  56.1 3.1 %collective-permute-start.5 = (s16[272,256]{1,0:T(8,128)(2,1)S(1)}, s16[272,256]{1,0:T(8,128)(2,1)S(1)}, u32[]{:S(2)}, u32[]{:S(2)}) collective-permute-start(s16[272,256]{1,0:T(8,128)(2,1)S(1)} %get-tuple-element.24), channel_id=1, source_target_pairs={{0,4},{1,5},{2,6},{3,7},{4,0},{5,1},{6,2},{7,3},{8,12},{9,13},{10,... | collective-permute-start | bytes 417800 | tf_op jit(solution)/shard_map/ppermute | solution.py:210
  59.2 0.0 collective-permute-done.11.refs_5_
  59.2 0.0 collective-permute-start.6
  59.2 0.0 collective-permute-done.12.refs_6_
  59.2 0.0 collective-permute-done.13.refs_7_
  59.3 2.4 %collective-permute-done.4.refs_1_ = s16[272,256]{1,0:T(8,128)(2,1)S(1)} collective-permute-done((s16[272,256]{1,0:T(8,128)(2,1)S(1)}, s16[272,256]{1,0:T(8,128)(2,1)S(1)}, u32[]{:S(2)}, u32[]{:S(2)}) %collective-permute-start.4) | collective-permute-done | bytes 139296 | tf_op jit(solution)/shard_map/ppermute | solution.py:210
  61.6 6.5 %collective-permute-done.5.refs_2_ = s16[272,256]{1,0:T(8,128)(2,1)S(1)} collective-permute-done((s16[272,256]{1,0:T(8,128)(2,1)S(1)}, s16[272,256]{1,0:T(8,128)(2,1)S(1)}, u32[]{:S(2)}, u32[]{:S(2)}) %collective-permute-start.5) | collective-permute-done | bytes 139296 | tf_op jit(solution)/shard_map/ppermute | solution.py:210
  68.1 3.4 %collective-permute-done.6.refs_3_ = s16[272,256]{1,0:T(8,128)(2,1)S(1)} collective-permute-done((s16[272,256]{1,0:T(8,128)(2,1)S(1)}, s16[272,256]{1,0:T(8,128)(2,1)S(1)}, u32[]{:S(2)}, u32[]{:S(2)}) %collective-permute-start.6) | collective-permute-done | bytes 139296 | tf_op jit(solution)/shard_map/ppermute | solution.py:210
  71.5 1.0 %last.1 = bf16[64,8,256]{2,1,0:T(8,128)(2,1)} custom-call(f32[8,32,256]{2,1,0:T(8,128)S(1)} %get-tuple-element.22.refs_0_, s16[272,256]{1,0:T(8,128)(2,1)S(1)} %collective-permute-done.4.refs_1_, s16[272,256]{1,0:T(8,128)(2,1)S(1)} %collective-permute-done.5.refs_2_, s16[272,256]{1,0:T(8,128)(2,1)S(1)} %collective-permute-done.6.refs_3_, ...), custom_call_target="tpu_custom_call" | custom-call | tf_op jit(solution)/shard_map/last/pallas_call | solution.py:270
  (10 shorter events, 0.0 us)
Async XLA Ops:
  0.0 1.0 %copy-start.2 = (bf16[128,8,256]{2,1,0:T(8,128)(2,1)S(1)}, bf16[128,8,256]{2,1,0:T(8,128)(2,1)}, u32[]{:S(2)}) copy-start(bf16[128,8,256]{2,1,0:T(8,128)(2,1)} %amps_ref.1) | copy-start | bytes 1572868
  1.3 18.3 %copy-start.3 = (bf16[2,8,32,256]{3,2,1,0:T(8,128)(2,1)}, bf16[2,8,32,256]{3,2,1,0:T(8,128)(2,1)S(1)}, u32[]{:S(2)}) copy-start(bf16[2,8,32,256]{3,2,1,0:T(8,128)(2,1)S(1)} %get-tuple-element.19.refs_0_) | copy-start | bytes 786436
  1.3 18.3 %copy-start.4 = (bf16[2,8,32,256]{3,2,1,0:T(8,128)(2,1)}, bf16[2,8,32,256]{3,2,1,0:T(8,128)(2,1)S(1)}, u32[]{:S(2)}) copy-start(bf16[2,8,32,256]{3,2,1,0:T(8,128)(2,1)S(1)} %get-tuple-element.26.refs_0_) | copy-start | bytes 786436
  1.4 9.3 %collective-permute-start.8 = (bf16[2,8,32,256]{3,2,1,0:T(8,128)(2,1)S(1)}, bf16[2,8,32,256]{3,2,1,0:T(8,128)(2,1)S(1)}, u32[]{:S(2)}, u32[]{:S(2)}) collective-permute-start(bf16[2,8,32,256]{3,2,1,0:T(8,128)(2,1)S(1)} %get-tuple-element.26.refs_0_), channel_id=1, source_target_pairs={{0,16},{8,24},{16,0},{24,8},{1,17},{9,25},{17,1},{25,9},{2,18},{10... | collective-permute-start | bytes 786440 | tf_op jit(solution)/shard_map/ppermute | solution.py:203
  1.9 13.2 %collective-permute-start.1 = (bf16[2,8,32,256]{3,2,1,0:T(8,128)(2,1)S(1)}, bf16[2,8,32,256]{3,2,1,0:T(8,128)(2,1)S(1)}, u32[]{:S(2)}, u32[]{:S(2)}) collective-permute-start(bf16[2,8,32,256]{3,2,1,0:T(8,128)(2,1)S(1)} %get-tuple-element.19.refs_0_), channel_id=1, source_target_pairs={{0,16},{8,24},{16,0},{24,8},{1,17},{9,25},{17,1},{25,9},{2,18},{10... | collective-permute-start | bytes 786440 | tf_op jit(solution)/shard_map/ppermute | solution.py:203
  3.4 16.3 %collective-permute-start.7 = (bf16[2,8,32,256]{3,2,1,0:T(8,128)(2,1)S(1)}, bf16[2,8,32,256]{3,2,1,0:T(8,128)(2,1)S(1)}, u32[]{:S(2)}, u32[]{:S(2)}) collective-permute-start(bf16[2,8,32,256]{3,2,1,0:T(8,128)(2,1)S(1)} %get-tuple-element.26.refs_0_), channel_id=1, source_target_pairs={{0,8},{8,0},{16,24},{24,16},{1,9},{9,1},{17,25},{25,17},{2,10},{10... | collective-permute-start | bytes 786440 | tf_op jit(solution)/shard_map/ppermute | solution.py:203
  10.6 9.1 %copy-start.6 = (bf16[2,8,32,256]{3,2,1,0:T(8,128)(2,1)}, bf16[2,8,32,256]{3,2,1,0:T(8,128)(2,1)S(1)}, u32[]{:S(2)}) copy-start(bf16[2,8,32,256]{3,2,1,0:T(8,128)(2,1)S(1)} %collective-permute-done.8.refs_2_) | copy-start | bytes 786436
  10.6 9.1 %collective-permute-start.9 = (bf16[2,8,32,256]{3,2,1,0:T(8,128)(2,1)S(1)}, bf16[2,8,32,256]{3,2,1,0:T(8,128)(2,1)S(1)}, u32[]{:S(2)}, u32[]{:S(2)}) collective-permute-start(bf16[2,8,32,256]{3,2,1,0:T(8,128)(2,1)S(1)} %collective-permute-done.8.refs_2_), channel_id=1, source_target_pairs={{0,8},{8,0},{16,24},{24,16},{1,9},{9,1},{17,25},{25,17},{2,10},{10... | collective-permute-start | bytes 786440 | tf_op jit(solution)/shard_map/ppermute | solution.py:203
  10.6 15.7 %collective-permute-start = (bf16[2,8,32,256]{3,2,1,0:T(8,128)(2,1)S(1)}, bf16[2,8,32,256]{3,2,1,0:T(8,128)(2,1)S(1)}, u32[]{:S(2)}, u32[]{:S(2)}) collective-permute-start(bf16[2,8,32,256]{3,2,1,0:T(8,128)(2,1)S(1)} %get-tuple-element.19.refs_0_), channel_id=1, source_target_pairs={{0,8},{8,0},{16,24},{24,16},{1,9},{9,1},{17,25},{25,17},{2,10},{10... | collective-permute-start | bytes 786440 | tf_op jit(solution)/shard_map/ppermute | solution.py:203
  15.1 4.6 %copy-start.5 = (bf16[2,8,32,256]{3,2,1,0:T(8,128)(2,1)}, bf16[2,8,32,256]{3,2,1,0:T(8,128)(2,1)S(1)}, u32[]{:S(2)}) copy-start(bf16[2,8,32,256]{3,2,1,0:T(8,128)(2,1)S(1)} %collective-permute-done.1.refs_2_) | copy-start | bytes 786436
  15.1 11.2 %collective-permute-start.2 = (bf16[2,8,32,256]{3,2,1,0:T(8,128)(2,1)S(1)}, bf16[2,8,32,256]{3,2,1,0:T(8,128)(2,1)S(1)}, u32[]{:S(2)}, u32[]{:S(2)}) collective-permute-start(bf16[2,8,32,256]{3,2,1,0:T(8,128)(2,1)S(1)} %collective-permute-done.1.refs_2_), channel_id=1, source_target_pairs={{0,8},{8,0},{16,24},{24,16},{1,9},{9,1},{17,25},{25,17},{2,10},{10... | collective-permute-start | bytes 786440 | tf_op jit(solution)/shard_map/ppermute | solution.py:203
  19.7 0.7 copy-start.8
  20.4 0.7 copy-start.10
  25.8 15.2 %copy-start.1 = (f32[4,8,32,256]{3,2,1,0:T(8,128)S(1)}, f32[4,8,32,256]{3,2,1,0:T(8,128)}, u32[]{:S(2)}) copy-start(f32[4,8,32,256]{3,2,1,0:T(8,128)} %get-tuple-element.27.keep_ref) | copy-start | bytes 3145732
  25.8 15.2 %collective-permute-start.10 = (s16[4,272,256]{2,1,0:T(8,128)(2,1)}, s16[4,272,256]{2,1,0:T(8,128)(2,1)S(1)}, u32[]{:S(2)}, u32[]{:S(2)}) collective-permute-start(s16[4,272,256]{2,1,0:T(8,128)(2,1)} %get-tuple-element.28), channel_id=1, source_target_pairs={{0,1},{1,0},{2,3},{3,2},{4,5},{5,4},{6,7},{7,6},{8,9},{9,8},{10,11... | collective-permute-start | bytes 1671176 | tf_op jit(solution)/shard_map/ppermute | solution.py:207
  26.3 0.7 copy-start.7
  27.0 0.7 copy-start.9
  32.4 20.6 %collective-permute-start.3 = (s16[4,272,256]{2,1,0:T(8,128)(2,1)}, s16[4,272,256]{2,1,0:T(8,128)(2,1)S(1)}, u32[]{:S(2)}, u32[]{:S(2)}) collective-permute-start(s16[4,272,256]{2,1,0:T(8,128)(2,1)} %get-tuple-element.21), channel_id=1, source_target_pairs={{0,1},{1,0},{2,3},{3,2},{4,5},{5,4},{6,7},{7,6},{8,9},{9,8},{10,11... | collective-permute-start | bytes 1671176 | tf_op jit(solution)/shard_map/ppermute | solution.py:207
  41.9 17.3 %collective-permute-start.11 = (s16[272,256]{1,0:T(8,128)(2,1)S(1)}, s16[272,256]{1,0:T(8,128)(2,1)S(1)}, u32[]{:S(2)}, u32[]{:S(2)}) collective-permute-start(s16[272,256]{1,0:T(8,128)(2,1)S(1)} %get-tuple-element.30), channel_id=1, source_target_pairs={{0,2},{1,3},{2,4},{3,5},{4,6},{5,7},{6,0},{7,1},{8,10},{9,11},{10,... | collective-permute-start | bytes 417800 | tf_op jit(solution)/shard_map/ppermute | solution.py:210
  43.3 15.9 %collective-permute-start.12 = (s16[272,256]{1,0:T(8,128)(2,1)S(1)}, s16[272,256]{1,0:T(8,128)(2,1)S(1)}, u32[]{:S(2)}, u32[]{:S(2)}) collective-permute-start(s16[272,256]{1,0:T(8,128)(2,1)S(1)} %get-tuple-element.31), channel_id=1, source_target_pairs={{0,4},{1,5},{2,6},{3,7},{4,0},{5,1},{6,2},{7,3},{8,12},{9,13},{10,... | collective-permute-start | bytes 417800 | tf_op jit(solution)/shard_map/ppermute | solution.py:210
  46.5 12.8 %collective-permute-start.13 = (s16[272,256]{1,0:T(8,128)(2,1)S(1)}, s16[272,256]{1,0:T(8,128)(2,1)S(1)}, u32[]{:S(2)}, u32[]{:S(2)}) collective-permute-start(s16[272,256]{1,0:T(8,128)(2,1)S(1)} %get-tuple-element.32), channel_id=1, source_target_pairs={{0,6},{1,7},{2,0},{3,1},{4,2},{5,3},{6,4},{7,5},{8,14},{9,15},{10,... | collective-permute-start | bytes 417800 | tf_op jit(solution)/shard_map/ppermute | solution.py:210
  53.0 1.2 %copy-start = (f32[4,8,32,256]{3,2,1,0:T(8,128)S(1)}, f32[4,8,32,256]{3,2,1,0:T(8,128)}, u32[]{:S(2)}) copy-start(f32[4,8,32,256]{3,2,1,0:T(8,128)} %get-tuple-element.20.keep_ref) | copy-start | bytes 3145732
  55.1 6.5 %collective-permute-start.4 = (s16[272,256]{1,0:T(8,128)(2,1)S(1)}, s16[272,256]{1,0:T(8,128)(2,1)S(1)}, u32[]{:S(2)}, u32[]{:S(2)}) collective-permute-start(s16[272,256]{1,0:T(8,128)(2,1)S(1)} %get-tuple-element.23), channel_id=1, source_target_pairs={{0,2},{1,3},{2,4},{3,5},{4,6},{5,7},{6,0},{7,1},{8,10},{9,11},{10,... | collective-permute-start | bytes 417800 | tf_op jit(solution)/shard_map/ppermute | solution.py:210
  56.1 12.0 %collective-permute-start.5 = (s16[272,256]{1,0:T(8,128)(2,1)S(1)}, s16[272,256]{1,0:T(8,128)(2,1)S(1)}, u32[]{:S(2)}, u32[]{:S(2)}) collective-permute-start(s16[272,256]{1,0:T(8,128)(2,1)S(1)} %get-tuple-element.24), channel_id=1, source_target_pairs={{0,4},{1,5},{2,6},{3,7},{4,0},{5,1},{6,2},{7,3},{8,12},{9,13},{10,... | collective-permute-start | bytes 417800 | tf_op jit(solution)/shard_map/ppermute | solution.py:210
  59.2 12.2 %collective-permute-start.6 = (s16[272,256]{1,0:T(8,128)(2,1)S(1)}, s16[272,256]{1,0:T(8,128)(2,1)S(1)}, u32[]{:S(2)}, u32[]{:S(2)}) collective-permute-start(s16[272,256]{1,0:T(8,128)(2,1)S(1)} %get-tuple-element.25), channel_id=1, source_target_pairs={{0,6},{1,7},{2,0},{3,1},{4,2},{5,3},{6,4},{7,5},{8,14},{9,15},{10,... | collective-permute-start | bytes 417800 | tf_op jit(solution)/shard_map/ppermute | solution.py:210

commit v2 on v1

v2 whole, which is shorter than its diff:
```python
import functools

import jax
import jax.numpy as jnp
from jax import lax
from jax.experimental import pallas as pl
from jax.experimental.pallas import tpu as pltpu
from jax.sharding import PartitionSpec as P

CD_COL = 8
PAIR_TILES_ROW = 8
CHUNKS = 2
LOADS = 8
LANES = 128
LEVELS = 32000.0
STEPS = 64.0
SMALLEST = 2.0**-110
VMEM_LIMIT = 16 * 1024 * 1024

F32 = jnp.float32
BF16 = jnp.bfloat16
I16 = jnp.int16

IN_VMEM = pl.BlockSpec(memory_space=pltpu.VMEM)
IN_SMEM = pl.BlockSpec(memory_space=pltpu.SMEM)
IN_HBM = pl.BlockSpec(memory_space=pl.ANY)


def held(x):
    return pltpu.with_memory_space_constraint(x, pltpu.VMEM)


def after(x, *others):
    return lax.optimization_barrier((x, *others))[0]


def kernel_call(body, outs, ins, scratch=(), flops=0, moved=0, name=None, outputs=IN_VMEM):
    return pl.pallas_call(
        body,
        out_shape=outs,
        in_specs=ins,
        out_specs=outputs if outputs is not IN_VMEM else jax.tree.map(lambda _: IN_VMEM, outs),
        scratch_shapes=list(scratch),
        compiler_params=pltpu.CompilerParams(vmem_limit_bytes=VMEM_LIMIT),
        cost_estimate=pl.CostEstimate(flops=flops, bytes_accessed=moved, transcendentals=0),
        name=name,
    )


def code(block):
    top = jnp.maximum(jnp.max(jnp.abs(block), axis=0, keepdims=True), SMALLEST)
    exponent = jnp.ceil(jnp.log2(top) * STEPS)
    scaled = block * (LEVELS * jnp.exp2(exponent * (-1.0 / STEPS)))
    return jnp.round(scaled).astype(jnp.int32).astype(I16), exponent


def store_exponents(ref, at, rows):
    tiles = len(rows)
    block = jnp.concatenate(list(rows) + [jnp.zeros_like(rows[0])] * (16 - tiles), axis=0)
    ref[at] = block.astype(jnp.int32).astype(I16)


def scales(exponents):
    return jnp.exp2(exponents.astype(jnp.int32).astype(F32) * (1.0 / STEPS)) * (1.0 / LEVELS)


def decode(block, scale):
    return block.astype(jnp.int32).astype(F32) * scale


def split_kernel(parts, here_ref, amps_ref, *refs):
    outs, flat = refs[:-1], refs[-1]
    rows, tiles, width = amps_ref.shape
    lanes, each = flat.shape[2], rows // parts
    for half in range(width // lanes):
        columns = pl.ds(half * lanes, lanes)
        flat[half] = amps_ref[:, :, columns].astype(F32).reshape(rows * tiles, lanes)
    for step in range(parts):
        part = lax.rem(here_ref[0] + step, parts)
        for tile in range(tiles):
            first = part * each * tiles + tile
            for half in range(width // lanes):
                picked = flat[half, pl.ds(first, each, stride=tiles), :]
                outs[step][tile, :, pl.ds(half * lanes, lanes)] = picked.astype(BF16)


def load_kernel(pieces, cd_ref, ab_ref, count_ref, ints_ref, slots_ref, table_ref, sems):
    per = ints_ref.shape[0] // pieces
    pairs = slots_ref.shape[0] // 2
    count = count_ref[0]
    live = lax.div(count + per - 1, per)

    def copy(piece):
        part = pl.ds(piece * per, per)
        return pltpu.make_async_copy(ints_ref.at[part], table_ref.at[part], sems.at[piece])

    def start(piece, carry):
        copy(piece).start()
        return carry

    def clear(pair, carry):
        slots_ref[pair] = 0
        slots_ref[pairs + pair] = CD_COL
        return carry

    def note(slot, carry):
        pair = ab_ref[slot] * CD_COL + cd_ref[slot]
        slots_ref[pair] = slot
        slots_ref[pairs + pair] = cd_ref[slot]
        return carry

    def finish(piece, carry):
        copy(piece).wait()
        return carry

    lax.fori_loop(0, live, start, 0)
    lax.fori_loop(0, pairs, clear, 0)
    lax.fori_loop(0, count, note, 0)
    lax.fori_loop(0, live, finish, 0)


def multiply(amps_refs, slots_ref, table_ref, left, use):
    tiles, each, width = amps_refs[0].shape
    pairs = slots_ref.shape[0] // 2
    rows = each * len(amps_refs)
    for tile in range(tiles):
        for block, ref in enumerate(amps_refs):
            left[tile, block * each : (block + 1) * each] = ref[tile]
    left[tiles] = jnp.zeros((rows, width), BF16)
    for ab in range(pairs // tiles):
        total = jnp.zeros((rows, table_ref.shape[2]), F32)
        for tile in range(tiles):
            pair = ab * tiles + tile
            total = total + jnp.dot(
                left[slots_ref[pairs + pair]], table_ref[slots_ref[pair]], preferred_element_type=F32
            )
        use(ab, total)


def keep_kernel(blocks, *refs):
    slots_ref, table_ref, keep_ref, left = refs[blocks:]
    each = refs[0].shape[1]

    def use(ab, total):
        for block in range(blocks):
            keep_ref[block, ab] = total[block * each : (block + 1) * each]

    multiply(refs[:blocks], slots_ref, table_ref, left, use)


def send_kernel(blocks, chunks, *refs):
    slots_ref, table_ref = refs[blocks : blocks + 2]
    send_refs, left = refs[blocks + 2 : -1], refs[-1]
    each = refs[0].shape[1] // chunks
    exponents = {}
    tiles = slots_ref.shape[0] // 2 // CD_COL

    def use(ab, total):
        for block in range(blocks):
            for chunk in range(chunks):
                at = (block * chunks + chunk) * each
                coded, exponent = code(total[at : at + each])
                send_refs[chunk][block, ab * each : (ab + 1) * each] = coded
                exponents.setdefault((block, chunk), []).append(exponent)

    multiply(refs[:blocks], slots_ref, table_ref, left, use)
    for (block, chunk), rows in exponents.items():
        store_exponents(send_refs[chunk].at[block], pl.ds(tiles * each, 16), rows)


def pair_kernel(chunk, near, places_ref, keep_ref, *refs):
    blocks, ab_tiles, _, width = keep_ref.shape
    sums = refs[-1]
    each = sums.shape[2]
    received = refs[: len(refs) - 1 - blocks]
    own_ref, send_refs = refs[len(received)], refs[len(received) + 1 : -1]
    half = len(received) // 2
    for block in range(blocks):
        mine = received[:half] if block < near else received[half:]
        at = block if block < near else block - near
        factors = [scales(ref[at, pl.ds(ab_tiles * each, 16)]) for ref in mine]
        for ab in range(ab_tiles):
            total = keep_ref[block, ab, chunk * each : (chunk + 1) * each]
            for ref, factor in zip(mine, factors):
                total = total + decode(ref[at, ab * each : (ab + 1) * each], factor[ab : ab + 1])
            sums[block, ab] = total
    own_ref[...] = sums[places_ref[0]]
    for step in range(1, blocks):
        exponents = []
        for ab in range(ab_tiles):
            coded, exponent = code(sums[places_ref[step], ab])
            send_refs[step - 1][ab * each : (ab + 1) * each] = coded
            exponents.append(exponent)
        store_exponents(send_refs[step - 1], pl.ds(ab_tiles * each, 16), exponents)


def last_kernel(chunks, *refs):
    flat, out_ref = refs[-1], refs[-2]
    per = (len(refs) - 2) // chunks
    rows, ab_tiles, width = out_ref.shape
    lanes = flat.shape[2]
    for chunk in range(chunks):
        own_ref, received = refs[chunk * per], refs[chunk * per + 1 : (chunk + 1) * per]
        each = own_ref.shape[1]
        factors = [scales(ref[pl.ds(ab_tiles * each, 16)]) for ref in received]
        for ab in range(ab_tiles):
            total = own_ref[ab]
            for ref, factor in zip(received, factors):
                total = total + decode(ref[ab * each : (ab + 1) * each], factor[ab : ab + 1])
            for half in range(width // lanes):
                piece = total[:, half * lanes : (half + 1) * lanes]
                flat[half, pl.ds(chunk * each * ab_tiles + ab, each, stride=ab_tiles), :] = piece
    for half in range(width // lanes):
        whole = flat[half].reshape(rows, ab_tiles, lanes)
        out_ref[:, :, pl.ds(half * lanes, lanes)] = whole.astype(out_ref.dtype)


def shards(n_row, n_col, amps, ints, task_cd, task_ab, task_count):
    n_x = n_col // n_row
    n_z = n_row
    n_y = n_row // 2
    rows, tiles, width = amps.shape
    out_rows = rows // n_x
    each = out_rows // CHUNKS
    pairs = PAIR_TILES_ROW * CD_COL
    coded_rows = PAIR_TILES_ROW * each + 16
    row, col = lax.axis_index("row"), lax.axis_index("col")
    x, z = lax.rem(col, n_x), lax.div(col, n_x)
    other_parts = range(1, n_x)

    def along_y(array, step):
        return lax.ppermute(array, "row", [(r, (r + 2 * step) % n_row) for r in range(n_row)])

    def to_partner(array):
        return lax.ppermute(array, "row", [(r, r ^ 1) for r in range(n_row)])

    def along_x(array, step):
        pairs = [(c, c - c % n_x + (c % n_x + step) % n_x) for c in range(n_col)]
        return lax.ppermute(array, "col", pairs)

    def along_z(array, step):
        return lax.ppermute(array, "col", [(c, (c + step * n_x) % n_col) for c in range(n_col)])

    def send_products(blocks):
        return kernel_call(
            functools.partial(send_kernel, len(blocks), CHUNKS),
            [pltpu.VMEM((len(blocks), coded_rows, width), I16)] * CHUNKS,
            [IN_VMEM] * len(blocks) + [IN_SMEM, IN_VMEM],
            [pltpu.VMEM((tiles + 1, len(blocks) * out_rows, width), BF16)],
            flops=2 * len(blocks) * out_rows * tiles * width * PAIR_TILES_ROW * width,
            name="send_products",
        )(*map(held, blocks), slots, held(table))

    places = []
    for step in range(n_z):
        wanted = lax.rem(z + step, n_z)
        far = lax.rem(row // 2 - wanted // 2 + n_y, n_y)
        places.append(2 * far + lax.rem(row + wanted, 2))
    places = jnp.stack(places).astype(jnp.int32)

    mine = kernel_call(
        functools.partial(split_kernel, n_x),
        [pltpu.VMEM((tiles, out_rows, width), BF16)] * n_x,
        [IN_SMEM, IN_VMEM],
        [pltpu.VMEM((width // LANES, rows * tiles, LANES), F32)],
        name="split",
    )(x[None], amps)
    order = [*other_parts, 0]
    beside = {part: to_partner(mine[part]) for part in order}
    far = {part: [along_y(mine[part], k) for k in range(1, n_y)] for part in order}
    slots, table = kernel_call(
        functools.partial(load_kernel, LOADS),
        [pltpu.SMEM((2 * pairs,), jnp.int32), pltpu.VMEM(ints.shape, BF16)],
        [IN_SMEM, IN_SMEM, IN_SMEM, IN_HBM],
        [pltpu.SemaphoreType.DMA((LOADS,))],
        moved=ints.size * 2,
        outputs=[IN_SMEM, IN_VMEM],
        name="load",
    )(task_cd, task_ab, task_count, pltpu.with_memory_space_constraint(ints, pltpu.HBM))

    near_sends = [send_products([mine[part], beside[part]]) for part in other_parts]
    x_sent = {}
    near_received = [[along_x(sends[0], part) for part, sends in zip(other_parts, near_sends)]]

    def fetch(part, *ties):
        blocks = []
        for array in far[part]:
            array = after(array, *ties)
            blocks += [array, to_partner(array)]
        return blocks

    far_blocks = {part: fetch(part, near_sends[-1][0]) for part in other_parts}
    far_sends = [send_products(far_blocks[part]) for part in other_parts]
    far_received = [[along_x(sends[0], part) for part, sends in zip(other_parts, far_sends)]]
    for q in range(1, CHUNKS):
        near_received.append(
            [along_x(after(sends[q], far_sends[-1][0]), part) for part, sends in zip(other_parts, near_sends)]
        )
        far_received.append([along_x(sends[q], part) for part, sends in zip(other_parts, far_sends)])
    far_blocks[0] = fetch(0, far_sends[-1][0])
    blocks = [mine[0], beside[0], *far_blocks[0]]
    keep = kernel_call(
        functools.partial(keep_kernel, n_row),
        pltpu.VMEM((n_row, PAIR_TILES_ROW, out_rows, width), F32),
        [IN_VMEM] * n_row + [IN_SMEM, IN_VMEM],
        [pltpu.VMEM((tiles + 1, n_row * out_rows, width), BF16)],
        flops=2 * n_row * out_rows * tiles * width * PAIR_TILES_ROW * width,
        name="keep_products",
    )(*map(held, blocks), slots, held(table))

    last = []
    for q in range(CHUNKS):
        own, *sends = kernel_call(
            functools.partial(pair_kernel, q, 2),
            [pltpu.VMEM((PAIR_TILES_ROW, each, width), F32)] + [pltpu.VMEM((coded_rows, width), I16)] * (n_z - 1),
            [IN_SMEM] + [IN_VMEM] * (2 * n_x - 1),
            [pltpu.VMEM((n_row, PAIR_TILES_ROW, each, width), F32)],
            name="pairs",
        )(places, held(keep), *map(held, near_received[q]), *map(held, far_received[q]))
        last += [own] + [along_z(send, step) for step, send in zip(range(1, n_z), sends)]
    return kernel_call(
        functools.partial(last_kernel, CHUNKS),
        jax.ShapeDtypeStruct((out_rows, PAIR_TILES_ROW, width), BF16),
        [IN_VMEM] * len(last),
        [pltpu.VMEM((width // LANES, out_rows * PAIR_TILES_ROW, LANES), F32)],
        name="last",
    )(*map(held, last))


def solution(mesh):
    return jax.shard_map(
        functools.partial(shards, mesh.shape["row"], mesh.shape["col"]),
        mesh=mesh,
        in_specs=(
            P("row", "col", None),
            P(("row", "col"), None, None),
            P(("row", "col")),
            P(("row", "col")),
            P(("row", "col")),
        ),
        out_specs=P("col", "row", None),
        check_vma=False,
    )
```

time: 72.7 us -> 63.7 us (0.88)
  the two profiles are of different devices: /device:TPU:12 before, /device:TPU:0 now
where the time goes in v2:
time: 63.7 us; the launch traced here: 62.6 us
  waiting for transfers between devices  23.8 us (37%)
  starting transfers between devices  21.4 us (34%)
  Pallas kernels  11 us (17%)
  local copies, waits for them, and re-layouts  5.73 us (9%)
  between operations  0.75 us (1%)
    ppermute x6, starting transfers between devices, along_z(): lax.ppermute(array, 'col', [(c, (c + step * n_x) % n_col) for c in range(...  12.2 us
    ppermute x4, waiting for transfers between devices, along_x(): return lax.ppermute(array, 'col', pairs)  10.1 us
    ppermute x6, waiting for transfers between devices, along_z(): lax.ppermute(array, 'col', [(c, (c + step * n_x) % n_col) for c in range(...  7.54 us
    ppermute x2, waiting for transfers between devices, along_y(): lax.ppermute(array, 'row', [(r, (r + 2 * step) % n_row) for r in range(n_...  6.15 us
    unnamed x10, local copies, waits for them, and re-layouts  5.73 us
    ppermute x2, starting transfers between devices, along_y(): lax.ppermute(array, 'row', [(r, (r + 2 * step) % n_row) for r in range(n_...  4.35 us
    ppermute x4, starting transfers between devices, along_x(): return lax.ppermute(array, 'col', pairs)  4.05 us
    pallas_call x1, Pallas kernels, shards(): kernel_call(functools.partial(load_kernel, LOADS), [pltpu.SMEM((2 * pairs...  2.8 us
  transfers between devices with their start and end apart: 16, of which 6 were waited for; matrix products, arithmetic and copies ran while one was open for 0% of the time, Pallas kernels for 15%

profile of v2, /device:TPU:0, one launch (start us, length us, event | category | flops | bytes accessed | tf_op | source)
XLA Modules:
  0.0 62.6 jit_solution(16425256434235243160)
XLA Ops:
  0.0 1.0 %copy-done.2 = bf16[128,8,256]{2,1,0:T(8,128)(2,1)S(1)} copy-done((bf16[128,8,256]{2,1,0:T(8,128)(2,1)S(1)}, bf16[128,8,256]{2,1,0:T(8,128)(2,1)}, u32[]{:S(2)}) %copy-start.2) | copy-done | bytes 524312
  1.0 0.3 split.1
  1.3 0.5 collective-permute-start.3
  1.9 2.6 %collective-permute-start.2 = (bf16[8,64,256]{2,1,0:T(8,128)(2,1)S(1)}, bf16[8,64,256]{2,1,0:T(8,128)(2,1)S(1)}, u32[]{:S(2)}, u32[]{:S(2)}) collective-permute-start(bf16[8,64,256]{2,1,0:T(8,128)(2,1)S(1)} %get-tuple-element.25.refs_0_), channel_id=1, source_target_pairs={{0,16},{8,24},{16,0},{24,8},{1,17},{9,25},{17,1},{25,9},{2,18},{10... | collective-permute-start | bytes 786440 | tf_op jit(solution)/shard_map/ppermute | solution.py:232
  5.1 0.0 copy-start.3
  5.1 0.6 %copy-done.3 = s32[64]{0:T(128)S(1)} copy-done((s32[64]{0:T(128)S(1)}, s32[64]{0:T(128)}, u32[]{:S(2)}) %copy-start.3) | copy-done | bytes 280
  5.8 0.7 %copy-done.4 = s32[64]{0:T(128)S(1)} copy-done((s32[64]{0:T(128)S(1)}, s32[64]{0:T(128)}, u32[]{:S(2)}) %copy-start.4) | copy-done | bytes 280
  6.4 2.8 %load.1 = (s32[128]{0:T(128)S(4)}, bf16[64,256,256]{2,1,0:T(8,128)(2,1)S(1)}) custom-call(s32[64]{0:T(128)S(1)} %copy-done.3, s32[64]{0:T(128)S(1)} %copy-done.4, s32[1]{0:T(128)S(6)} %copy.6.count_ref, bf16[64,256,256]{2,1,0:T(8,128)(2,1)} %ints_ref.1), custom_call_target="tpu_custom_call" | custom-call | bytes 8388608 | tf_op jit(solution)/shard_map/load/pallas_call | solution.py:271
  9.2 0.0 copy-start
  9.2 0.0 collective-permute-done.3.refs_1_
  9.2 1.3 %send_products.2 = (s16[2,272,256]{2,1,0:T(8,128)(2,1)S(1)}, s16[2,272,256]{2,1,0:T(8,128)(2,1)S(1)}) custom-call(bf16[8,64,256]{2,1,0:T(8,128)(2,1)S(1)} %get-tuple-element.25.refs_0_, bf16[8,64,256]{2,1,0:T(8,128)(2,1)S(1)} %collective-permute-done.3.refs_1_, s32[128]{0:T(128)S(4)} %get-tuple-element.26.refs_2_.refs_4_, ...), custom_call_target="tpu_custom_call" | custom-call | flops 1073741824 | tf_op jit(solution)/shard_map/send_products/pallas_call | solution.py:245
  10.6 0.8 %collective-permute-done.2.refs_0_ = bf16[8,64,256]{2,1,0:T(8,128)(2,1)S(1)} collective-permute-done((bf16[8,64,256]{2,1,0:T(8,128)(2,1)S(1)}, bf16[8,64,256]{2,1,0:T(8,128)(2,1)S(1)}, u32[]{:S(2)}, u32[]{:S(2)}) %collective-permute-start.2) | collective-permute-done | bytes 262176 | tf_op jit(solution)/shard_map/ppermute | solution.py:232
  11.3 0.0 collective-permute-start.4
  11.3 1.8 %collective-permute-start.1 = (bf16[8,64,256]{2,1,0:T(8,128)(2,1)S(1)}, bf16[8,64,256]{2,1,0:T(8,128)(2,1)S(1)}, u32[]{:S(2)}, u32[]{:S(2)}) collective-permute-start(bf16[8,64,256]{2,1,0:T(8,128)(2,1)S(1)} %get-tuple-element.24.refs_0_), channel_id=1, source_target_pairs={{0,16},{8,24},{16,0},{24,8},{1,17},{9,25},{17,1},{25,9},{2,18},{10... | collective-permute-start | bytes 786440 | tf_op jit(solution)/shard_map/ppermute | solution.py:232
  13.1 0.2 collective-permute-start
  13.3 0.0 collective-permute-done.4.refs_1_
  13.3 1.3 %send_products.3 = (s16[2,272,256]{2,1,0:T(8,128)(2,1)S(1)}, s16[2,272,256]{2,1,0:T(8,128)(2,1)S(1)}) custom-call(bf16[8,64,256]{2,1,0:T(8,128)(2,1)S(1)} %collective-permute-done.2.refs_0_, bf16[8,64,256]{2,1,0:T(8,128)(2,1)S(1)} %collective-permute-done.4.refs_1_, s32[128]{0:T(128)S(4)} %get-tuple-element.26.refs_2_.refs_4_, ...), custom_call_target="tpu_custom_call" | custom-call | flops 1073741824 | tf_op jit(solution)/shard_map/send_products/pallas_call | solution.py:245
  14.7 0.0 copy-done
  14.7 5.4 %collective-permute-done.1.refs_2_ = bf16[8,64,256]{2,1,0:T(8,128)(2,1)S(1)} collective-permute-done((bf16[8,64,256]{2,1,0:T(8,128)(2,1)S(1)}, bf16[8,64,256]{2,1,0:T(8,128)(2,1)S(1)}, u32[]{:S(2)}, u32[]{:S(2)}) %collective-permute-start.1) | collective-permute-done | bytes 262176 | tf_op jit(solution)/shard_map/ppermute | solution.py:232
  20.1 0.0 collective-permute-start.5
  20.1 1.8 %collective-permute-start.11 = (s16[2,272,256]{2,1,0:T(8,128)(2,1)S(1)}, s16[2,272,256]{2,1,0:T(8,128)(2,1)S(1)}, u32[]{:S(2)}, u32[]{:S(2)}) collective-permute-start(s16[2,272,256]{2,1,0:T(8,128)(2,1)S(1)} %get-tuple-element.37), channel_id=1, source_target_pairs={{0,1},{1,0},{2,3},{3,2},{4,5},{5,4},{6,7},{7,6},{8,9},{9,8},{10,11... | collective-permute-start | bytes 835592 | tf_op jit(solution)/shard_map/ppermute | solution.py:239
  21.8 0.3 collective-permute-start.12
  22.1 0.1 pad_add_fusion.places_ref
  22.2 1.8 %collective-permute-start.6 = (s16[2,272,256]{2,1,0:T(8,128)(2,1)S(1)}, s16[2,272,256]{2,1,0:T(8,128)(2,1)S(1)}, u32[]{:S(2)}, u32[]{:S(2)}) collective-permute-start(s16[2,272,256]{2,1,0:T(8,128)(2,1)S(1)} %get-tuple-element.28), channel_id=1, source_target_pairs={{0,1},{1,0},{2,3},{3,2},{4,5},{5,4},{6,7},{7,6},{8,9},{9,8},{10,11... | collective-permute-start | bytes 835592 | tf_op jit(solution)/shard_map/ppermute | solution.py:239
  24.0 0.0 collective-permute-done.refs_1_
  24.0 0.3 collective-permute-start.7
  24.2 0.0 collective-permute-done.5.refs_3_
  24.2 3.4 %copy-done.1 = bf16[64,256,256]{2,1,0:T(8,128)(2,1)S(1)} copy-done((bf16[64,256,256]{2,1,0:T(8,128)(2,1)S(1)}, bf16[64,256,256]{2,1,0:T(8,128)(2,1)}, u32[]{:S(2)}) %copy-start.1) | copy-done | bytes 8388632
  27.6 2.4 %keep_products.1.keep_ref = f32[4,8,64,256]{3,2,1,0:T(8,128)S(1)} custom-call(bf16[8,64,256]{2,1,0:T(8,128)(2,1)S(1)} %get-tuple-element.24.refs_0_, bf16[8,64,256]{2,1,0:T(8,128)(2,1)S(1)} %collective-permute-done.refs_1_, bf16[8,64,256]{2,1,0:T(8,128)(2,1)S(1)} %collective-permute-done.1.refs_2_, bf16[8,64,256]{2,1,0:T(8,128)(2,1)S(1)} %collective-permute-done.5.refs_3_, ...), custom_call_target="tpu_custom_call" | custom-call | flops 2147483648 | tf_op jit(solution)/shard_map/keep_products/pallas_call | solution.py:302
  30.0 0.0 collective-permute-done.11.refs_0_
  30.0 5.5 %collective-permute-done.12.refs_1_ = s16[2,272,256]{2,1,0:T(8,128)(2,1)S(1)} collective-permute-done((s16[2,272,256]{2,1,0:T(8,128)(2,1)S(1)}, s16[2,272,256]{2,1,0:T(8,128)(2,1)S(1)}, u32[]{:S(2)}, u32[]{:S(2)}) %collective-permute-start.12) | collective-permute-done | bytes 278560 | tf_op jit(solution)/shard_map/ppermute | solution.py:239
  35.5 0.9 %pairs.3 = (f32[8,32,256]{2,1,0:T(8,128)S(1)}, s16[272,256]{1,0:T(8,128)(2,1)S(1)}, s16[272,256]{1,0:T(8,128)(2,1)S(1)}, s16[272,256]{1,0:T(8,128)(2,1)S(1)}) custom-call(s32[4]{0:T(128)S(1)} %pad_add_fusion.places_ref, f32[4,8,64,256]{3,2,1,0:T(8,128)S(1)} %keep_products.1.keep_ref, s16[2,272,256]{2,1,0:T(8,128)(2,1)S(1)} %collective-permute-done.11.refs_0_, ...), custom_call_target="tpu_custom_call" | custom-call | tf_op jit(solution)/shard_map/pairs/pallas_call | solution.py:313
  36.4 1.8 %collective-permute-start.13 = (s16[272,256]{1,0:T(8,128)(2,1)S(1)}, s16[272,256]{1,0:T(8,128)(2,1)S(1)}, u32[]{:S(2)}, u32[]{:S(2)}) collective-permute-start(s16[272,256]{1,0:T(8,128)(2,1)S(1)} %get-tuple-element.40), channel_id=1, source_target_pairs={{0,2},{1,3},{2,4},{3,5},{4,6},{5,7},{6,0},{7,1},{8,10},{9,11},{10,... | collective-permute-start | bytes 417800 | tf_op jit(solution)/shard_map/ppermute | solution.py:242
  38.2 2.6 %collective-permute-start.14 = (s16[272,256]{1,0:T(8,128)(2,1)S(1)}, s16[272,256]{1,0:T(8,128)(2,1)S(1)}, u32[]{:S(2)}, u32[]{:S(2)}) collective-permute-start(s16[272,256]{1,0:T(8,128)(2,1)S(1)} %get-tuple-element.41), channel_id=1, source_target_pairs={{0,4},{1,5},{2,6},{3,7},{4,0},{5,1},{6,2},{7,3},{8,12},{9,13},{10,... | collective-permute-start | bytes 417800 | tf_op jit(solution)/shard_map/ppermute | solution.py:242
  40.8 1.7 %collective-permute-start.15 = (s16[272,256]{1,0:T(8,128)(2,1)S(1)}, s16[272,256]{1,0:T(8,128)(2,1)S(1)}, u32[]{:S(2)}, u32[]{:S(2)}) collective-permute-start(s16[272,256]{1,0:T(8,128)(2,1)S(1)} %get-tuple-element.42), channel_id=1, source_target_pairs={{0,6},{1,7},{2,0},{3,1},{4,2},{5,3},{6,4},{7,5},{8,14},{9,15},{10,... | collective-permute-start | bytes 417800 | tf_op jit(solution)/shard_map/ppermute | solution.py:242
  42.5 0.0 collective-permute-done.6.refs_0_
  42.5 4.6 %collective-permute-done.7.refs_1_ = s16[2,272,256]{2,1,0:T(8,128)(2,1)S(1)} collective-permute-done((s16[2,272,256]{2,1,0:T(8,128)(2,1)S(1)}, s16[2,272,256]{2,1,0:T(8,128)(2,1)S(1)}, u32[]{:S(2)}, u32[]{:S(2)}) %collective-permute-start.7) | collective-permute-done | bytes 278560 | tf_op jit(solution)/shard_map/ppermute | solution.py:239
  47.1 0.9 %pairs.2 = (f32[8,32,256]{2,1,0:T(8,128)S(1)}, s16[272,256]{1,0:T(8,128)(2,1)S(1)}, s16[272,256]{1,0:T(8,128)(2,1)S(1)}, s16[272,256]{1,0:T(8,128)(2,1)S(1)}) custom-call(s32[4]{0:T(128)S(1)} %pad_add_fusion.places_ref, f32[4,8,64,256]{3,2,1,0:T(8,128)S(1)} %keep_products.1.keep_ref, s16[2,272,256]{2,1,0:T(8,128)(2,1)S(1)} %collective-permute-done.6.refs_0_, ...), custom_call_target="tpu_custom_call" | custom-call | tf_op jit(solution)/shard_map/pairs/pallas_call | solution.py:313
  48.0 1.9 %collective-permute-start.8 = (s16[272,256]{1,0:T(8,128)(2,1)S(1)}, s16[272,256]{1,0:T(8,128)(2,1)S(1)}, u32[]{:S(2)}, u32[]{:S(2)}) collective-permute-start(s16[272,256]{1,0:T(8,128)(2,1)S(1)} %get-tuple-element.33), channel_id=1, source_target_pairs={{0,2},{1,3},{2,4},{3,5},{4,6},{5,7},{6,0},{7,1},{8,10},{9,11},{10,... | collective-permute-start | bytes 417800 | tf_op jit(solution)/shard_map/ppermute | solution.py:242
  49.9 2.6 %collective-permute-start.9 = (s16[272,256]{1,0:T(8,128)(2,1)S(1)}, s16[272,256]{1,0:T(8,128)(2,1)S(1)}, u32[]{:S(2)}, u32[]{:S(2)}) collective-permute-start(s16[272,256]{1,0:T(8,128)(2,1)S(1)} %get-tuple-element.34), channel_id=1, source_target_pairs={{0,4},{1,5},{2,6},{3,7},{4,0},{5,1},{6,2},{7,3},{8,12},{9,13},{10,... | collective-permute-start | bytes 417800 | tf_op jit(solution)/shard_map/ppermute | solution.py:242
  52.5 0.0 collective-permute-done.13.refs_5_
  52.5 1.6 %collective-permute-start.10 = (s16[272,256]{1,0:T(8,128)(2,1)S(1)}, s16[272,256]{1,0:T(8,128)(2,1)S(1)}, u32[]{:S(2)}, u32[]{:S(2)}) collective-permute-start(s16[272,256]{1,0:T(8,128)(2,1)S(1)} %get-tuple-element.35), channel_id=1, source_target_pairs={{0,6},{1,7},{2,0},{3,1},{4,2},{5,3},{6,4},{7,5},{8,14},{9,15},{10,... | collective-permute-start | bytes 417800 | tf_op jit(solution)/shard_map/ppermute | solution.py:242
  54.1 0.0 collective-permute-done.14.refs_6_
  54.1 0.0 collective-permute-done.15.refs_7_
  54.1 2.4 %collective-permute-done.8.refs_1_ = s16[272,256]{1,0:T(8,128)(2,1)S(1)} collective-permute-done((s16[272,256]{1,0:T(8,128)(2,1)S(1)}, s16[272,256]{1,0:T(8,128)(2,1)S(1)}, u32[]{:S(2)}, u32[]{:S(2)}) %collective-permute-start.8) | collective-permute-done | bytes 139296 | tf_op jit(solution)/shard_map/ppermute | solution.py:242
  56.5 5.1 %collective-permute-done.9.refs_2_ = s16[272,256]{1,0:T(8,128)(2,1)S(1)} collective-permute-done((s16[272,256]{1,0:T(8,128)(2,1)S(1)}, s16[272,256]{1,0:T(8,128)(2,1)S(1)}, u32[]{:S(2)}, u32[]{:S(2)}) %collective-permute-start.9) | collective-permute-done | bytes 139296 | tf_op jit(solution)/shard_map/ppermute | solution.py:242
  61.6 0.0 collective-permute-done.10.refs_3_
  61.6 1.0 %last.1 = bf16[64,8,256]{2,1,0:T(8,128)(2,1)} custom-call(f32[8,32,256]{2,1,0:T(8,128)S(1)} %get-tuple-element.32.refs_0_, s16[272,256]{1,0:T(8,128)(2,1)S(1)} %collective-permute-done.8.refs_1_, s16[272,256]{1,0:T(8,128)(2,1)S(1)} %collective-permute-done.9.refs_2_, s16[272,256]{1,0:T(8,128)(2,1)S(1)} %collective-permute-done.10.refs_3_, ...), custom_call_target="tpu_custom_call" | custom-call | tf_op jit(solution)/shard_map/last/pallas_call | solution.py:321
  (3 shorter events, 0.0 us)
Async XLA Ops:
  0.0 1.0 %copy-start.2 = (bf16[128,8,256]{2,1,0:T(8,128)(2,1)S(1)}, bf16[128,8,256]{2,1,0:T(8,128)(2,1)}, u32[]{:S(2)}) copy-start(bf16[128,8,256]{2,1,0:T(8,128)(2,1)} %amps_ref.1) | copy-start | bytes 1572868
  1.3 7.9 %collective-permute-start.3 = (bf16[8,64,256]{2,1,0:T(8,128)(2,1)S(1)}, bf16[8,64,256]{2,1,0:T(8,128)(2,1)S(1)}, u32[]{:S(2)}, u32[]{:S(2)}) collective-permute-start(bf16[8,64,256]{2,1,0:T(8,128)(2,1)S(1)} %get-tuple-element.25.refs_0_), channel_id=1, source_target_pairs={{0,8},{8,0},{16,24},{24,16},{1,9},{9,1},{17,25},{25,17},{2,10},{10... | collective-permute-start | bytes 786440 | tf_op jit(solution)/shard_map/ppermute | solution.py:235
  1.9 9.5 %collective-permute-start.2 = (bf16[8,64,256]{2,1,0:T(8,128)(2,1)S(1)}, bf16[8,64,256]{2,1,0:T(8,128)(2,1)S(1)}, u32[]{:S(2)}, u32[]{:S(2)}) collective-permute-start(bf16[8,64,256]{2,1,0:T(8,128)(2,1)S(1)} %get-tuple-element.25.refs_0_), channel_id=1, source_target_pairs={{0,16},{8,24},{16,0},{24,8},{1,17},{9,25},{17,1},{25,9},{2,18},{10... | collective-permute-start | bytes 786440 | tf_op jit(solution)/shard_map/ppermute | solution.py:232
  5.1 0.7 %copy-start.3 = (s32[64]{0:T(128)S(1)}, s32[64]{0:T(128)}, u32[]{:S(2)}) copy-start(s32[64]{0:T(128)} %cd_ref.1) | copy-start | bytes 772
  5.8 0.7 %copy-start.4 = (s32[64]{0:T(128)S(1)}, s32[64]{0:T(128)}, u32[]{:S(2)}) copy-start(s32[64]{0:T(128)} %ab_ref.1) | copy-start | bytes 772
  9.2 5.5 %copy-start = (bf16[64,256,256]{2,1,0:T(8,128)(2,1)}, bf16[64,256,256]{2,1,0:T(8,128)(2,1)S(1)}, u32[]{:S(2)}) copy-start(bf16[64,256,256]{2,1,0:T(8,128)(2,1)S(1)} %get-tuple-element.27.refs_3_.refs_5_) | copy-start | bytes 25165828
  11.3 2.0 %collective-permute-start.4 = (bf16[8,64,256]{2,1,0:T(8,128)(2,1)S(1)}, bf16[8,64,256]{2,1,0:T(8,128)(2,1)S(1)}, u32[]{:S(2)}, u32[]{:S(2)}) collective-permute-start(bf16[8,64,256]{2,1,0:T(8,128)(2,1)S(1)} %collective-permute-done.2.refs_0_), channel_id=1, source_target_pairs={{0,8},{8,0},{16,24},{24,16},{1,9},{9,1},{17,25},{25,17},{2,10},{10... | collective-permute-start | bytes 786440 | tf_op jit(solution)/shard_map/ppermute | solution.py:235
  11.3 8.7 %collective-permute-start.1 = (bf16[8,64,256]{2,1,0:T(8,128)(2,1)S(1)}, bf16[8,64,256]{2,1,0:T(8,128)(2,1)S(1)}, u32[]{:S(2)}, u32[]{:S(2)}) collective-permute-start(bf16[8,64,256]{2,1,0:T(8,128)(2,1)S(1)} %get-tuple-element.24.refs_0_), channel_id=1, source_target_pairs={{0,16},{8,24},{16,0},{24,8},{1,17},{9,25},{17,1},{25,9},{2,18},{10... | collective-permute-start | bytes 786440 | tf_op jit(solution)/shard_map/ppermute | solution.py:232
  13.1 10.9 %collective-permute-start = (bf16[8,64,256]{2,1,0:T(8,128)(2,1)S(1)}, bf16[8,64,256]{2,1,0:T(8,128)(2,1)S(1)}, u32[]{:S(2)}, u32[]{:S(2)}) collective-permute-start(bf16[8,64,256]{2,1,0:T(8,128)(2,1)S(1)} %get-tuple-element.24.refs_0_), channel_id=1, source_target_pairs={{0,8},{8,0},{16,24},{24,16},{1,9},{9,1},{17,25},{25,17},{2,10},{10... | collective-permute-start | bytes 786440 | tf_op jit(solution)/shard_map/ppermute | solution.py:235
  20.1 4.1 %collective-permute-start.5 = (bf16[8,64,256]{2,1,0:T(8,128)(2,1)S(1)}, bf16[8,64,256]{2,1,0:T(8,128)(2,1)S(1)}, u32[]{:S(2)}, u32[]{:S(2)}) collective-permute-start(bf16[8,64,256]{2,1,0:T(8,128)(2,1)S(1)} %collective-permute-done.1.refs_2_), channel_id=1, source_target_pairs={{0,8},{8,0},{16,24},{24,16},{1,9},{9,1},{17,25},{25,17},{2,10},{10... | collective-permute-start | bytes 786440 | tf_op jit(solution)/shard_map/ppermute | solution.py:235
  20.1 9.9 %collective-permute-start.11 = (s16[2,272,256]{2,1,0:T(8,128)(2,1)S(1)}, s16[2,272,256]{2,1,0:T(8,128)(2,1)S(1)}, u32[]{:S(2)}, u32[]{:S(2)}) collective-permute-start(s16[2,272,256]{2,1,0:T(8,128)(2,1)S(1)} %get-tuple-element.37), channel_id=1, source_target_pairs={{0,1},{1,0},{2,3},{3,2},{4,5},{5,4},{6,7},{7,6},{8,9},{9,8},{10,11... | collective-permute-start | bytes 835592 | tf_op jit(solution)/shard_map/ppermute | solution.py:239
  21.8 13.7 %collective-permute-start.12 = (s16[2,272,256]{2,1,0:T(8,128)(2,1)S(1)}, s16[2,272,256]{2,1,0:T(8,128)(2,1)S(1)}, u32[]{:S(2)}, u32[]{:S(2)}) collective-permute-start(s16[2,272,256]{2,1,0:T(8,128)(2,1)S(1)} %get-tuple-element.38), channel_id=1, source_target_pairs={{0,1},{1,0},{2,3},{3,2},{4,5},{5,4},{6,7},{7,6},{8,9},{9,8},{10,11... | collective-permute-start | bytes 835592 | tf_op jit(solution)/shard_map/ppermute | solution.py:239
  22.2 20.3 %collective-permute-start.6 = (s16[2,272,256]{2,1,0:T(8,128)(2,1)S(1)}, s16[2,272,256]{2,1,0:T(8,128)(2,1)S(1)}, u32[]{:S(2)}, u32[]{:S(2)}) collective-permute-start(s16[2,272,256]{2,1,0:T(8,128)(2,1)S(1)} %get-tuple-element.28), channel_id=1, source_target_pairs={{0,1},{1,0},{2,3},{3,2},{4,5},{5,4},{6,7},{7,6},{8,9},{9,8},{10,11... | collective-permute-start | bytes 835592 | tf_op jit(solution)/shard_map/ppermute | solution.py:239
  24.0 23.1 %collective-permute-start.7 = (s16[2,272,256]{2,1,0:T(8,128)(2,1)S(1)}, s16[2,272,256]{2,1,0:T(8,128)(2,1)S(1)}, u32[]{:S(2)}, u32[]{:S(2)}) collective-permute-start(s16[2,272,256]{2,1,0:T(8,128)(2,1)S(1)} %get-tuple-element.30), channel_id=1, source_target_pairs={{0,1},{1,0},{2,3},{3,2},{4,5},{5,4},{6,7},{7,6},{8,9},{9,8},{10,11... | collective-permute-start | bytes 835592 | tf_op jit(solution)/shard_map/ppermute | solution.py:239
  24.2 3.4 %copy-start.1 = (bf16[64,256,256]{2,1,0:T(8,128)(2,1)S(1)}, bf16[64,256,256]{2,1,0:T(8,128)(2,1)}, u32[]{:S(2)}) copy-start(bf16[64,256,256]{2,1,0:T(8,128)(2,1)} %copy-done) | copy-start | bytes 25165828
  36.4 16.1 %collective-permute-start.13 = (s16[272,256]{1,0:T(8,128)(2,1)S(1)}, s16[272,256]{1,0:T(8,128)(2,1)S(1)}, u32[]{:S(2)}, u32[]{:S(2)}) collective-permute-start(s16[272,256]{1,0:T(8,128)(2,1)S(1)} %get-tuple-element.40), channel_id=1, source_target_pairs={{0,2},{1,3},{2,4},{3,5},{4,6},{5,7},{6,0},{7,1},{8,10},{9,11},{10,... | collective-permute-start | bytes 417800 | tf_op jit(solution)/shard_map/ppermute | solution.py:242
  38.2 15.8 %collective-permute-start.14 = (s16[272,256]{1,0:T(8,128)(2,1)S(1)}, s16[272,256]{1,0:T(8,128)(2,1)S(1)}, u32[]{:S(2)}, u32[]{:S(2)}) collective-permute-start(s16[272,256]{1,0:T(8,128)(2,1)S(1)} %get-tuple-element.41), channel_id=1, source_target_pairs={{0,4},{1,5},{2,6},{3,7},{4,0},{5,1},{6,2},{7,3},{8,12},{9,13},{10,... | collective-permute-start | bytes 417800 | tf_op jit(solution)/shard_map/ppermute | solution.py:242
  40.8 13.2 %collective-permute-start.15 = (s16[272,256]{1,0:T(8,128)(2,1)S(1)}, s16[272,256]{1,0:T(8,128)(2,1)S(1)}, u32[]{:S(2)}, u32[]{:S(2)}) collective-permute-start(s16[272,256]{1,0:T(8,128)(2,1)S(1)} %get-tuple-element.42), channel_id=1, source_target_pairs={{0,6},{1,7},{2,0},{3,1},{4,2},{5,3},{6,4},{7,5},{8,14},{9,15},{10,... | collective-permute-start | bytes 417800 | tf_op jit(solution)/shard_map/ppermute | solution.py:242
  48.0 8.5 %collective-permute-start.8 = (s16[272,256]{1,0:T(8,128)(2,1)S(1)}, s16[272,256]{1,0:T(8,128)(2,1)S(1)}, u32[]{:S(2)}, u32[]{:S(2)}) collective-permute-start(s16[272,256]{1,0:T(8,128)(2,1)S(1)} %get-tuple-element.33), channel_id=1, source_target_pairs={{0,2},{1,3},{2,4},{3,5},{4,6},{5,7},{6,0},{7,1},{8,10},{9,11},{10,... | collective-permute-start | bytes 417800 | tf_op jit(solution)/shard_map/ppermute | solution.py:242
  49.9 11.7 %collective-permute-start.9 = (s16[272,256]{1,0:T(8,128)(2,1)S(1)}, s16[272,256]{1,0:T(8,128)(2,1)S(1)}, u32[]{:S(2)}, u32[]{:S(2)}) collective-permute-start(s16[272,256]{1,0:T(8,128)(2,1)S(1)} %get-tuple-element.34), channel_id=1, source_target_pairs={{0,4},{1,5},{2,6},{3,7},{4,0},{5,1},{6,2},{7,3},{8,12},{9,13},{10,... | collective-permute-start | bytes 417800 | tf_op jit(solution)/shard_map/ppermute | solution.py:242
  52.5 9.1 %collective-permute-start.10 = (s16[272,256]{1,0:T(8,128)(2,1)S(1)}, s16[272,256]{1,0:T(8,128)(2,1)S(1)}, u32[]{:S(2)}, u32[]{:S(2)}) collective-permute-start(s16[272,256]{1,0:T(8,128)(2,1)S(1)} %get-tuple-element.35), channel_id=1, source_target_pairs={{0,6},{1,7},{2,0},{3,1},{4,2},{5,3},{6,4},{7,5},{8,14},{9,15},{10,... | collective-permute-start | bytes 417800 | tf_op jit(solution)/shard_map/ppermute | solution.py:242

commit v3 on v2

v3 whole, which is shorter than its diff:
```python
import functools

import jax
import jax.numpy as jnp
from jax import lax
from jax.experimental import pallas as pl
from jax.experimental.pallas import tpu as pltpu
from jax.sharding import PartitionSpec as P

CD_COL = 8
PAIR_TILES_ROW = 8
PARTS = (2, 1, 1)
LOADS = 8
LANES = 128
LEVELS = 32000.0
STEPS = 64.0
SMALLEST = 2.0**-110
VMEM_LIMIT = 16 * 1024 * 1024

F32 = jnp.float32
BF16 = jnp.bfloat16
I16 = jnp.int16

IN_VMEM = pl.BlockSpec(memory_space=pltpu.VMEM)
IN_SMEM = pl.BlockSpec(memory_space=pltpu.SMEM)
IN_HBM = pl.BlockSpec(memory_space=pl.ANY)


def held(x):
    return pltpu.with_memory_space_constraint(x, pltpu.VMEM)


def after(x, *others):
    return lax.optimization_barrier((x, *others))[0]


def kernel_call(body, outs, ins, scratch=(), name=None, outputs=IN_VMEM):
    return pl.pallas_call(
        body,
        out_shape=outs,
        in_specs=ins,
        out_specs=outputs if outputs is not IN_VMEM else jax.tree.map(lambda _: IN_VMEM, outs),
        scratch_shapes=list(scratch),
        compiler_params=pltpu.CompilerParams(vmem_limit_bytes=VMEM_LIMIT),
        cost_estimate=pl.CostEstimate(flops=1, bytes_accessed=1, transcendentals=0),
        name=name,
    )


def code(block):
    top = jnp.maximum(jnp.max(jnp.abs(block), axis=0, keepdims=True), SMALLEST)
    exponent = jnp.ceil(jnp.log2(top) * STEPS)
    scaled = block * (LEVELS * jnp.exp2(exponent * (-1.0 / STEPS)))
    return jnp.round(scaled).astype(jnp.int32).astype(I16), exponent


def store_exponents(ref, at, rows):
    tiles = len(rows)
    block = jnp.concatenate(list(rows) + [jnp.zeros_like(rows[0])] * (16 - tiles), axis=0)
    ref[at] = block.astype(jnp.int32).astype(I16)


def scales(exponents):
    return jnp.exp2(exponents.astype(jnp.int32).astype(F32) * (1.0 / STEPS)) * (1.0 / LEVELS)


def decode(block, scale):
    return block.astype(jnp.int32).astype(F32) * scale


def begin_kernel(parts, pieces, count_ref, cd_hbm, ab_hbm, amps_hbm, ints_hbm, *refs):
    outs, (slots_ref, table_ref, amps, flat, cd, ab, sems) = refs[:parts], refs[parts:]
    rows, tiles, width = amps.shape
    lanes, each = flat.shape[2], rows // parts
    per = ints_hbm.shape[0] // pieces
    pairs = slots_ref.shape[0] // 2
    copies = [pltpu.make_async_copy(amps_hbm, amps, sems.at[0])]
    copies += [pltpu.make_async_copy(cd_hbm, cd, sems.at[1]), pltpu.make_async_copy(ab_hbm, ab, sems.at[2])]
    for piece in range(pieces):
        part = pl.ds(piece * per, per)
        copies.append(pltpu.make_async_copy(ints_hbm.at[part], table_ref.at[part], sems.at[3 + piece]))
    for copy in copies:
        copy.start()

    def clear(pair, carry):
        slots_ref[pair] = 0
        slots_ref[pairs + pair] = CD_COL
        return carry

    def note(slot, carry):
        pair = ab[slot] * CD_COL + cd[slot]
        slots_ref[pair] = slot
        slots_ref[pairs + pair] = cd[slot]
        return carry

    lax.fori_loop(0, pairs, clear, 0)
    copies[0].wait()
    for half in range(width // lanes):
        columns = pl.ds(half * lanes, lanes)
        flat[half] = amps[:, :, columns].astype(F32).reshape(rows * tiles, lanes)
    here = lax.rem(lax.axis_index("col"), parts)
    for step in range(parts):
        part = lax.rem(here + step, parts)
        for tile in range(tiles):
            first = part * each * tiles + tile
            for half in range(width // lanes):
                picked = flat[half, pl.ds(first, each, stride=tiles), :]
                outs[step][tile, :, pl.ds(half * lanes, lanes)] = picked.astype(BF16)
    copies[1].wait()
    copies[2].wait()
    lax.fori_loop(0, count_ref[0], note, 0)
    for copy in copies[3:]:
        copy.wait()


def multiply(amps_refs, slots_ref, table_ref, left, use):
    tiles, each, width = amps_refs[0].shape
    pairs = slots_ref.shape[0] // 2
    rows = each * len(amps_refs)
    for tile in range(tiles):
        for block, ref in enumerate(amps_refs):
            left[tile, block * each : (block + 1) * each] = ref[tile]
    left[tiles] = jnp.zeros((rows, width), BF16)
    for ab in range(pairs // tiles):
        total = jnp.zeros((rows, table_ref.shape[2]), F32)
        for tile in range(tiles):
            pair = ab * tiles + tile
            total = total + jnp.dot(
                left[slots_ref[pairs + pair]], table_ref[slots_ref[pair]], preferred_element_type=F32
            )
        use(ab, total)


def keep_kernel(blocks, *refs):
    slots_ref, table_ref, keep_ref, left = refs[blocks:]
    each = refs[0].shape[1]

    def use(ab, total):
        for block in range(blocks):
            keep_ref[block, ab] = total[block * each : (block + 1) * each]

    multiply(refs[:blocks], slots_ref, table_ref, left, use)


def send_kernel(blocks, sizes, stacked, *refs):
    slots_ref, table_ref = refs[blocks : blocks + 2]
    send_refs, left = refs[blocks + 2 : -1], refs[-1]
    out_rows = refs[0].shape[1]
    exponents = {}
    tiles = slots_ref.shape[0] // 2 // CD_COL
    starts = [sum(sizes[:chunk]) for chunk in range(len(sizes))]

    def place(block, chunk):
        if stacked and chunk:
            return send_refs[1].at[chunk - 1, block]
        return send_refs[chunk].at[block]

    def use(ab, total):
        for block in range(blocks):
            for chunk, each in enumerate(sizes):
                at = block * out_rows + starts[chunk]
                coded, exponent = code(total[at : at + each])
                place(block, chunk)[ab * each : (ab + 1) * each] = coded
                exponents.setdefault((block, chunk), []).append(exponent)

    multiply(refs[:blocks], slots_ref, table_ref, left, use)
    for (block, chunk), rows in exponents.items():
        store_exponents(place(block, chunk), pl.ds(tiles * sizes[chunk], 16), rows)


def add_decoded(total, ref, ab, ab_tiles, factor):
    each = total.shape[0]
    return total + decode(ref[ab * each : (ab + 1) * each], factor[ab : ab + 1])


def tail_scales(ref, ab_tiles, each):
    return scales(ref[pl.ds(ab_tiles * each, 16)])


def code_into(ref, tiles):
    each = tiles[0].shape[0]
    exponents = []
    for ab, tile in enumerate(tiles):
        coded, exponent = code(tile)
        ref[ab * each : (ab + 1) * each] = coded
        exponents.append(exponent)
    store_exponents(ref, pl.ds(len(tiles) * each, 16), exponents)


def pair_kernel(start, stack, near_ref, far_ref, *refs):
    near, ab_tiles = near_ref.shape[:2]
    blocks = near + far_ref.shape[0]
    received, (kept_ref, sent_ref, sums) = refs[:-3], refs[-3:]
    each = sums.shape[2]
    half = len(received) // 2
    near_received = [ref if stack is None else ref.at[stack] for ref in received[:half]]
    row, col = lax.axis_index("row"), lax.axis_index("col")
    n_y, z = blocks // 2, lax.div(col, half + 1)
    places = []
    for m in range(blocks):
        wanted = z ^ m
        away = lax.rem(lax.div(row, 2) - lax.div(wanted, 2) + n_y, n_y)
        places.append(2 * away + lax.rem(row + wanted, 2))
    for block in range(blocks):
        keep_ref, mine = (near_ref, near_received) if block < near else (far_ref, received[half:])
        at = block if block < near else block - near
        factors = [tail_scales(ref.at[at], ab_tiles, each) for ref in mine]
        for ab in range(ab_tiles):
            total = keep_ref[at, ab, start : start + each]
            for ref, factor in zip(mine, factors):
                total = add_decoded(total, ref.at[at], ab, ab_tiles, factor)
            sums[block, ab] = total
    for m in range(0, blocks, 2):
        kept_ref[m // 2] = sums[places[m]]
        code_into(sent_ref.at[m // 2], [sums[places[m + 1], ab] for ab in range(ab_tiles)])


def halve_kernel(kept_ref, received_ref, next_ref, sent_ref):
    count, ab_tiles, each, width = kept_ref.shape
    for item in range(count):
        factor = tail_scales(received_ref.at[item], ab_tiles, each)
        tiles = [
            add_decoded(kept_ref[item, ab], received_ref.at[item], ab, ab_tiles, factor) for ab in range(ab_tiles)
        ]
        if item % 2:
            code_into(sent_ref.at[item // 2], tiles)
        else:
            for ab in range(ab_tiles):
                next_ref[item // 2, ab] = tiles[ab]


def last_kernel(*refs):
    flat, out_ref = refs[-1], refs[-2]
    rows, ab_tiles, width = out_ref.shape
    lanes = flat.shape[2]
    start = 0
    for kept_ref, received_ref in zip(refs[:-2:2], refs[1:-2:2]):
        each = kept_ref.shape[2]
        factor = tail_scales(received_ref.at[0], ab_tiles, each)
        for ab in range(ab_tiles):
            total = add_decoded(kept_ref[0, ab], received_ref.at[0], ab, ab_tiles, factor)
            for half in range(width // lanes):
                piece = total[:, half * lanes : (half + 1) * lanes]
                flat[half, pl.ds(start * ab_tiles + ab, each, stride=ab_tiles), :] = piece
        start += each
    for half in range(width // lanes):
        whole = flat[half].reshape(rows, ab_tiles, lanes)
        out_ref[:, :, pl.ds(half * lanes, lanes)] = whole.astype(out_ref.dtype)


def chunk_sizes(rows):
    parts = PARTS
    while parts[-1] > 1 and (rows % sum(parts) or (rows // sum(parts)) % 16):
        parts = (1,) * (len(parts) - 1)
    if rows % sum(parts) or (rows // sum(parts)) % 16:
        parts = (1,)
    return [rows // sum(parts) * part for part in parts]


def shards(n_row, n_col, amps, ints, task_cd, task_ab, task_count):
    n_x = n_col // n_row
    n_z = n_row
    n_y = n_row // 2
    rows, tiles, width = amps.shape
    out_rows = rows // n_x
    sizes = chunk_sizes(out_rows)
    pairs = PAIR_TILES_ROW * CD_COL
    other_parts = range(1, n_x)

    def along_y(array, step):
        return lax.ppermute(array, "row", [(r, (r + 2 * step) % n_row) for r in range(n_row)])

    def to_partner(array):
        return lax.ppermute(array, "row", [(r, r ^ 1) for r in range(n_row)])

    def along_x(array, step):
        pairs = [(c, c - c % n_x + (c % n_x + step) % n_x) for c in range(n_col)]
        return lax.ppermute(array, "col", pairs)

    def along_z(array, bit):
        return lax.ppermute(array, "col", [(c, (c // n_x ^ bit) * n_x + c % n_x) for c in range(n_col)])

    def coded(each, *lead):
        return pltpu.VMEM((*lead, PAIR_TILES_ROW * each + 16, width), I16)

    def summed(each, *lead):
        return pltpu.VMEM((*lead, PAIR_TILES_ROW, each, width), F32)

    def send_products(blocks, stacked):
        count = len(blocks)
        outs = [coded(each, count) for each in sizes]
        if stacked:
            outs = outs[:1] + [coded(sizes[-1], len(sizes) - 1, count)]
        return kernel_call(
            functools.partial(send_kernel, count, sizes, stacked),
            outs,
            [IN_VMEM] * count + [IN_SMEM, IN_VMEM],
            [pltpu.VMEM((tiles + 1, count * out_rows, width), BF16)],
            name="send_products",
        )(*map(held, blocks), slots, held(table))

    def keep_products(blocks):
        return kernel_call(
            functools.partial(keep_kernel, len(blocks)),
            pltpu.VMEM((len(blocks), PAIR_TILES_ROW, out_rows, width), F32),
            [IN_VMEM] * len(blocks) + [IN_SMEM, IN_VMEM],
            [pltpu.VMEM((tiles + 1, len(blocks) * out_rows, width), BF16)],
            name="keep_products",
        )(*map(held, blocks), slots, held(table))

    *mine, slots, table = pl.pallas_call(
        functools.partial(begin_kernel, n_x, LOADS),
        out_shape=[pltpu.VMEM((tiles, out_rows, width), BF16)] * n_x
        + [pltpu.SMEM((2 * pairs,), jnp.int32), pltpu.VMEM(ints.shape, BF16)],
        in_specs=[IN_SMEM] + [IN_HBM] * 4,
        out_specs=[IN_VMEM] * n_x + [IN_SMEM, IN_VMEM],
        scratch_shapes=[
            pltpu.VMEM(amps.shape, BF16),
            pltpu.VMEM((width // LANES, rows * tiles, LANES), F32),
            pltpu.SMEM(task_cd.shape, jnp.int32),
            pltpu.SMEM(task_ab.shape, jnp.int32),
            pltpu.SemaphoreType.DMA((3 + LOADS,)),
        ],
        compiler_params=pltpu.CompilerParams(vmem_limit_bytes=VMEM_LIMIT),
        cost_estimate=pl.CostEstimate(flops=1, bytes_accessed=1, transcendentals=0),
        name="begin",
    )(task_count, *(pltpu.with_memory_space_constraint(v, pltpu.HBM) for v in (task_cd, task_ab, amps, ints)))
    order = [*other_parts, 0]
    beside = {part: to_partner(mine[part]) for part in order}
    far = {part: [along_y(mine[part], k) for k in range(1, n_y)] for part in order}
    stacked = len(sizes) > 2
    near_sends = [send_products([mine[part], beside[part]], stacked) for part in other_parts]
    near_received = [[along_x(group, part) for part, group in zip(other_parts, groups)] for groups in zip(*near_sends)]
    near_keep = keep_products([after(mine[0], near_sends[-1][0]), beside[0]])

    def fetch(part, *ties):
        blocks = []
        for array in far[part]:
            array = after(array, *ties)
            blocks += [array, to_partner(array)]
        return blocks

    far_blocks = {part: fetch(part, near_keep) for part in other_parts}
    far_blocks = {part: [after(v, near_received[0][-1]) for v in blocks] for part, blocks in far_blocks.items()}
    far_sends = [send_products(far_blocks[part], False) for part in other_parts]
    far_received = []
    for q in range(len(sizes)):
        ties = near_received[1] if q else []
        far_received.append([along_x(after(sends[q], *ties), part) for part, sends in zip(other_parts, far_sends)])
    far_keep = keep_products(fetch(0, far_sends[-1][0], near_received[-1][-1]))

    last = []
    for q, each in enumerate(sizes):
        group = min(q, len(near_received) - 1)
        kept, sent = kernel_call(
            functools.partial(pair_kernel, sum(sizes[:q]), q - 1 if stacked and q else None),
            [summed(each, n_z // 2), coded(each, n_z // 2)],
            [IN_VMEM] * (2 * n_x),
            [summed(each, n_z)],
            name="pairs",
        )(held(near_keep), held(far_keep), *map(held, near_received[group]), *map(held, far_received[q]))
        received = along_z(sent, 1)
        bit, count = 2, n_z // 2
        while count > 1:
            count //= 2
            kept, sent = kernel_call(
                halve_kernel, [summed(each, count), coded(each, count)], [IN_VMEM] * 2, name="halve"
            )(held(kept), held(received))
            received = along_z(sent, bit)
            bit *= 2
        last += [kept, received]
    return kernel_call(
        last_kernel,
        jax.ShapeDtypeStruct((out_rows, PAIR_TILES_ROW, width), BF16),
        [IN_VMEM] * len(last),
        [pltpu.VMEM((width // LANES, out_rows * PAIR_TILES_ROW, LANES), F32)],
        name="last",
    )(*map(held, last))


def solution(mesh):
    return jax.shard_map(
        functools.partial(shards, mesh.shape["row"], mesh.shape["col"]),
        mesh=mesh,
        in_specs=(
            P("row", "col", None),
            P(("row", "col"), None, None),
            P(("row", "col")),
            P(("row", "col")),
            P(("row", "col")),
        ),
        out_specs=P("col", "row", None),
        check_vma=False,
    )
```

time: 63.7 us -> 55.7 us (0.87); the launches traced: 62.6 us -> 55.5 us
  local copies, waits for them, and re-layouts: 5.73 us -> 0 us
  starting transfers between devices: 21.4 us -> 20.4 us
    unnamed x10 -> x0, local copies, waits for them, and re-layouts: 5.73 us -> none
    ppermute x2, waiting for transfers between devices: 6.15 us -> 3.17 us  [along_y(): lax.ppermute(array, 'row', [(r, (r + 2 * step) % n_row) for r in range(n_...]
    ppermute x6, starting transfers between devices: 12.2 us -> 9.42 us  [along_z(): lax.ppermute(array, 'col', [(c, (c // n_x ^ bit) * n_x + c % n_x) for c i...]
    ppermute x4 -> x5, starting transfers between devices: 4.05 us -> 5.67 us  [along_x(): return lax.ppermute(array, 'col', pairs)]
    ppermute x4, waiting for transfers between devices: 0.01 us -> 1.54 us  [to_partner(): return lax.ppermute(array, 'row', [(r, r ^ 1) for r in range(n_row)])]
    ppermute x4 -> x5, waiting for transfers between devices: 10.1 us -> 11.5 us  [along_x(): return lax.ppermute(array, 'col', pairs)]
    pallas_call x8 -> x12, Pallas kernels: 11 us -> 11.1 us  [the longest x1 3.66 us: shards(): pl.pallas_call(functools.partial(begin_kernel, n_x, LOADS), out_shape=[pl...]
  transfers between devices with their start and end apart: 16 -> 17, of which waited for: 6 -> 12; matrix products, arithmetic and copies ran while one was open for 0% -> 0% of each run, Pallas kernels for 15% -> 11%
where the time goes in v3:
time: 55.7 us; the launch traced here: 55.5 us
  waiting for transfers between devices  23.4 us (42%)
  starting transfers between devices  20.4 us (37%)
  Pallas kernels  11.1 us (20%)
  between operations  0.72 us (1%)
    ppermute x5, waiting for transfers between devices, along_x(): return lax.ppermute(array, 'col', pairs)  11.5 us
    ppermute x6, starting transfers between devices, along_z(): lax.ppermute(array, 'col', [(c, (c // n_x ^ bit) * n_x + c % n_x) for c i...  9.42 us
    ppermute x6, waiting for transfers between devices, along_z(): lax.ppermute(array, 'col', [(c, (c // n_x ^ bit) * n_x + c % n_x) for c i...  7.23 us
    ppermute x5, starting transfers between devices, along_x(): return lax.ppermute(array, 'col', pairs)  5.67 us
    ppermute x2, starting transfers between devices, along_y(): lax.ppermute(array, 'row', [(r, (r + 2 * step) % n_row) for r in range(n_...  4.69 us
    pallas_call x1, Pallas kernels, shards(): pl.pallas_call(functools.partial(begin_kernel, n_x, LOADS), out_shape=[pl...  3.66 us
    ppermute x2, waiting for transfers between devices, along_y(): lax.ppermute(array, 'row', [(r, (r + 2 * step) % n_row) for r in range(n_...  3.17 us
    pallas_call x2, Pallas kernels, send_products(): kernel_call(functools.partial(send_kernel, count, sizes, stacked), outs,...  2.71 us
  transfers between devices with their start and end apart: 17, of which 12 were waited for; matrix products, arithmetic and copies ran while one was open for 0% of the time, Pallas kernels for 11%

profile of v3, /device:TPU:0, one launch (start us, length us, event | category | flops | bytes accessed | tf_op | source)
XLA Modules:
  0.0 55.5 jit_solution(10728666512604773567)
XLA Ops:
  0.7 3.7 %begin.1 = (bf16[8,64,256]{2,1,0:T(8,128)(2,1)S(1)}, bf16[8,64,256]{2,1,0:T(8,128)(2,1)S(1)}, s32[128]{0:T(128)S(4)}, bf16[64,256,256]{2,1,0:T(8,128)(2,1)S(1)}) custom-call(s32[1]{0:T(128)S(6)} %copy.6.count_ref, s32[64]{0:T(128)} %cd_hbm.1, s32[64]{0:T(128)} %ab_hbm.1, bf16[128,8,256]{2,1,0:T(8,128)(2,1)} %amps_hbm.1, bf16[64,256,256]{2,1,0:T(8,128)(2,1)} %ints_hbm.1), custom_call_target="tpu_custom_call" | custom-call | flops 1 | bytes 1 | tf_op jit(solution)/shard_map/begin/pallas_call | solution.py:311
  4.3 0.5 collective-permute-start
  4.8 0.1 collective-permute-start.1
  4.9 2.9 %collective-permute-start.3 = (bf16[8,64,256]{2,1,0:T(8,128)(2,1)S(1)}, bf16[8,64,256]{2,1,0:T(8,128)(2,1)S(1)}, u32[]{:S(2)}, u32[]{:S(2)}) collective-permute-start(bf16[8,64,256]{2,1,0:T(8,128)(2,1)S(1)} %get-tuple-element.34.refs_0_), channel_id=1, source_target_pairs={{0,16},{8,24},{16,0},{24,8},{1,17},{9,25},{17,1},{25,9},{2,18},{10... | collective-permute-start | bytes 786440 | tf_op jit(solution)/shard_map/ppermute | solution.py:271
  7.9 0.0 collective-permute-done.refs_1_
  7.9 1.4 %send_products.2 = (s16[2,272,256]{2,1,0:T(8,128)(2,1)S(1)}, s16[2,2,144,256]{3,2,1,0:T(8,128)(2,1)S(1)}) custom-call(bf16[8,64,256]{2,1,0:T(8,128)(2,1)S(1)} %get-tuple-element.34.refs_0_, bf16[8,64,256]{2,1,0:T(8,128)(2,1)S(1)} %collective-permute-done.refs_1_, s32[128]{0:T(128)S(4)} %get-tuple-element.35.refs_2_, ...), custom_call_target="tpu_custom_call" | custom-call | flops 1 | bytes 1 | tf_op jit(solution)/shard_map/send_products/pallas_call | solution.py:294
  9.2 1.6 %collective-permute-start.4 = (s16[2,272,256]{2,1,0:T(8,128)(2,1)S(1)}, s16[2,272,256]{2,1,0:T(8,128)(2,1)S(1)}, u32[]{:S(2)}, u32[]{:S(2)}) collective-permute-start(s16[2,272,256]{2,1,0:T(8,128)(2,1)S(1)} %get-tuple-element.37), channel_id=1, source_target_pairs={{0,1},{1,0},{2,3},{3,2},{4,5},{5,4},{6,7},{7,6},{8,9},{9,8},{10,11... | collective-permute-start | bytes 835592 | tf_op jit(solution)/shard_map/ppermute | solution.py:278
  10.8 0.5 collective-permute-start.6
  11.3 0.0 collective-permute-done.1.refs_1_
  11.3 1.3 %keep_products.2.near_ref = f32[2,8,64,256]{3,2,1,0:T(8,128)S(1)} custom-call(bf16[8,64,256]{2,1,0:T(8,128)(2,1)S(1)} %get-tuple-element.38.refs_0_, bf16[8,64,256]{2,1,0:T(8,128)(2,1)S(1)} %collective-permute-done.1.refs_1_, s32[128]{0:T(128)S(4)} %get-tuple-element.35.refs_2_, bf16[64,256,256]{2,1,0:T(8,128)(2,1)S(1)} %get-tuple-element.36.refs_3_), custom_call_target="tpu_custom_call" | custom-call | flops 1 | bytes 1 | tf_op jit(solution)/shard_map/keep_products/pallas_call | solution.py:303
  12.6 1.8 %collective-permute-done.3.refs_0_ = bf16[8,64,256]{2,1,0:T(8,128)(2,1)S(1)} collective-permute-done((bf16[8,64,256]{2,1,0:T(8,128)(2,1)S(1)}, bf16[8,64,256]{2,1,0:T(8,128)(2,1)S(1)}, u32[]{:S(2)}, u32[]{:S(2)}) %collective-permute-start.3) | collective-permute-done | bytes 262176 | tf_op jit(solution)/shard_map/ppermute | solution.py:271
  14.4 0.0 collective-permute-start.5
  14.4 1.7 %collective-permute-start.2 = (bf16[8,64,256]{2,1,0:T(8,128)(2,1)S(1)}, bf16[8,64,256]{2,1,0:T(8,128)(2,1)S(1)}, u32[]{:S(2)}, u32[]{:S(2)}) collective-permute-start(bf16[8,64,256]{2,1,0:T(8,128)(2,1)S(1)} %get-tuple-element.38.refs_0_), channel_id=1, source_target_pairs={{0,16},{8,24},{16,0},{24,8},{1,17},{9,25},{17,1},{25,9},{2,18},{10... | collective-permute-start | bytes 786440 | tf_op jit(solution)/shard_map/ppermute | solution.py:271
  16.2 2.7 %collective-permute-done.4.refs_0_ = s16[2,272,256]{2,1,0:T(8,128)(2,1)S(1)} collective-permute-done((s16[2,272,256]{2,1,0:T(8,128)(2,1)S(1)}, s16[2,272,256]{2,1,0:T(8,128)(2,1)S(1)}, u32[]{:S(2)}, u32[]{:S(2)}) %collective-permute-start.4) | collective-permute-done | bytes 278560 | tf_op jit(solution)/shard_map/ppermute | solution.py:278
  18.8 0.0 collective-permute-done.5.refs_1_
  18.8 1.4 %send_products.3 = (s16[2,272,256]{2,1,0:T(8,128)(2,1)S(1)}, s16[2,144,256]{2,1,0:T(8,128)(2,1)S(1)}, s16[2,144,256]{2,1,0:T(8,128)(2,1)S(1)}) custom-call(bf16[8,64,256]{2,1,0:T(8,128)(2,1)S(1)} %collective-permute-done.3.refs_0_, bf16[8,64,256]{2,1,0:T(8,128)(2,1)S(1)} %collective-permute-done.5.refs_1_, s32[128]{0:T(128)S(4)} %get-tuple-element.35.refs_2_, ...), custom_call_target="tpu_custom_call" | custom-call | flops 1 | bytes 1 | tf_op jit(solution)/shard_map/send_products/pallas_call | solution.py:294
  20.2 1.6 %collective-permute-start.8 = (s16[2,272,256]{2,1,0:T(8,128)(2,1)S(1)}, s16[2,272,256]{2,1,0:T(8,128)(2,1)S(1)}, u32[]{:S(2)}, u32[]{:S(2)}) collective-permute-start(s16[2,272,256]{2,1,0:T(8,128)(2,1)S(1)} %get-tuple-element.42), channel_id=1, source_target_pairs={{0,1},{1,0},{2,3},{3,2},{4,5},{5,4},{6,7},{7,6},{8,9},{9,8},{10,11... | collective-permute-start | bytes 835592 | tf_op jit(solution)/shard_map/ppermute | solution.py:278
  21.8 1.4 %collective-permute-done.2.refs_0_ = bf16[8,64,256]{2,1,0:T(8,128)(2,1)S(1)} collective-permute-done((bf16[8,64,256]{2,1,0:T(8,128)(2,1)S(1)}, bf16[8,64,256]{2,1,0:T(8,128)(2,1)S(1)}, u32[]{:S(2)}, u32[]{:S(2)}) %collective-permute-start.2) | collective-permute-done | bytes 262176 | tf_op jit(solution)/shard_map/ppermute | solution.py:271
  23.1 2.0 %collective-permute-done.6.refs_0_ = s16[2,2,144,256]{3,2,1,0:T(8,128)(2,1)S(1)} collective-permute-done((s16[2,2,144,256]{3,2,1,0:T(8,128)(2,1)S(1)}, s16[2,2,144,256]{3,2,1,0:T(8,128)(2,1)S(1)}, u32[]{:S(2)}, u32[]{:S(2)}) %collective-permute-start.6) | collective-permute-done | bytes 294944 | tf_op jit(solution)/shard_map/ppermute | solution.py:278
  25.2 0.0 collective-permute-start.7
  25.2 1.5 %collective-permute-done.7.refs_1_ = bf16[8,64,256]{2,1,0:T(8,128)(2,1)S(1)} collective-permute-done((bf16[8,64,256]{2,1,0:T(8,128)(2,1)S(1)}, bf16[8,64,256]{2,1,0:T(8,128)(2,1)S(1)}, u32[]{:S(2)}, u32[]{:S(2)}) %collective-permute-start.7) | collective-permute-done | bytes 262176 | tf_op jit(solution)/shard_map/ppermute | solution.py:274
  26.7 1.3 %keep_products.3.far_ref = f32[2,8,64,256]{3,2,1,0:T(8,128)S(1)} custom-call(bf16[8,64,256]{2,1,0:T(8,128)(2,1)S(1)} %collective-permute-done.2.refs_0_, bf16[8,64,256]{2,1,0:T(8,128)(2,1)S(1)} %collective-permute-done.7.refs_1_, s32[128]{0:T(128)S(4)} %get-tuple-element.35.refs_2_, bf16[64,256,256]{2,1,0:T(8,128)(2,1)S(1)} %get-tuple-element.36.refs_3_), custom_call_target="tpu_custom_call" | custom-call | flops 1 | bytes 1 | tf_op jit(solution)/shard_map/keep_products/pallas_call | solution.py:303
  28.0 2.0 %collective-permute-done.8.refs_1_ = s16[2,272,256]{2,1,0:T(8,128)(2,1)S(1)} collective-permute-done((s16[2,272,256]{2,1,0:T(8,128)(2,1)S(1)}, s16[2,272,256]{2,1,0:T(8,128)(2,1)S(1)}, u32[]{:S(2)}, u32[]{:S(2)}) %collective-permute-start.8) | collective-permute-done | bytes 278560 | tf_op jit(solution)/shard_map/ppermute | solution.py:278
  29.9 0.4 pairs.3
  30.4 1.6 %collective-permute-start.9 = (s16[2,272,256]{2,1,0:T(8,128)(2,1)S(1)}, s16[2,272,256]{2,1,0:T(8,128)(2,1)S(1)}, u32[]{:S(2)}, u32[]{:S(2)}) collective-permute-start(s16[2,272,256]{2,1,0:T(8,128)(2,1)S(1)} %get-tuple-element.46), channel_id=1, source_target_pairs={{0,2},{1,3},{2,0},{3,1},{4,6},{5,7},{6,4},{7,5},{8,10},{9,11},{10,... | collective-permute-start | bytes 835592 | tf_op jit(solution)/shard_map/ppermute | solution.py:281
  32.0 1.5 %collective-permute-start.14 = (s16[2,144,256]{2,1,0:T(8,128)(2,1)S(1)}, s16[2,144,256]{2,1,0:T(8,128)(2,1)S(1)}, u32[]{:S(2)}, u32[]{:S(2)}) collective-permute-start(s16[2,144,256]{2,1,0:T(8,128)(2,1)S(1)} %get-tuple-element.56), channel_id=1, source_target_pairs={{0,1},{1,0},{2,3},{3,2},{4,5},{5,4},{6,7},{7,6},{8,9},{9,8},{10,11... | collective-permute-start | bytes 442376 | tf_op jit(solution)/shard_map/ppermute | solution.py:278
  33.5 0.5 collective-permute-start.11
  34.0 3.9 %collective-permute-done.14.refs_1_ = s16[2,144,256]{2,1,0:T(8,128)(2,1)S(1)} collective-permute-done((s16[2,144,256]{2,1,0:T(8,128)(2,1)S(1)}, s16[2,144,256]{2,1,0:T(8,128)(2,1)S(1)}, u32[]{:S(2)}, u32[]{:S(2)}) %collective-permute-start.14) | collective-permute-done | bytes 147488 | tf_op jit(solution)/shard_map/ppermute | solution.py:278
  38.0 0.2 pairs.5
  38.2 0.5 collective-permute-start.15
  38.7 0.8 %collective-permute-done.11.refs_1_ = s16[2,144,256]{2,1,0:T(8,128)(2,1)S(1)} collective-permute-done((s16[2,144,256]{2,1,0:T(8,128)(2,1)S(1)}, s16[2,144,256]{2,1,0:T(8,128)(2,1)S(1)}, u32[]{:S(2)}, u32[]{:S(2)}) %collective-permute-start.11) | collective-permute-done | bytes 147488 | tf_op jit(solution)/shard_map/ppermute | solution.py:278
  39.6 0.2 pairs.4
  39.8 0.8 %collective-permute-start.12 = (s16[2,144,256]{2,1,0:T(8,128)(2,1)S(1)}, s16[2,144,256]{2,1,0:T(8,128)(2,1)S(1)}, u32[]{:S(2)}, u32[]{:S(2)}) collective-permute-start(s16[2,144,256]{2,1,0:T(8,128)(2,1)S(1)} %get-tuple-element.52), channel_id=1, source_target_pairs={{0,2},{1,3},{2,0},{3,1},{4,6},{5,7},{6,4},{7,5},{8,10},{9,11},{10,... | collective-permute-start | bytes 442376 | tf_op jit(solution)/shard_map/ppermute | solution.py:281
  40.6 0.0 collective-permute-done.9.received_ref
  40.6 0.2 halve.3
  40.8 2.7 %collective-permute-start.10 = (s16[1,272,256]{2,1,0:T(8,128)(2,1)S(1)}, s16[1,272,256]{2,1,0:T(8,128)(2,1)S(1)}, u32[]{:S(2)}, u32[]{:S(2)}) collective-permute-start(s16[1,272,256]{2,1,0:T(8,128)(2,1)S(1)} %get-tuple-element.48), channel_id=1, source_target_pairs={{0,4},{1,5},{2,6},{3,7},{4,0},{5,1},{6,2},{7,3},{8,12},{9,13},{10,... | collective-permute-start | bytes 417800 | tf_op jit(solution)/shard_map/ppermute | solution.py:281
  43.4 2.3 %collective-permute-done.15.received_ref = s16[2,144,256]{2,1,0:T(8,128)(2,1)S(1)} collective-permute-done((s16[2,144,256]{2,1,0:T(8,128)(2,1)S(1)}, s16[2,144,256]{2,1,0:T(8,128)(2,1)S(1)}, u32[]{:S(2)}, u32[]{:S(2)}) %collective-permute-start.15) | collective-permute-done | bytes 147488 | tf_op jit(solution)/shard_map/ppermute | solution.py:281
  45.7 0.1 halve.5
  45.8 2.0 %collective-permute-start.16 = (s16[1,144,256]{2,1,0:T(8,128)(2,1)S(1)}, s16[1,144,256]{2,1,0:T(8,128)(2,1)S(1)}, u32[]{:S(2)}, u32[]{:S(2)}) collective-permute-start(s16[1,144,256]{2,1,0:T(8,128)(2,1)S(1)} %get-tuple-element.60), channel_id=1, source_target_pairs={{0,4},{1,5},{2,6},{3,7},{4,0},{5,1},{6,2},{7,3},{8,12},{9,13},{10,... | collective-permute-start | bytes 221192 | tf_op jit(solution)/shard_map/ppermute | solution.py:281
  47.8 1.0 %collective-permute-done.12.received_ref = s16[2,144,256]{2,1,0:T(8,128)(2,1)S(1)} collective-permute-done((s16[2,144,256]{2,1,0:T(8,128)(2,1)S(1)}, s16[2,144,256]{2,1,0:T(8,128)(2,1)S(1)}, u32[]{:S(2)}, u32[]{:S(2)}) %collective-permute-start.12) | collective-permute-done | bytes 147488 | tf_op jit(solution)/shard_map/ppermute | solution.py:281
  48.9 0.1 halve.4
  49.0 1.8 %collective-permute-start.13 = (s16[1,144,256]{2,1,0:T(8,128)(2,1)S(1)}, s16[1,144,256]{2,1,0:T(8,128)(2,1)S(1)}, u32[]{:S(2)}, u32[]{:S(2)}) collective-permute-start(s16[1,144,256]{2,1,0:T(8,128)(2,1)S(1)} %get-tuple-element.54), channel_id=1, source_target_pairs={{0,4},{1,5},{2,6},{3,7},{4,0},{5,1},{6,2},{7,3},{8,12},{9,13},{10,... | collective-permute-start | bytes 221192 | tf_op jit(solution)/shard_map/ppermute | solution.py:281
  50.7 3.1 %collective-permute-done.16.refs_5_ = s16[1,144,256]{2,1,0:T(8,128)(2,1)S(1)} collective-permute-done((s16[1,144,256]{2,1,0:T(8,128)(2,1)S(1)}, s16[1,144,256]{2,1,0:T(8,128)(2,1)S(1)}, u32[]{:S(2)}, u32[]{:S(2)}) %collective-permute-start.16) | collective-permute-done | bytes 73760 | tf_op jit(solution)/shard_map/ppermute | solution.py:281
  53.9 0.8 %collective-permute-done.13.refs_3_ = s16[1,144,256]{2,1,0:T(8,128)(2,1)S(1)} collective-permute-done((s16[1,144,256]{2,1,0:T(8,128)(2,1)S(1)}, s16[1,144,256]{2,1,0:T(8,128)(2,1)S(1)}, u32[]{:S(2)}, u32[]{:S(2)}) %collective-permute-start.13) | collective-permute-done | bytes 73760 | tf_op jit(solution)/shard_map/ppermute | solution.py:281
  54.7 0.0 collective-permute-done.10.refs_1_
  54.7 0.9 %last.1 = bf16[64,8,256]{2,1,0:T(8,128)(2,1)} custom-call(f32[1,8,32,256]{3,2,1,0:T(8,128)S(1)} %get-tuple-element.47.refs_0_, s16[1,272,256]{2,1,0:T(8,128)(2,1)S(1)} %collective-permute-done.10.refs_1_, f32[1,8,16,256]{3,2,1,0:T(8,128)S(1)} %get-tuple-element.53.refs_2_, s16[1,144,256]{2,1,0:T(8,128)(2,1)S(1)} %collective-permute-done.13.refs_3_, ...), custom_call_target="tpu_custom_call" | custom-call | flops 1 | bytes 1 | tf_op jit(solution)/shard_map/last/pallas_call | solution.py:372
Async XLA Ops:
  4.3 3.5 %collective-permute-start = (bf16[8,64,256]{2,1,0:T(8,128)(2,1)S(1)}, bf16[8,64,256]{2,1,0:T(8,128)(2,1)S(1)}, u32[]{:S(2)}, u32[]{:S(2)}) collective-permute-start(bf16[8,64,256]{2,1,0:T(8,128)(2,1)S(1)} %get-tuple-element.34.refs_0_), channel_id=1, source_target_pairs={{0,8},{8,0},{16,24},{24,16},{1,9},{9,1},{17,25},{25,17},{2,10},{10... | collective-permute-start | bytes 786440 | tf_op jit(solution)/shard_map/ppermute | solution.py:274
  4.8 6.5 %collective-permute-start.1 = (bf16[8,64,256]{2,1,0:T(8,128)(2,1)S(1)}, bf16[8,64,256]{2,1,0:T(8,128)(2,1)S(1)}, u32[]{:S(2)}, u32[]{:S(2)}) collective-permute-start(bf16[8,64,256]{2,1,0:T(8,128)(2,1)S(1)} %get-tuple-element.38.refs_0_), channel_id=1, source_target_pairs={{0,8},{8,0},{16,24},{24,16},{1,9},{9,1},{17,25},{25,17},{2,10},{10... | collective-permute-start | bytes 786440 | tf_op jit(solution)/shard_map/ppermute | solution.py:274
  4.9 9.5 %collective-permute-start.3 = (bf16[8,64,256]{2,1,0:T(8,128)(2,1)S(1)}, bf16[8,64,256]{2,1,0:T(8,128)(2,1)S(1)}, u32[]{:S(2)}, u32[]{:S(2)}) collective-permute-start(bf16[8,64,256]{2,1,0:T(8,128)(2,1)S(1)} %get-tuple-element.34.refs_0_), channel_id=1, source_target_pairs={{0,16},{8,24},{16,0},{24,8},{1,17},{9,25},{17,1},{25,9},{2,18},{10... | collective-permute-start | bytes 786440 | tf_op jit(solution)/shard_map/ppermute | solution.py:271
  9.2 9.6 %collective-permute-start.4 = (s16[2,272,256]{2,1,0:T(8,128)(2,1)S(1)}, s16[2,272,256]{2,1,0:T(8,128)(2,1)S(1)}, u32[]{:S(2)}, u32[]{:S(2)}) collective-permute-start(s16[2,272,256]{2,1,0:T(8,128)(2,1)S(1)} %get-tuple-element.37), channel_id=1, source_target_pairs={{0,1},{1,0},{2,3},{3,2},{4,5},{5,4},{6,7},{7,6},{8,9},{9,8},{10,11... | collective-permute-start | bytes 835592 | tf_op jit(solution)/shard_map/ppermute | solution.py:278
  10.8 14.4 %collective-permute-start.6 = (s16[2,2,144,256]{3,2,1,0:T(8,128)(2,1)S(1)}, s16[2,2,144,256]{3,2,1,0:T(8,128)(2,1)S(1)}, u32[]{:S(2)}, u32[]{:S(2)}) collective-permute-start(s16[2,2,144,256]{3,2,1,0:T(8,128)(2,1)S(1)} %get-tuple-element.43), channel_id=1, source_target_pairs={{0,1},{1,0},{2,3},{3,2},{4,5},{5,4},{6,7},{7,6},{8,9},{9,8},{10,11... | collective-permute-start | bytes 884744 | tf_op jit(solution)/shard_map/ppermute | solution.py:278
  14.4 4.4 %collective-permute-start.5 = (bf16[8,64,256]{2,1,0:T(8,128)(2,1)S(1)}, bf16[8,64,256]{2,1,0:T(8,128)(2,1)S(1)}, u32[]{:S(2)}, u32[]{:S(2)}) collective-permute-start(bf16[8,64,256]{2,1,0:T(8,128)(2,1)S(1)} %collective-permute-done.3.refs_0_), channel_id=1, source_target_pairs={{0,8},{8,0},{16,24},{24,16},{1,9},{9,1},{17,25},{25,17},{2,10},{10... | collective-permute-start | bytes 786440 | tf_op jit(solution)/shard_map/ppermute | solution.py:274
  14.4 8.7 %collective-permute-start.2 = (bf16[8,64,256]{2,1,0:T(8,128)(2,1)S(1)}, bf16[8,64,256]{2,1,0:T(8,128)(2,1)S(1)}, u32[]{:S(2)}, u32[]{:S(2)}) collective-permute-start(bf16[8,64,256]{2,1,0:T(8,128)(2,1)S(1)} %get-tuple-element.38.refs_0_), channel_id=1, source_target_pairs={{0,16},{8,24},{16,0},{24,8},{1,17},{9,25},{17,1},{25,9},{2,18},{10... | collective-permute-start | bytes 786440 | tf_op jit(solution)/shard_map/ppermute | solution.py:271
  20.2 9.7 %collective-permute-start.8 = (s16[2,272,256]{2,1,0:T(8,128)(2,1)S(1)}, s16[2,272,256]{2,1,0:T(8,128)(2,1)S(1)}, u32[]{:S(2)}, u32[]{:S(2)}) collective-permute-start(s16[2,272,256]{2,1,0:T(8,128)(2,1)S(1)} %get-tuple-element.42), channel_id=1, source_target_pairs={{0,1},{1,0},{2,3},{3,2},{4,5},{5,4},{6,7},{7,6},{8,9},{9,8},{10,11... | collective-permute-start | bytes 835592 | tf_op jit(solution)/shard_map/ppermute | solution.py:278
  25.2 1.5 %collective-permute-start.7 = (bf16[8,64,256]{2,1,0:T(8,128)(2,1)S(1)}, bf16[8,64,256]{2,1,0:T(8,128)(2,1)S(1)}, u32[]{:S(2)}, u32[]{:S(2)}) collective-permute-start(bf16[8,64,256]{2,1,0:T(8,128)(2,1)S(1)} %collective-permute-done.2.refs_0_), channel_id=1, source_target_pairs={{0,8},{8,0},{16,24},{24,16},{1,9},{9,1},{17,25},{25,17},{2,10},{10... | collective-permute-start | bytes 786440 | tf_op jit(solution)/shard_map/ppermute | solution.py:274
  30.4 10.3 %collective-permute-start.9 = (s16[2,272,256]{2,1,0:T(8,128)(2,1)S(1)}, s16[2,272,256]{2,1,0:T(8,128)(2,1)S(1)}, u32[]{:S(2)}, u32[]{:S(2)}) collective-permute-start(s16[2,272,256]{2,1,0:T(8,128)(2,1)S(1)} %get-tuple-element.46), channel_id=1, source_target_pairs={{0,2},{1,3},{2,0},{3,1},{4,6},{5,7},{6,4},{7,5},{8,10},{9,11},{10,... | collective-permute-start | bytes 835592 | tf_op jit(solution)/shard_map/ppermute | solution.py:281
  32.0 6.0 %collective-permute-start.14 = (s16[2,144,256]{2,1,0:T(8,128)(2,1)S(1)}, s16[2,144,256]{2,1,0:T(8,128)(2,1)S(1)}, u32[]{:S(2)}, u32[]{:S(2)}) collective-permute-start(s16[2,144,256]{2,1,0:T(8,128)(2,1)S(1)} %get-tuple-element.56), channel_id=1, source_target_pairs={{0,1},{1,0},{2,3},{3,2},{4,5},{5,4},{6,7},{7,6},{8,9},{9,8},{10,11... | collective-permute-start | bytes 442376 | tf_op jit(solution)/shard_map/ppermute | solution.py:278
  33.5 6.1 %collective-permute-start.11 = (s16[2,144,256]{2,1,0:T(8,128)(2,1)S(1)}, s16[2,144,256]{2,1,0:T(8,128)(2,1)S(1)}, u32[]{:S(2)}, u32[]{:S(2)}) collective-permute-start(s16[2,144,256]{2,1,0:T(8,128)(2,1)S(1)} %get-tuple-element.50), channel_id=1, source_target_pairs={{0,1},{1,0},{2,3},{3,2},{4,5},{5,4},{6,7},{7,6},{8,9},{9,8},{10,11... | collective-permute-start | bytes 442376 | tf_op jit(solution)/shard_map/ppermute | solution.py:278
  38.2 7.5 %collective-permute-start.15 = (s16[2,144,256]{2,1,0:T(8,128)(2,1)S(1)}, s16[2,144,256]{2,1,0:T(8,128)(2,1)S(1)}, u32[]{:S(2)}, u32[]{:S(2)}) collective-permute-start(s16[2,144,256]{2,1,0:T(8,128)(2,1)S(1)} %get-tuple-element.58), channel_id=1, source_target_pairs={{0,2},{1,3},{2,0},{3,1},{4,6},{5,7},{6,4},{7,5},{8,10},{9,11},{10,... | collective-permute-start | bytes 442376 | tf_op jit(solution)/shard_map/ppermute | solution.py:281
  39.8 9.1 %collective-permute-start.12 = (s16[2,144,256]{2,1,0:T(8,128)(2,1)S(1)}, s16[2,144,256]{2,1,0:T(8,128)(2,1)S(1)}, u32[]{:S(2)}, u32[]{:S(2)}) collective-permute-start(s16[2,144,256]{2,1,0:T(8,128)(2,1)S(1)} %get-tuple-element.52), channel_id=1, source_target_pairs={{0,2},{1,3},{2,0},{3,1},{4,6},{5,7},{6,4},{7,5},{8,10},{9,11},{10,... | collective-permute-start | bytes 442376 | tf_op jit(solution)/shard_map/ppermute | solution.py:281
  40.8 13.9 %collective-permute-start.10 = (s16[1,272,256]{2,1,0:T(8,128)(2,1)S(1)}, s16[1,272,256]{2,1,0:T(8,128)(2,1)S(1)}, u32[]{:S(2)}, u32[]{:S(2)}) collective-permute-start(s16[1,272,256]{2,1,0:T(8,128)(2,1)S(1)} %get-tuple-element.48), channel_id=1, source_target_pairs={{0,4},{1,5},{2,6},{3,7},{4,0},{5,1},{6,2},{7,3},{8,12},{9,13},{10,... | collective-permute-start | bytes 417800 | tf_op jit(solution)/shard_map/ppermute | solution.py:281
  45.8 8.0 %collective-permute-start.16 = (s16[1,144,256]{2,1,0:T(8,128)(2,1)S(1)}, s16[1,144,256]{2,1,0:T(8,128)(2,1)S(1)}, u32[]{:S(2)}, u32[]{:S(2)}) collective-permute-start(s16[1,144,256]{2,1,0:T(8,128)(2,1)S(1)} %get-tuple-element.60), channel_id=1, source_target_pairs={{0,4},{1,5},{2,6},{3,7},{4,0},{5,1},{6,2},{7,3},{8,12},{9,13},{10,... | collective-permute-start | bytes 221192 | tf_op jit(solution)/shard_map/ppermute | solution.py:281
  49.0 5.7 %collective-permute-start.13 = (s16[1,144,256]{2,1,0:T(8,128)(2,1)S(1)}, s16[1,144,256]{2,1,0:T(8,128)(2,1)S(1)}, u32[]{:S(2)}, u32[]{:S(2)}) collective-permute-start(s16[1,144,256]{2,1,0:T(8,128)(2,1)S(1)} %get-tuple-element.54), channel_id=1, source_target_pairs={{0,4},{1,5},{2,6},{3,7},{4,0},{5,1},{6,2},{7,3},{8,12},{9,13},{10,... | collective-permute-start | bytes 221192 | tf_op jit(solution)/shard_map/ppermute | solution.py:281

commit v4 on v3

v4 whole, which is shorter than its diff:
```python
import functools

import jax
import jax.numpy as jnp
from jax import lax
from jax.experimental import pallas as pl
from jax.experimental.pallas import tpu as pltpu
from jax.sharding import PartitionSpec as P

CD_COL = 8
PAIR_TILES_ROW = 8
LOADS = 8
HINT = 3 * 10**9
LANES = 128
LEVELS = 32000.0
STEPS = 64.0
SMALLEST = 2.0**-110
VMEM_LIMIT = 16 * 1024 * 1024

F32 = jnp.float32
BF16 = jnp.bfloat16
I16 = jnp.int16

IN_VMEM = pl.BlockSpec(memory_space=pltpu.VMEM)
IN_SMEM = pl.BlockSpec(memory_space=pltpu.SMEM)
IN_HBM = pl.BlockSpec(memory_space=pl.ANY)


def held(x):
    return pltpu.with_memory_space_constraint(x, pltpu.VMEM)


def after(x, *others):
    return lax.optimization_barrier((x, *others))[0]


def kernel_call(body, outs, ins, scratch=(), name=None, hint=0, outputs=IN_VMEM):
    return pl.pallas_call(
        body,
        out_shape=outs,
        in_specs=ins,
        out_specs=outputs if outputs is not IN_VMEM else jax.tree.map(lambda _: IN_VMEM, outs),
        scratch_shapes=list(scratch),
        compiler_params=pltpu.CompilerParams(vmem_limit_bytes=VMEM_LIMIT),
        cost_estimate=pl.CostEstimate(flops=1 + hint, bytes_accessed=1, transcendentals=0),
        name=name,
    )


def code(block):
    top = jnp.maximum(jnp.max(jnp.abs(block), axis=0, keepdims=True), SMALLEST)
    exponent = jnp.ceil(jnp.log2(top) * STEPS)
    scaled = block * (LEVELS * jnp.exp2(exponent * (-1.0 / STEPS)))
    return jnp.round(scaled).astype(jnp.int32).astype(I16), exponent


def store_exponents(ref, at, rows):
    tiles = len(rows)
    block = jnp.concatenate(list(rows) + [jnp.zeros_like(rows[0])] * (16 - tiles), axis=0)
    ref[at] = block.astype(jnp.int32).astype(I16)


def scales(exponents):
    return jnp.exp2(exponents.astype(jnp.int32).astype(F32) * (1.0 / STEPS)) * (1.0 / LEVELS)


def decode(block, scale):
    return block.astype(jnp.int32).astype(F32) * scale


def split_kernel(parts, amps_hbm, *refs):
    outs, (amps, flat, sem) = refs[:-3], refs[-3:]
    rows, tiles, width = amps.shape
    lanes = flat.shape[2]
    copy = pltpu.make_async_copy(amps_hbm, amps, sem)
    copy.start()
    copy.wait()
    for half in range(width // lanes):
        columns = pl.ds(half * lanes, lanes)
        flat[half] = amps[:, :, columns].astype(F32).reshape(rows * tiles, lanes)
    here = lax.rem(lax.axis_index("col"), parts)
    start = 0
    for out in outs:
        each = out.shape[2]
        for step in range(parts):
            part = lax.rem(here + step, parts)
            for tile in range(tiles):
                first = (part * (rows // parts) + start) * tiles + tile
                for half in range(width // lanes):
                    picked = flat[half, pl.ds(first, each, stride=tiles), :]
                    out[step, tile, :, pl.ds(half * lanes, lanes)] = picked.astype(BF16)
        start += each


def load_kernel(pieces, count_ref, cd_hbm, ab_hbm, ints_hbm, slots_ref, table_ref, cd, ab, sems):
    per = ints_hbm.shape[0] // pieces
    pairs = slots_ref.shape[0] // 2
    copies = [pltpu.make_async_copy(cd_hbm, cd, sems.at[0]), pltpu.make_async_copy(ab_hbm, ab, sems.at[1])]
    for piece in range(pieces):
        part = pl.ds(piece * per, per)
        copies.append(pltpu.make_async_copy(ints_hbm.at[part], table_ref.at[part], sems.at[2 + piece]))
    for copy in copies:
        copy.start()

    def clear(pair, carry):
        slots_ref[pair] = 0
        slots_ref[pairs + pair] = CD_COL
        return carry

    def note(slot, carry):
        pair = ab[slot] * CD_COL + cd[slot]
        slots_ref[pair] = slot
        slots_ref[pairs + pair] = cd[slot]
        return carry

    lax.fori_loop(0, pairs, clear, 0)
    copies[0].wait()
    copies[1].wait()
    lax.fori_loop(0, count_ref[0], note, 0)
    for copy in copies[2:]:
        copy.wait()


def multiply(left, slots_ref, table_ref, use):
    tiles, rows = left.shape[0] - 1, left.shape[1]
    pairs = slots_ref.shape[0] // 2
    left[tiles] = jnp.zeros(left.shape[1:], BF16)
    for ab in range(pairs // tiles):
        total = jnp.zeros((rows, table_ref.shape[2]), F32)
        for tile in range(tiles):
            pair = ab * tiles + tile
            total = total + jnp.dot(
                left[slots_ref[pairs + pair]], table_ref[slots_ref[pair]], preferred_element_type=F32
            )
        use(ab, total)


def product_kernel(blocks, x_first, *refs):
    amps_refs, (slots_ref, table_ref) = refs[:blocks], refs[blocks : blocks + 2]
    keep_ref, send_refs, left = refs[blocks + 2], refs[blocks + 3 : -1], refs[-1]
    parts, tiles, each, _ = amps_refs[0].shape
    kept = keep_ref.shape[0]
    if x_first:
        order = [(block, part) for part in range(parts) for block in range(blocks)]
        for tile in range(tiles):
            for at, (block, part) in enumerate(order):
                left[tile, at * each : (at + 1) * each] = amps_refs[block][part, tile]
    else:
        swapped = lax.rem(lax.axis_index("row") + lax.div(lax.axis_index("col"), parts), 2) == 1
        for tile in range(tiles):
            for pair in range(blocks // 2):
                for part in range(parts):
                    even, odd = amps_refs[2 * pair][part, tile], amps_refs[2 * pair + 1][part, tile]
                    at = pair * parts + part
                    left[tile, at * each : (at + 1) * each] = jnp.where(swapped, odd, even)
                    at += kept
                    left[tile, at * each : (at + 1) * each] = jnp.where(swapped, even, odd)
    sends = [ref.at[item] for ref in send_refs for item in range(ref.shape[0])]
    exponents = [[] for _ in sends]

    def use(ab, total):
        for at in range(kept):
            keep_ref[at, ab] = total[at * each : (at + 1) * each]
        for at, ref in enumerate(sends):
            first = (kept + at) * each
            coded, exponent = code(total[first : first + each])
            ref[ab * each : (ab + 1) * each] = coded
            exponents[at].append(exponent)

    multiply(left, slots_ref, table_ref, use)
    for ref, rows in zip(sends, exponents):
        store_exponents(ref, pl.ds(len(rows) * each, 16), rows)


def add_decoded(total, ref, ab, ab_tiles, factor):
    each = total.shape[0]
    return total + decode(ref[ab * each : (ab + 1) * each], factor[ab : ab + 1])


def tail_scales(ref, ab_tiles, each):
    return scales(ref[pl.ds(ab_tiles * each, 16)])


def code_into(ref, tiles):
    each = tiles[0].shape[0]
    exponents = []
    for ab, tile in enumerate(tiles):
        coded, exponent = code(tile)
        ref[ab * each : (ab + 1) * each] = coded
        exponents.append(exponent)
    store_exponents(ref, pl.ds(len(tiles) * each, 16), exponents)


def x_pair_kernel(n_x, n_z, *refs):
    refs, (kept_ref, sent_ref, sums) = refs[:-3], refs[-3:]
    half = len(refs) // 2
    ab_tiles, each = sums.shape[1:3]
    at = 0
    for keep_ref, *received in (refs[:half], refs[half:]):
        for item in range(keep_ref.shape[0]):
            factors = [tail_scales(ref.at[item], ab_tiles, each) for ref in received]
            for ab in range(ab_tiles):
                total = keep_ref[item, ab]
                for ref, factor in zip(received, factors):
                    total = add_decoded(total, ref.at[item], ab, ab_tiles, factor)
                sums[at, ab] = total
            at += 1
    put_in_order(False, n_x, n_z, sums, kept_ref, sent_ref)


def put_in_order(z_first, n_x, n_z, sums, kept_ref, sent_ref):
    ab_tiles = sums.shape[1]
    row, z, n_y = lax.axis_index("row"), lax.div(lax.axis_index("col"), n_x), n_z // 2
    places = []
    for m in range(sums.shape[0]):
        wanted = z ^ (2 * m if z_first else m)
        away = lax.rem(lax.div(row, 2) - lax.div(wanted, 2) + n_y, n_y)
        places.append(away if z_first else 2 * away + lax.rem(row + wanted, 2))
    for m in range(0, len(places), 2):
        kept_ref[m // 2] = sums[places[m]]
        code_into(sent_ref.at[m // 2], [sums[places[m + 1], ab] for ab in range(ab_tiles)])


def z_pair_kernel(parts, near_ref, near_received, far_ref, far_received, kept_ref, *send_refs):
    ab_tiles, each = kept_ref.shape[1:3]
    at = 0
    for keep_ref, received in ((near_ref, near_received), (far_ref, far_received)):
        for item in range(keep_ref.shape[0]):
            factor = tail_scales(received.at[item], ab_tiles, each)
            tiles = [add_decoded(keep_ref[item, ab], received.at[item], ab, ab_tiles, factor) for ab in range(ab_tiles)]
            part = item % parts
            if part:
                code_into(send_refs[part - 1].at[at], tiles)
            else:
                for ab in range(ab_tiles):
                    kept_ref[at, ab] = tiles[ab]
            at += part == parts - 1


def zx_pair_kernel(n_x, n_z, keep_ref, *refs):
    *received, kept_ref, sent_ref, sums = refs
    ab_tiles, each = sums.shape[1:3]
    for item in range(keep_ref.shape[0]):
        factors = [tail_scales(ref.at[item], ab_tiles, each) for ref in received]
        for ab in range(ab_tiles):
            total = keep_ref[item, ab]
            for ref, factor in zip(received, factors):
                total = add_decoded(total, ref.at[item], ab, ab_tiles, factor)
            sums[item, ab] = total
    put_in_order(True, n_x, n_z, sums, kept_ref, sent_ref)


def halve_kernel(kept_ref, received_ref, next_ref, sent_ref):
    count, ab_tiles, each, width = kept_ref.shape
    for item in range(count):
        factor = tail_scales(received_ref.at[item], ab_tiles, each)
        tiles = [
            add_decoded(kept_ref[item, ab], received_ref.at[item], ab, ab_tiles, factor) for ab in range(ab_tiles)
        ]
        if item % 2:
            code_into(sent_ref.at[item // 2], tiles)
        else:
            for ab in range(ab_tiles):
                next_ref[item // 2, ab] = tiles[ab]


def last_kernel(*refs):
    flat, out_ref = refs[-1], refs[-2]
    rows, ab_tiles, width = out_ref.shape
    lanes = flat.shape[2]
    start = 0
    for kept_ref, received_ref in zip(refs[:-2:2], refs[1:-2:2]):
        each = kept_ref.shape[2]
        factor = tail_scales(received_ref.at[0], ab_tiles, each)
        for ab in range(ab_tiles):
            total = add_decoded(kept_ref[0, ab], received_ref.at[0], ab, ab_tiles, factor)
            for half in range(width // lanes):
                piece = total[:, half * lanes : (half + 1) * lanes]
                flat[half, pl.ds(start * ab_tiles + ab, each, stride=ab_tiles), :] = piece
        start += each
    for half in range(width // lanes):
        whole = flat[half].reshape(rows, ab_tiles, lanes)
        out_ref[:, :, pl.ds(half * lanes, lanes)] = whole.astype(out_ref.dtype)


def shards(n_row, n_col, amps, ints, task_cd, task_ab, task_count):
    n_x = n_col // n_row
    n_z = n_row
    n_y = n_row // 2
    rows, tiles, width = amps.shape
    out_rows = rows // n_x
    sizes = [out_rows // 2] * 2
    pairs = PAIR_TILES_ROW * CD_COL
    other_parts = range(1, n_x)

    def along_y(array, step):
        return lax.ppermute(array, "row", [(r, (r + 2 * step) % n_row) for r in range(n_row)])

    def to_partner(array):
        return lax.ppermute(array, "row", [(r, r ^ 1) for r in range(n_row)])

    def along_x(array, step):
        pairs = [(c, c - c % n_x + (c % n_x + step) % n_x) for c in range(n_col)]
        return lax.ppermute(array, "col", pairs)

    def along_z(array, bit):
        return lax.ppermute(array, "col", [(c, (c // n_x ^ bit) * n_x + c % n_x) for c in range(n_col)])

    def coded(each, *lead):
        return pltpu.VMEM((*lead, PAIR_TILES_ROW * each + 16, width), I16)

    def summed(each, *lead):
        return pltpu.VMEM((*lead, PAIR_TILES_ROW, each, width), F32)

    hbm = functools.partial(pltpu.with_memory_space_constraint, memory_space=pltpu.HBM)

    def products(blocks, x_first):
        count, each = len(blocks), blocks[0].shape[2]
        if x_first:
            outs = [summed(each, count)] + [coded(each, count)] * (n_x - 1)
        else:
            outs = [summed(each, count * n_x // 2), coded(each, count * n_x // 2)]
        return kernel_call(
            functools.partial(product_kernel, count, x_first),
            outs,
            [IN_VMEM] * count + [IN_SMEM, IN_VMEM],
            [pltpu.VMEM((tiles + 1, count * n_x * each, width), BF16)],
            name="x_products" if x_first else "z_products",
        )(*map(held, blocks), slots, held(table))

    mine = kernel_call(
        functools.partial(split_kernel, n_x),
        [pltpu.VMEM((n_x, tiles, each, width), BF16) for each in sizes],
        [IN_HBM],
        [
            pltpu.VMEM(amps.shape, BF16),
            pltpu.VMEM((width // LANES, rows * tiles, LANES), F32),
            pltpu.SemaphoreType.DMA,
        ],
        name="split",
    )(hbm(amps))
    far = [[along_y(chunk, k) for k in range(1, n_y)] for chunk in mine]
    beside = [to_partner(chunk) for chunk in mine]
    slots, table = kernel_call(
        functools.partial(load_kernel, LOADS),
        [pltpu.SMEM((2 * pairs,), jnp.int32), pltpu.VMEM(ints.shape, BF16)],
        [IN_SMEM] + [IN_HBM] * 3,
        [
            pltpu.SMEM(task_cd.shape, jnp.int32),
            pltpu.SMEM(task_ab.shape, jnp.int32),
            pltpu.SemaphoreType.DMA((2 + LOADS,)),
        ],
        outputs=[IN_SMEM, IN_VMEM],
        name="load",
    )(task_count, hbm(task_cd), hbm(task_ab), hbm(ints))

    def over_x(sends):
        return [along_x(send, step) for step, send in zip(range(1, n_x), sends)]

    def fetch(arrays, *ties):
        blocks = []
        for array in arrays:
            array = after(array, *ties)
            blocks += [array, to_partner(array)]
        return blocks

    def reduce_z(kept, sent, bit):
        each, count = kept.shape[2], kept.shape[0]
        received = along_z(sent, bit)
        while count > 1:
            count, bit = count // 2, bit * 2
            kept, sent = kernel_call(
                halve_kernel, [summed(each, count), coded(each, count)], [IN_VMEM] * 2, name="halve"
            )(held(kept), held(received))
            received = along_z(sent, bit)
        return [kept, received]

    near_keep, *sends = products([mine[0], beside[0]], True)
    near_received = over_x(sends)
    near_zkeep, send = products([after(mine[1], near_keep), beside[1]], False)
    near_zreceived = along_z(send, 1)
    far_blocks = fetch(far[0], near_zkeep)
    far_keep, *sends = products(far_blocks, True)
    far_received = over_x(sends)
    far_zblocks = fetch(far[1], far_keep)
    far_zkeep, send = products([after(v, near_received[-1], near_zreceived) for v in far_zblocks], False)
    far_zreceived = along_z(send, 1)

    first, second = sizes
    kept, sent = kernel_call(
        functools.partial(x_pair_kernel, n_x, n_z),
        [summed(first, n_z // 2), coded(first, n_z // 2)],
        [IN_VMEM] * (2 * n_x),
        [summed(first, n_z)],
        name="x_pairs",
        hint=HINT,
    )(*map(held, [near_keep, *near_received, far_keep, *far_received]))
    last = reduce_z(kept, sent, 1)
    kept, *sends = kernel_call(
        functools.partial(z_pair_kernel, n_x),
        [summed(second, n_y)] + [coded(second, n_y)] * (n_x - 1),
        [IN_VMEM] * 4,
        name="z_pairs",
    )(*map(held, [near_zkeep, near_zreceived, far_zkeep, far_zreceived]))
    kept, sent = kernel_call(
        functools.partial(zx_pair_kernel, n_x, n_z),
        [summed(second, n_y // 2), coded(second, n_y // 2)],
        [IN_VMEM] * n_x,
        [summed(second, n_y)],
        name="zx_pairs",
    )(*map(held, [kept, *over_x(sends)]))
    last += reduce_z(kept, sent, 2)
    return kernel_call(
        last_kernel,
        jax.ShapeDtypeStruct((out_rows, PAIR_TILES_ROW, width), BF16),
        [IN_VMEM] * len(last),
        [pltpu.VMEM((width // LANES, out_rows * PAIR_TILES_ROW, LANES), F32)],
        name="last",
    )(*map(held, last))


def solution(mesh):
    return jax.shard_map(
        functools.partial(shards, mesh.shape["row"], mesh.shape["col"]),
        mesh=mesh,
        in_specs=(
            P("row", "col", None),
            P(("row", "col"), None, None),
            P(("row", "col")),
            P(("row", "col")),
            P(("row", "col")),
        ),
        out_specs=P("col", "row", None),
        check_vma=False,
    )
```

time: 55.7 us -> 53.3 us (0.957)
  starting transfers between devices: 20.4 us -> 18.4 us
  waiting for transfers between devices: 23.4 us -> 21.9 us
  Pallas kernels: 11.1 us -> 12.1 us
    ppermute x6 -> x5, waiting for transfers between devices: 7.23 us -> 15.6 us  [along_z(): lax.ppermute(array, 'col', [(c, (c // n_x ^ bit) * n_x + c % n_x) for c i...]
    ppermute x5 -> x3, waiting for transfers between devices: 11.5 us -> 3.95 us  [along_x(): return lax.ppermute(array, 'col', pairs)]
    ppermute x5 -> x3, starting transfers between devices: 5.67 us -> 3.35 us  [along_x(): return lax.ppermute(array, 'col', pairs)]
    ppermute x4, waiting for transfers between devices: 1.54 us -> 0.01 us  [to_partner(): return lax.ppermute(array, 'row', [(r, r ^ 1) for r in range(n_row)])]
    pallas_call x11 -> x10, Pallas kernels: 10.2 us -> 11.2 us  [the longest x4 5.25 us: products(): kernel_call(functools.partial(product_kernel, count, x_first), outs, [IN_...]
    ppermute x2, waiting for transfers between devices: 3.17 us -> 2.35 us  [along_y(): lax.ppermute(array, 'row', [(r, (r + 2 * step) % n_row) for r in range(n_...]
    ppermute x6 -> x5, starting transfers between devices: 9.42 us -> 10 us  [along_z(): lax.ppermute(array, 'col', [(c, (c // n_x ^ bit) * n_x + c % n_x) for c i...]
  transfers between devices with their start and end apart: 17 -> 14, of which waited for: 12 -> 8; matrix products, arithmetic and copies ran while one was open for 0% -> 0% of each run, Pallas kernels for 11% -> 19%
where the time goes in v4:
time: 53.3 us; the launch traced here: 53.1 us
  waiting for transfers between devices  21.9 us (41%)
  starting transfers between devices  18.4 us (35%)
  Pallas kernels  12.1 us (23%)
  between operations  0.75 us (1%)
    ppermute x5, waiting for transfers between devices, along_z(): lax.ppermute(array, 'col', [(c, (c // n_x ^ bit) * n_x + c % n_x) for c i...  15.6 us
    ppermute x5, starting transfers between devices, along_z(): lax.ppermute(array, 'col', [(c, (c // n_x ^ bit) * n_x + c % n_x) for c i...  10 us
    pallas_call x4, Pallas kernels, products(): kernel_call(functools.partial(product_kernel, count, x_first), outs, [IN_...  5.25 us
    ppermute x2, starting transfers between devices, along_y(): lax.ppermute(array, 'row', [(r, (r + 2 * step) % n_row) for r in range(n_...  4.33 us
    ppermute x3, waiting for transfers between devices, along_x(): return lax.ppermute(array, 'col', pairs)  3.95 us
    pallas_call x1, Pallas kernels, shards(): kernel_call(functools.partial(load_kernel, LOADS), [pltpu.SMEM((2 * pairs...  3.5 us
    ppermute x3, starting transfers between devices, along_x(): return lax.ppermute(array, 'col', pairs)  3.35 us
    ppermute x2, waiting for transfers between devices, along_y(): lax.ppermute(array, 'row', [(r, (r + 2 * step) % n_row) for r in range(n_...  2.35 us
  transfers between devices with their start and end apart: 14, of which 8 were waited for; matrix products, arithmetic and copies ran while one was open for 0% of the time, Pallas kernels for 19%

profile of v4, /device:TPU:0, one launch (start us, length us, event | category | flops | bytes accessed | tf_op | source)
XLA Modules:
  0.0 53.1 jit_solution(976708059222517582)
XLA Ops:
  0.0 1.3 %split.1 = (bf16[2,8,32,256]{3,2,1,0:T(8,128)(2,1)S(1)}, bf16[2,8,32,256]{3,2,1,0:T(8,128)(2,1)S(1)}) custom-call(bf16[128,8,256]{2,1,0:T(8,128)(2,1)} %amps_hbm.1), custom_call_target="tpu_custom_call" | custom-call | flops 1 | bytes 1 | tf_op jit(solution)/shard_map/split/pallas_call | solution.py:331
  1.3 0.5 collective-permute-start
  1.9 0.1 collective-permute-start.3
  1.9 2.9 %collective-permute-start.2 = (bf16[2,8,32,256]{3,2,1,0:T(8,128)(2,1)S(1)}, bf16[2,8,32,256]{3,2,1,0:T(8,128)(2,1)S(1)}, u32[]{:S(2)}, u32[]{:S(2)}) collective-permute-start(bf16[2,8,32,256]{3,2,1,0:T(8,128)(2,1)S(1)} %get-tuple-element.30.refs_0_), channel_id=1, source_target_pairs={{0,16},{8,24},{16,0},{24,8},{1,17},{9,25},{17,1},{25,9},{2,18},{10... | collective-permute-start | bytes 786440 | tf_op jit(solution)/shard_map/ppermute | solution.py:297
  5.5 3.5 %load.1 = (s32[128]{0:T(128)S(4)}, bf16[64,256,256]{2,1,0:T(8,128)(2,1)S(1)}) custom-call(s32[1]{0:T(128)S(6)} %copy.6.count_ref, s32[64]{0:T(128)} %cd_hbm.1, s32[64]{0:T(128)} %ab_hbm.1, bf16[64,256,256]{2,1,0:T(8,128)(2,1)} %ints_hbm.1), custom_call_target="tpu_custom_call" | custom-call | flops 1 | bytes 1 | tf_op jit(solution)/shard_map/load/pallas_call | solution.py:344
  9.0 0.0 collective-permute-done.refs_1_
  9.0 1.3 %x_products.2 = (f32[2,8,32,256]{3,2,1,0:T(8,128)S(1)}, s16[2,272,256]{2,1,0:T(8,128)(2,1)S(1)}) custom-call(bf16[2,8,32,256]{3,2,1,0:T(8,128)(2,1)S(1)} %get-tuple-element.30.refs_0_, bf16[2,8,32,256]{3,2,1,0:T(8,128)(2,1)S(1)} %collective-permute-done.refs_1_, s32[128]{0:T(128)S(4)} %get-tuple-element.31.refs_2_, ...), custom_call_target="tpu_custom_call" | custom-call | flops 1 | bytes 1 | tf_op jit(solution)/shard_map/x_products/pallas_call | solution.py:323
  10.4 0.0 collective-permute-done.3.refs_1_
  10.4 1.3 %z_products.2 = (f32[2,8,32,256]{3,2,1,0:T(8,128)S(1)}, s16[2,272,256]{2,1,0:T(8,128)(2,1)S(1)}) custom-call(bf16[2,8,32,256]{3,2,1,0:T(8,128)(2,1)S(1)} %get-tuple-element.36.refs_0_, bf16[2,8,32,256]{3,2,1,0:T(8,128)(2,1)S(1)} %collective-permute-done.3.refs_1_, s32[128]{0:T(128)S(4)} %get-tuple-element.31.refs_2_, ...), custom_call_target="tpu_custom_call" | custom-call | flops 1 | bytes 1 | tf_op jit(solution)/shard_map/z_products/pallas_call | solution.py:323
  11.7 0.0 collective-permute-done.2.refs_0_
  11.7 0.1 collective-permute-start.4
  11.8 1.4 %collective-permute-start.9 = (bf16[2,8,32,256]{3,2,1,0:T(8,128)(2,1)S(1)}, bf16[2,8,32,256]{3,2,1,0:T(8,128)(2,1)S(1)}, u32[]{:S(2)}, u32[]{:S(2)}) collective-permute-start(bf16[2,8,32,256]{3,2,1,0:T(8,128)(2,1)S(1)} %get-tuple-element.36.refs_0_), channel_id=1, source_target_pairs={{0,16},{8,24},{16,0},{24,8},{1,17},{9,25},{17,1},{25,9},{2,18},{10... | collective-permute-start | bytes 786440 | tf_op jit(solution)/shard_map/ppermute | solution.py:297
  13.2 1.5 %collective-permute-start.1 = (s16[2,272,256]{2,1,0:T(8,128)(2,1)S(1)}, s16[2,272,256]{2,1,0:T(8,128)(2,1)S(1)}, u32[]{:S(2)}, u32[]{:S(2)}) collective-permute-start(s16[2,272,256]{2,1,0:T(8,128)(2,1)S(1)} %get-tuple-element.34), channel_id=1, source_target_pairs={{0,1},{1,0},{2,3},{3,2},{4,5},{5,4},{6,7},{7,6},{8,9},{9,8},{10,11... | collective-permute-start | bytes 835592 | tf_op jit(solution)/shard_map/ppermute | solution.py:304
  14.7 1.6 %collective-permute-start.8 = (s16[2,272,256]{2,1,0:T(8,128)(2,1)S(1)}, s16[2,272,256]{2,1,0:T(8,128)(2,1)S(1)}, u32[]{:S(2)}, u32[]{:S(2)}) collective-permute-start(s16[2,272,256]{2,1,0:T(8,128)(2,1)S(1)} %get-tuple-element.45), channel_id=1, source_target_pairs={{0,2},{1,3},{2,0},{3,1},{4,6},{5,7},{6,4},{7,5},{8,10},{9,11},{10,... | collective-permute-start | bytes 835592 | tf_op jit(solution)/shard_map/ppermute | solution.py:307
  16.2 0.0 collective-permute-done.4.refs_1_
  16.2 1.3 %x_products.3 = (f32[2,8,32,256]{3,2,1,0:T(8,128)S(1)}, s16[2,272,256]{2,1,0:T(8,128)(2,1)S(1)}) custom-call(bf16[2,8,32,256]{3,2,1,0:T(8,128)(2,1)S(1)} %collective-permute-done.2.refs_0_, bf16[2,8,32,256]{3,2,1,0:T(8,128)(2,1)S(1)} %collective-permute-done.4.refs_1_, s32[128]{0:T(128)S(4)} %get-tuple-element.31.refs_2_, ...), custom_call_target="tpu_custom_call" | custom-call | flops 1 | bytes 1 | tf_op jit(solution)/shard_map/x_products/pallas_call | solution.py:323
  17.6 0.6 %collective-permute-start.5 = (s16[2,272,256]{2,1,0:T(8,128)(2,1)S(1)}, s16[2,272,256]{2,1,0:T(8,128)(2,1)S(1)}, u32[]{:S(2)}, u32[]{:S(2)}) collective-permute-start(s16[2,272,256]{2,1,0:T(8,128)(2,1)S(1)} %get-tuple-element.40), channel_id=1, source_target_pairs={{0,1},{1,0},{2,3},{3,2},{4,5},{5,4},{6,7},{7,6},{8,9},{9,8},{10,11... | collective-permute-start | bytes 835592 | tf_op jit(solution)/shard_map/ppermute | solution.py:304
  18.2 2.3 %collective-permute-done.9.refs_0_ = bf16[2,8,32,256]{3,2,1,0:T(8,128)(2,1)S(1)} collective-permute-done((bf16[2,8,32,256]{3,2,1,0:T(8,128)(2,1)S(1)}, bf16[2,8,32,256]{3,2,1,0:T(8,128)(2,1)S(1)}, u32[]{:S(2)}, u32[]{:S(2)}) %collective-permute-start.9) | collective-permute-done | bytes 262176 | tf_op jit(solution)/shard_map/ppermute | solution.py:297
  20.5 0.0 collective-permute-start.10
  20.5 2.2 %collective-permute-done.1.refs_1_ = s16[2,272,256]{2,1,0:T(8,128)(2,1)S(1)} collective-permute-done((s16[2,272,256]{2,1,0:T(8,128)(2,1)S(1)}, s16[2,272,256]{2,1,0:T(8,128)(2,1)S(1)}, u32[]{:S(2)}, u32[]{:S(2)}) %collective-permute-start.1) | collective-permute-done | bytes 278560 | tf_op jit(solution)/shard_map/ppermute | solution.py:304
  22.7 0.5 collective-permute-done.8.near_received
  23.2 0.0 collective-permute-done.10.refs_1_
  23.2 1.3 %z_products.3 = (f32[2,8,32,256]{3,2,1,0:T(8,128)S(1)}, s16[2,272,256]{2,1,0:T(8,128)(2,1)S(1)}) custom-call(bf16[2,8,32,256]{3,2,1,0:T(8,128)(2,1)S(1)} %collective-permute-done.9.refs_0_, bf16[2,8,32,256]{3,2,1,0:T(8,128)(2,1)S(1)} %collective-permute-done.10.refs_1_, s32[128]{0:T(128)S(4)} %get-tuple-element.31.refs_2_, ...), custom_call_target="tpu_custom_call" | custom-call | flops 1 | bytes 1 | tf_op jit(solution)/shard_map/z_products/pallas_call | solution.py:323
  24.5 1.6 %collective-permute-start.11 = (s16[2,272,256]{2,1,0:T(8,128)(2,1)S(1)}, s16[2,272,256]{2,1,0:T(8,128)(2,1)S(1)}, u32[]{:S(2)}, u32[]{:S(2)}) collective-permute-start(s16[2,272,256]{2,1,0:T(8,128)(2,1)S(1)} %get-tuple-element.50), channel_id=1, source_target_pairs={{0,2},{1,3},{2,0},{3,1},{4,6},{5,7},{6,4},{7,5},{8,10},{9,11},{10,... | collective-permute-start | bytes 835592 | tf_op jit(solution)/shard_map/ppermute | solution.py:307
  26.1 1.8 %collective-permute-done.5.refs_3_ = s16[2,272,256]{2,1,0:T(8,128)(2,1)S(1)} collective-permute-done((s16[2,272,256]{2,1,0:T(8,128)(2,1)S(1)}, s16[2,272,256]{2,1,0:T(8,128)(2,1)S(1)}, u32[]{:S(2)}, u32[]{:S(2)}) %collective-permute-start.5) | collective-permute-done | bytes 278560 | tf_op jit(solution)/shard_map/ppermute | solution.py:304
  27.9 0.4 x_pairs.1
  28.3 1.6 %collective-permute-start.6 = (s16[2,272,256]{2,1,0:T(8,128)(2,1)S(1)}, s16[2,272,256]{2,1,0:T(8,128)(2,1)S(1)}, u32[]{:S(2)}, u32[]{:S(2)}) collective-permute-start(s16[2,272,256]{2,1,0:T(8,128)(2,1)S(1)} %get-tuple-element.42), channel_id=1, source_target_pairs={{0,2},{1,3},{2,0},{3,1},{4,6},{5,7},{6,4},{7,5},{8,10},{9,11},{10,... | collective-permute-start | bytes 835592 | tf_op jit(solution)/shard_map/ppermute | solution.py:307
  30.0 4.0 %collective-permute-done.11.far_received = s16[2,272,256]{2,1,0:T(8,128)(2,1)S(1)} collective-permute-done((s16[2,272,256]{2,1,0:T(8,128)(2,1)S(1)}, s16[2,272,256]{2,1,0:T(8,128)(2,1)S(1)}, u32[]{:S(2)}, u32[]{:S(2)}) %collective-permute-start.11) | collective-permute-done | bytes 278560 | tf_op jit(solution)/shard_map/ppermute | solution.py:307
  33.9 0.3 z_pairs.1
  34.2 1.3 %collective-permute-start.12 = (s16[2,272,256]{2,1,0:T(8,128)(2,1)S(1)}, s16[2,272,256]{2,1,0:T(8,128)(2,1)S(1)}, u32[]{:S(2)}, u32[]{:S(2)}) collective-permute-start(s16[2,272,256]{2,1,0:T(8,128)(2,1)S(1)} %get-tuple-element.52), channel_id=1, source_target_pairs={{0,1},{1,0},{2,3},{3,2},{4,5},{5,4},{6,7},{7,6},{8,9},{9,8},{10,11... | collective-permute-start | bytes 835592 | tf_op jit(solution)/shard_map/ppermute | solution.py:304
  35.5 2.7 %collective-permute-done.6.received_ref = s16[2,272,256]{2,1,0:T(8,128)(2,1)S(1)} collective-permute-done((s16[2,272,256]{2,1,0:T(8,128)(2,1)S(1)}, s16[2,272,256]{2,1,0:T(8,128)(2,1)S(1)}, u32[]{:S(2)}, u32[]{:S(2)}) %collective-permute-start.6) | collective-permute-done | bytes 278560 | tf_op jit(solution)/shard_map/ppermute | solution.py:307
  38.2 0.2 halve.1
  38.3 2.7 %collective-permute-start.7 = (s16[1,272,256]{2,1,0:T(8,128)(2,1)S(1)}, s16[1,272,256]{2,1,0:T(8,128)(2,1)S(1)}, u32[]{:S(2)}, u32[]{:S(2)}) collective-permute-start(s16[1,272,256]{2,1,0:T(8,128)(2,1)S(1)} %get-tuple-element.44), channel_id=1, source_target_pairs={{0,4},{1,5},{2,6},{3,7},{4,0},{5,1},{6,2},{7,3},{8,12},{9,13},{10,... | collective-permute-start | bytes 417800 | tf_op jit(solution)/shard_map/ppermute | solution.py:307
  41.0 0.0 collective-permute-done.12.refs_0_
  41.0 0.3 zx_pairs.1
  41.3 2.5 %collective-permute-start.13 = (s16[1,272,256]{2,1,0:T(8,128)(2,1)S(1)}, s16[1,272,256]{2,1,0:T(8,128)(2,1)S(1)}, u32[]{:S(2)}, u32[]{:S(2)}) collective-permute-start(s16[1,272,256]{2,1,0:T(8,128)(2,1)S(1)} %get-tuple-element.54), channel_id=1, source_target_pairs={{0,4},{1,5},{2,6},{3,7},{4,0},{5,1},{6,2},{7,3},{8,12},{9,13},{10,... | collective-permute-start | bytes 417800 | tf_op jit(solution)/shard_map/ppermute | solution.py:307
  43.8 6.6 %collective-permute-done.7.refs_1_ = s16[1,272,256]{2,1,0:T(8,128)(2,1)S(1)} collective-permute-done((s16[1,272,256]{2,1,0:T(8,128)(2,1)S(1)}, s16[1,272,256]{2,1,0:T(8,128)(2,1)S(1)}, u32[]{:S(2)}, u32[]{:S(2)}) %collective-permute-start.7) | collective-permute-done | bytes 139296 | tf_op jit(solution)/shard_map/ppermute | solution.py:307
  50.4 1.8 %collective-permute-done.13.refs_3_ = s16[1,272,256]{2,1,0:T(8,128)(2,1)S(1)} collective-permute-done((s16[1,272,256]{2,1,0:T(8,128)(2,1)S(1)}, s16[1,272,256]{2,1,0:T(8,128)(2,1)S(1)}, u32[]{:S(2)}, u32[]{:S(2)}) %collective-permute-start.13) | collective-permute-done | bytes 139296 | tf_op jit(solution)/shard_map/ppermute | solution.py:307
  52.2 0.9 %last.1 = bf16[64,8,256]{2,1,0:T(8,128)(2,1)} custom-call(f32[1,8,32,256]{3,2,1,0:T(8,128)S(1)} %get-tuple-element.43.refs_0_, s16[1,272,256]{2,1,0:T(8,128)(2,1)S(1)} %collective-permute-done.7.refs_1_, f32[1,8,32,256]{3,2,1,0:T(8,128)S(1)} %get-tuple-element.53.refs_2_, s16[1,272,256]{2,1,0:T(8,128)(2,1)S(1)} %collective-permute-done.13.refs_3_), custom_call_target="tpu_custom_call" | custom-call | flops 1 | bytes 1 | tf_op jit(solution)/shard_map/last/pallas_call | solution.py:413
Async XLA Ops:
  1.3 7.7 %collective-permute-start = (bf16[2,8,32,256]{3,2,1,0:T(8,128)(2,1)S(1)}, bf16[2,8,32,256]{3,2,1,0:T(8,128)(2,1)S(1)}, u32[]{:S(2)}, u32[]{:S(2)}) collective-permute-start(bf16[2,8,32,256]{3,2,1,0:T(8,128)(2,1)S(1)} %get-tuple-element.30.refs_0_), channel_id=1, source_target_pairs={{0,8},{8,0},{16,24},{24,16},{1,9},{9,1},{17,25},{25,17},{2,10},{10... | collective-permute-start | bytes 786440 | tf_op jit(solution)/shard_map/ppermute | solution.py:300
  1.9 8.5 %collective-permute-start.3 = (bf16[2,8,32,256]{3,2,1,0:T(8,128)(2,1)S(1)}, bf16[2,8,32,256]{3,2,1,0:T(8,128)(2,1)S(1)}, u32[]{:S(2)}, u32[]{:S(2)}) collective-permute-start(bf16[2,8,32,256]{3,2,1,0:T(8,128)(2,1)S(1)} %get-tuple-element.36.refs_0_), channel_id=1, source_target_pairs={{0,8},{8,0},{16,24},{24,16},{1,9},{9,1},{17,25},{25,17},{2,10},{10... | collective-permute-start | bytes 786440 | tf_op jit(solution)/shard_map/ppermute | solution.py:300
  1.9 9.8 %collective-permute-start.2 = (bf16[2,8,32,256]{3,2,1,0:T(8,128)(2,1)S(1)}, bf16[2,8,32,256]{3,2,1,0:T(8,128)(2,1)S(1)}, u32[]{:S(2)}, u32[]{:S(2)}) collective-permute-start(bf16[2,8,32,256]{3,2,1,0:T(8,128)(2,1)S(1)} %get-tuple-element.30.refs_0_), channel_id=1, source_target_pairs={{0,16},{8,24},{16,0},{24,8},{1,17},{9,25},{17,1},{25,9},{2,18},{10... | collective-permute-start | bytes 786440 | tf_op jit(solution)/shard_map/ppermute | solution.py:297
  11.7 4.5 %collective-permute-start.4 = (bf16[2,8,32,256]{3,2,1,0:T(8,128)(2,1)S(1)}, bf16[2,8,32,256]{3,2,1,0:T(8,128)(2,1)S(1)}, u32[]{:S(2)}, u32[]{:S(2)}) collective-permute-start(bf16[2,8,32,256]{3,2,1,0:T(8,128)(2,1)S(1)} %collective-permute-done.2.refs_0_), channel_id=1, source_target_pairs={{0,8},{8,0},{16,24},{24,16},{1,9},{9,1},{17,25},{25,17},{2,10},{10... | collective-permute-start | bytes 786440 | tf_op jit(solution)/shard_map/ppermute | solution.py:300
  11.8 8.7 %collective-permute-start.9 = (bf16[2,8,32,256]{3,2,1,0:T(8,128)(2,1)S(1)}, bf16[2,8,32,256]{3,2,1,0:T(8,128)(2,1)S(1)}, u32[]{:S(2)}, u32[]{:S(2)}) collective-permute-start(bf16[2,8,32,256]{3,2,1,0:T(8,128)(2,1)S(1)} %get-tuple-element.36.refs_0_), channel_id=1, source_target_pairs={{0,16},{8,24},{16,0},{24,8},{1,17},{9,25},{17,1},{25,9},{2,18},{10... | collective-permute-start | bytes 786440 | tf_op jit(solution)/shard_map/ppermute | solution.py:297
  13.2 9.5 %collective-permute-start.1 = (s16[2,272,256]{2,1,0:T(8,128)(2,1)S(1)}, s16[2,272,256]{2,1,0:T(8,128)(2,1)S(1)}, u32[]{:S(2)}, u32[]{:S(2)}) collective-permute-start(s16[2,272,256]{2,1,0:T(8,128)(2,1)S(1)} %get-tuple-element.34), channel_id=1, source_target_pairs={{0,1},{1,0},{2,3},{3,2},{4,5},{5,4},{6,7},{7,6},{8,9},{9,8},{10,11... | collective-permute-start | bytes 835592 | tf_op jit(solution)/shard_map/ppermute | solution.py:304
  14.7 8.5 %collective-permute-start.8 = (s16[2,272,256]{2,1,0:T(8,128)(2,1)S(1)}, s16[2,272,256]{2,1,0:T(8,128)(2,1)S(1)}, u32[]{:S(2)}, u32[]{:S(2)}) collective-permute-start(s16[2,272,256]{2,1,0:T(8,128)(2,1)S(1)} %get-tuple-element.45), channel_id=1, source_target_pairs={{0,2},{1,3},{2,0},{3,1},{4,6},{5,7},{6,4},{7,5},{8,10},{9,11},{10,... | collective-permute-start | bytes 835592 | tf_op jit(solution)/shard_map/ppermute | solution.py:307
  17.6 10.4 %collective-permute-start.5 = (s16[2,272,256]{2,1,0:T(8,128)(2,1)S(1)}, s16[2,272,256]{2,1,0:T(8,128)(2,1)S(1)}, u32[]{:S(2)}, u32[]{:S(2)}) collective-permute-start(s16[2,272,256]{2,1,0:T(8,128)(2,1)S(1)} %get-tuple-element.40), channel_id=1, source_target_pairs={{0,1},{1,0},{2,3},{3,2},{4,5},{5,4},{6,7},{7,6},{8,9},{9,8},{10,11... | collective-permute-start | bytes 835592 | tf_op jit(solution)/shard_map/ppermute | solution.py:304
  20.5 2.7 %collective-permute-start.10 = (bf16[2,8,32,256]{3,2,1,0:T(8,128)(2,1)S(1)}, bf16[2,8,32,256]{3,2,1,0:T(8,128)(2,1)S(1)}, u32[]{:S(2)}, u32[]{:S(2)}) collective-permute-start(bf16[2,8,32,256]{3,2,1,0:T(8,128)(2,1)S(1)} %collective-permute-done.9.refs_0_), channel_id=1, source_target_pairs={{0,8},{8,0},{16,24},{24,16},{1,9},{9,1},{17,25},{25,17},{2,10},{10... | collective-permute-start | bytes 786440 | tf_op jit(solution)/shard_map/ppermute | solution.py:300
  24.5 9.5 %collective-permute-start.11 = (s16[2,272,256]{2,1,0:T(8,128)(2,1)S(1)}, s16[2,272,256]{2,1,0:T(8,128)(2,1)S(1)}, u32[]{:S(2)}, u32[]{:S(2)}) collective-permute-start(s16[2,272,256]{2,1,0:T(8,128)(2,1)S(1)} %get-tuple-element.50), channel_id=1, source_target_pairs={{0,2},{1,3},{2,0},{3,1},{4,6},{5,7},{6,4},{7,5},{8,10},{9,11},{10,... | collective-permute-start | bytes 835592 | tf_op jit(solution)/shard_map/ppermute | solution.py:307
  28.3 9.8 %collective-permute-start.6 = (s16[2,272,256]{2,1,0:T(8,128)(2,1)S(1)}, s16[2,272,256]{2,1,0:T(8,128)(2,1)S(1)}, u32[]{:S(2)}, u32[]{:S(2)}) collective-permute-start(s16[2,272,256]{2,1,0:T(8,128)(2,1)S(1)} %get-tuple-element.42), channel_id=1, source_target_pairs={{0,2},{1,3},{2,0},{3,1},{4,6},{5,7},{6,4},{7,5},{8,10},{9,11},{10,... | collective-permute-start | bytes 835592 | tf_op jit(solution)/shard_map/ppermute | solution.py:307
  34.2 6.8 %collective-permute-start.12 = (s16[2,272,256]{2,1,0:T(8,128)(2,1)S(1)}, s16[2,272,256]{2,1,0:T(8,128)(2,1)S(1)}, u32[]{:S(2)}, u32[]{:S(2)}) collective-permute-start(s16[2,272,256]{2,1,0:T(8,128)(2,1)S(1)} %get-tuple-element.52), channel_id=1, source_target_pairs={{0,1},{1,0},{2,3},{3,2},{4,5},{5,4},{6,7},{7,6},{8,9},{9,8},{10,11... | collective-permute-start | bytes 835592 | tf_op jit(solution)/shard_map/ppermute | solution.py:304
  38.3 12.1 %collective-permute-start.7 = (s16[1,272,256]{2,1,0:T(8,128)(2,1)S(1)}, s16[1,272,256]{2,1,0:T(8,128)(2,1)S(1)}, u32[]{:S(2)}, u32[]{:S(2)}) collective-permute-start(s16[1,272,256]{2,1,0:T(8,128)(2,1)S(1)} %get-tuple-element.44), channel_id=1, source_target_pairs={{0,4},{1,5},{2,6},{3,7},{4,0},{5,1},{6,2},{7,3},{8,12},{9,13},{10,... | collective-permute-start | bytes 417800 | tf_op jit(solution)/shard_map/ppermute | solution.py:307
  41.3 11.0 %collective-permute-start.13 = (s16[1,272,256]{2,1,0:T(8,128)(2,1)S(1)}, s16[1,272,256]{2,1,0:T(8,128)(2,1)S(1)}, u32[]{:S(2)}, u32[]{:S(2)}) collective-permute-start(s16[1,272,256]{2,1,0:T(8,128)(2,1)S(1)} %get-tuple-element.54), channel_id=1, source_target_pairs={{0,4},{1,5},{2,6},{3,7},{4,0},{5,1},{6,2},{7,3},{8,12},{9,13},{10,... | collective-permute-start | bytes 417800 | tf_op jit(solution)/shard_map/ppermute | solution.py:307

commit v5 on v4

--- a/solution.py
+++ b/solution.py
@@ -54,10 +54,10 @@
     return jnp.round(scaled).astype(jnp.int32).astype(I16), exponent
 
 
-def store_exponents(ref, at, rows):
-    tiles = len(rows)
-    block = jnp.concatenate(list(rows) + [jnp.zeros_like(rows[0])] * (16 - tiles), axis=0)
-    ref[at] = block.astype(jnp.int32).astype(I16)
+def store_exponents(ref, rows):
+    pad = -len(rows) % 16
+    block = jnp.concatenate(list(rows) + [jnp.zeros_like(rows[0])] * pad, axis=0)
+    ref[ref.shape[0] - len(rows) - pad :] = block.astype(jnp.int32).astype(I16)
 
 
 def scales(exponents):
@@ -155,40 +155,43 @@
                     left[tile, at * each : (at + 1) * each] = jnp.where(swapped, odd, even)
                     at += kept
                     left[tile, at * each : (at + 1) * each] = jnp.where(swapped, even, odd)
-    sends = [ref.at[item] for ref in send_refs for item in range(ref.shape[0])]
+    sends = [(ref, item) for ref in send_refs for item in range(kept)]
+    ab_tiles = slots_ref.shape[0] // 2 // tiles
     exponents = [[] for _ in sends]
 
     def use(ab, total):
         for at in range(kept):
             keep_ref[at, ab] = total[at * each : (at + 1) * each]
-        for at, ref in enumerate(sends):
+        for at, (ref, item) in enumerate(sends):
             first = (kept + at) * each
             coded, exponent = code(total[first : first + each])
-            ref[ab * each : (ab + 1) * each] = coded
+            to = (item * ab_tiles + ab) * each
+            ref[to : to + each] = coded
             exponents[at].append(exponent)
 
     multiply(left, slots_ref, table_ref, use)
-    for ref, rows in zip(sends, exponents):
-        store_exponents(ref, pl.ds(len(rows) * each, 16), rows)
-
-
-def add_decoded(total, ref, ab, ab_tiles, factor):
+    for at, ref in enumerate(send_refs):
+        store_exponents(ref, sum(exponents[at * kept : (at + 1) * kept], []))
+
+
+def add_decoded(total, ref, at, factors):
     each = total.shape[0]
-    return total + decode(ref[ab * each : (ab + 1) * each], factor[ab : ab + 1])
-
-
-def tail_scales(ref, ab_tiles, each):
-    return scales(ref[pl.ds(ab_tiles * each, 16)])
-
-
-def code_into(ref, tiles):
+    return total + decode(ref[at * each : (at + 1) * each], factors[at : at + 1])
+
+
+def tail_scales(ref, blocks, each):
+    return scales(ref[blocks * each :])
+
+
+def code_into(ref, item, tiles):
     each = tiles[0].shape[0]
     exponents = []
     for ab, tile in enumerate(tiles):
         coded, exponent = code(tile)
-        ref[ab * each : (ab + 1) * each] = coded
+        at = (item * len(tiles) + ab) * each
+        ref[at : at + each] = coded
         exponents.append(exponent)
-    store_exponents(ref, pl.ds(len(tiles) * each, 16), exponents)
+    return exponents
 
 
 def x_pair_kernel(n_x, n_z, *refs):
@@ -197,12 +200,12 @@
     ab_tiles, each = sums.shape[1:3]
     at = 0
     for keep_ref, *received in (refs[:half], refs[half:]):
+        factors = [tail_scales(ref, keep_ref.shape[0] * ab_tiles, each) for ref in received]
         for item in range(keep_ref.shape[0]):
-            factors = [tail_scales(ref.at[item], ab_tiles, each) for ref in received]
             for ab in range(ab_tiles):
                 total = keep_ref[item, ab]
                 for ref, factor in zip(received, factors):
-                    total = add_decoded(total, ref.at[item], ab, ab_tiles, factor)
+                    total = add_decoded(total, ref, item * ab_tiles + ab, factor)
                 sums[at, ab] = total
             at += 1
     put_in_order(False, n_x, n_z, sums, kept_ref, sent_ref)
@@ -216,71 +219,78 @@
         wanted = z ^ (2 * m if z_first else m)
         away = lax.rem(lax.div(row, 2) - lax.div(wanted, 2) + n_y, n_y)
         places.append(away if z_first else 2 * away + lax.rem(row + wanted, 2))
+    exponents = []
     for m in range(0, len(places), 2):
         kept_ref[m // 2] = sums[places[m]]
-        code_into(sent_ref.at[m // 2], [sums[places[m + 1], ab] for ab in range(ab_tiles)])
+        exponents += code_into(sent_ref, m // 2, [sums[places[m + 1], ab] for ab in range(ab_tiles)])
+    store_exponents(sent_ref, exponents)
 
 
 def z_pair_kernel(parts, near_ref, near_received, far_ref, far_received, kept_ref, *send_refs):
     ab_tiles, each = kept_ref.shape[1:3]
     at = 0
+    exponents = [[] for _ in send_refs]
     for keep_ref, received in ((near_ref, near_received), (far_ref, far_received)):
+        factor = tail_scales(received, keep_ref.shape[0] * ab_tiles, each)
         for item in range(keep_ref.shape[0]):
-            factor = tail_scales(received.at[item], ab_tiles, each)
-            tiles = [add_decoded(keep_ref[item, ab], received.at[item], ab, ab_tiles, factor) for ab in range(ab_tiles)]
+            tiles = [
+                add_decoded(keep_ref[item, ab], received, item * ab_tiles + ab, factor) for ab in range(ab_tiles)
+            ]
             part = item % parts
             if part:
-                code_into(send_refs[part - 1].at[at], tiles)
+                exponents[part - 1] += code_into(send_refs[part - 1], at, tiles)
             else:
                 for ab in range(ab_tiles):
                     kept_ref[at, ab] = tiles[ab]
             at += part == parts - 1
+    for ref, rows in zip(send_refs, exponents):
+        store_exponents(ref, rows)
 
 
 def zx_pair_kernel(n_x, n_z, keep_ref, *refs):
     *received, kept_ref, sent_ref, sums = refs
     ab_tiles, each = sums.shape[1:3]
+    factors = [tail_scales(ref, keep_ref.shape[0] * ab_tiles, each) for ref in received]
     for item in range(keep_ref.shape[0]):
-        factors = [tail_scales(ref.at[item], ab_tiles, each) for ref in received]
         for ab in range(ab_tiles):
             total = keep_ref[item, ab]
             for ref, factor in zip(received, factors):
-                total = add_decoded(total, ref.at[item], ab, ab_tiles, factor)
+                total = add_decoded(total, ref, item * ab_tiles + ab, factor)
             sums[item, ab] = total
     put_in_order(True, n_x, n_z, sums, kept_ref, sent_ref)
 
 
 def halve_kernel(kept_ref, received_ref, next_ref, sent_ref):
-    count, ab_tiles, each, width = kept_ref.shape
+    count, ab_tiles, each, _ = kept_ref.shape
+    factor = tail_scales(received_ref, count * ab_tiles, each)
+    exponents = []
     for item in range(count):
-        factor = tail_scales(received_ref.at[item], ab_tiles, each)
         tiles = [
-            add_decoded(kept_ref[item, ab], received_ref.at[item], ab, ab_tiles, factor) for ab in range(ab_tiles)
+            add_decoded(kept_ref[item, ab], received_ref, item * ab_tiles + ab, factor) for ab in range(ab_tiles)
         ]
         if item % 2:
-            code_into(sent_ref.at[item // 2], tiles)
+            exponents += code_into(sent_ref, item // 2, tiles)
         else:
             for ab in range(ab_tiles):
                 next_ref[item // 2, ab] = tiles[ab]
+    store_exponents(sent_ref, exponents)
 
 
 def last_kernel(*refs):
-    flat, out_ref = refs[-1], refs[-2]
-    rows, ab_tiles, width = out_ref.shape
-    lanes = flat.shape[2]
+    *ready_refs, kept_ref, received_ref, out_ref, flat = refs
+    each, ab_tiles, lanes = kept_ref.shape[2], out_ref.shape[1], flat.shape[2]
     start = 0
-    for kept_ref, received_ref in zip(refs[:-2:2], refs[1:-2:2]):
-        each = kept_ref.shape[2]
-        factor = tail_scales(received_ref.at[0], ab_tiles, each)
-        for ab in range(ab_tiles):
-            total = add_decoded(kept_ref[0, ab], received_ref.at[0], ab, ab_tiles, factor)
-            for half in range(width // lanes):
-                piece = total[:, half * lanes : (half + 1) * lanes]
-                flat[half, pl.ds(start * ab_tiles + ab, each, stride=ab_tiles), :] = piece
-        start += each
-    for half in range(width // lanes):
-        whole = flat[half].reshape(rows, ab_tiles, lanes)
-        out_ref[:, :, pl.ds(half * lanes, lanes)] = whole.astype(out_ref.dtype)
+    for ready_ref in ready_refs:
+        out_ref[start : start + ready_ref.shape[0]] = ready_ref[...]
+        start += ready_ref.shape[0]
+    factor = tail_scales(received_ref, ab_tiles, each)
+    for ab in range(ab_tiles):
+        total = add_decoded(kept_ref[0, ab], received_ref, ab, factor)
+        for half in range(out_ref.shape[2] // lanes):
+            flat[half, pl.ds(ab, each, stride=ab_tiles), :] = total[:, half * lanes : (half + 1) * lanes]
+    for half in range(out_ref.shape[2] // lanes):
+        whole = flat[half].reshape(each, ab_tiles, lanes)
+        out_ref[start : start + each, :, pl.ds(half * lanes, lanes)] = whole.astype(out_ref.dtype)
 
 
 def shards(n_row, n_col, amps, ints, task_cd, task_ab, task_count):
@@ -306,8 +316,9 @@
     def along_z(array, bit):
         return lax.ppermute(array, "col", [(c, (c // n_x ^ bit) * n_x + c % n_x) for c in range(n_col)])
 
-    def coded(each, *lead):
-        return pltpu.VMEM((*lead, PAIR_TILES_ROW * each + 16, width), I16)
+    def coded(each, count):
+        blocks = count * PAIR_TILES_ROW
+        return pltpu.VMEM((blocks * each + -(-blocks // 16) * 16, width), I16)
 
     def summed(each, *lead):
         return pltpu.VMEM((*lead, PAIR_TILES_ROW, each, width), F32)
@@ -375,6 +386,16 @@
             received = along_z(sent, bit)
         return [kept, received]
 
+    def finish(place, kept, received, *ready):
+        each = kept.shape[2]
+        return kernel_call(
+            last_kernel,
+            place((each + sum(v.shape[0] for v in ready), PAIR_TILES_ROW, width), BF16),
+            [IN_VMEM] * (len(ready) + 2),
+            [pltpu.VMEM((width // LANES, each * PAIR_TILES_ROW, LANES), F32)],
+            name="last",
+        )(*ready, held(kept), held(received))
+
     near_keep, *sends = products([mine[0], beside[0]], True)
     near_received = over_x(sends)
     near_zkeep, send = products([after(mine[1], near_keep), beside[1]], False)
@@ -395,7 +416,7 @@
         name="x_pairs",
         hint=HINT,
     )(*map(held, [near_keep, *near_received, far_keep, *far_received]))
-    last = reduce_z(kept, sent, 1)
+    ready = finish(pltpu.VMEM, *reduce_z(kept, sent, 1))
     kept, *sends = kernel_call(
         functools.partial(z_pair_kernel, n_x),
         [summed(second, n_y)] + [coded(second, n_y)] * (n_x - 1),
@@ -409,14 +430,7 @@
         [summed(second, n_y)],
         name="zx_pairs",
     )(*map(held, [kept, *over_x(sends)]))
-    last += reduce_z(kept, sent, 2)
-    return kernel_call(
-        last_kernel,
-        jax.ShapeDtypeStruct((out_rows, PAIR_TILES_ROW, width), BF16),
-        [IN_VMEM] * len(last),
-        [pltpu.VMEM((width // LANES, out_rows * PAIR_TILES_ROW, LANES), F32)],
-        name="last",
-    )(*map(held, last))
+    return finish(jax.ShapeDtypeStruct, *reduce_z(kept, sent, 2), held(ready))
 
 
 def solution(mesh):

time: 53.3 us -> 53.4 us (level)
  starting transfers between devices: 18.4 us -> 17.7 us
  Pallas kernels: 12.1 us -> 12.7 us
    ppermute x5, waiting for transfers between devices: 15.6 us -> 16.4 us  [along_z(): lax.ppermute(array, 'col', [(c, (c // n_x ^ bit) * n_x + c % n_x) for c i...]
    ppermute x3, waiting for transfers between devices: 3.95 us -> 3.14 us  [along_x(): return lax.ppermute(array, 'col', pairs)]
    pallas_call x4, Pallas kernels: 5.25 us -> 5.85 us  [products(): kernel_call(functools.partial(product_kernel, count, x_first), outs, [IN_...]
  transfers between devices with their start and end apart: 14 -> 14, of which waited for: 8 -> 8; matrix products, arithmetic and copies ran while one was open for 0% -> 0% of each run, Pallas kernels for 19% -> 20%
where the time goes in v5:
time: 53.4 us; the launch traced here: 53.2 us
  waiting for transfers between devices  22.1 us (41%)
  starting transfers between devices  17.7 us (33%)
  Pallas kernels  12.7 us (24%)
  between operations  0.76 us (1%)
    ppermute x5, waiting for transfers between devices, along_z(): lax.ppermute(array, 'col', [(c, (c // n_x ^ bit) * n_x + c % n_x) for c i...  16.4 us
    ppermute x5, starting transfers between devices, along_z(): lax.ppermute(array, 'col', [(c, (c // n_x ^ bit) * n_x + c % n_x) for c i...  9.93 us
    pallas_call x4, Pallas kernels, products(): kernel_call(functools.partial(product_kernel, count, x_first), outs, [IN_...  5.85 us
    ppermute x2, starting transfers between devices, along_y(): lax.ppermute(array, 'row', [(r, (r + 2 * step) % n_row) for r in range(n_...  4.03 us
    pallas_call x1, Pallas kernels, shards(): kernel_call(functools.partial(load_kernel, LOADS), [pltpu.SMEM((2 * pairs...  3.5 us
    ppermute x3, waiting for transfers between devices, along_x(): return lax.ppermute(array, 'col', pairs)  3.14 us
    ppermute x3, starting transfers between devices, along_x(): return lax.ppermute(array, 'col', pairs)  3.06 us
    ppermute x2, waiting for transfers between devices, along_y(): lax.ppermute(array, 'row', [(r, (r + 2 * step) % n_row) for r in range(n_...  2.51 us
  transfers between devices with their start and end apart: 14, of which 8 were waited for; matrix products, arithmetic and copies ran while one was open for 0% of the time, Pallas kernels for 20%

profile of v5, /device:TPU:0, one launch (start us, length us, event | category | flops | bytes accessed | tf_op | source)
XLA Modules:
  0.0 53.2 jit_solution(5366964885310213789)
XLA Ops:
  0.0 1.3 %split.1 = (bf16[2,8,32,256]{3,2,1,0:T(8,128)(2,1)S(1)}, bf16[2,8,32,256]{3,2,1,0:T(8,128)(2,1)S(1)}) custom-call(bf16[128,8,256]{2,1,0:T(8,128)(2,1)} %amps_hbm.1), custom_call_target="tpu_custom_call" | custom-call | flops 1 | bytes 1 | tf_op jit(solution)/shard_map/split/pallas_call | solution.py:342
  1.3 0.5 collective-permute-start
  1.9 0.1 collective-permute-start.3
  1.9 2.9 %collective-permute-start.2 = (bf16[2,8,32,256]{3,2,1,0:T(8,128)(2,1)S(1)}, bf16[2,8,32,256]{3,2,1,0:T(8,128)(2,1)S(1)}, u32[]{:S(2)}, u32[]{:S(2)}) collective-permute-start(bf16[2,8,32,256]{3,2,1,0:T(8,128)(2,1)S(1)} %get-tuple-element.30.refs_0_), channel_id=1, source_target_pairs={{0,16},{8,24},{16,0},{24,8},{1,17},{9,25},{17,1},{25,9},{2,18},{10... | collective-permute-start | bytes 786440 | tf_op jit(solution)/shard_map/ppermute | solution.py:307
  5.5 3.5 %load.1 = (s32[128]{0:T(128)S(4)}, bf16[64,256,256]{2,1,0:T(8,128)(2,1)S(1)}) custom-call(s32[1]{0:T(128)S(6)} %copy.6.count_ref, s32[64]{0:T(128)} %cd_hbm.1, s32[64]{0:T(128)} %ab_hbm.1, bf16[64,256,256]{2,1,0:T(8,128)(2,1)} %ints_hbm.1), custom_call_target="tpu_custom_call" | custom-call | flops 1 | bytes 1 | tf_op jit(solution)/shard_map/load/pallas_call | solution.py:355
  9.0 0.0 collective-permute-done.refs_1_
  9.0 1.4 %x_products.2 = (f32[2,8,32,256]{3,2,1,0:T(8,128)S(1)}, s16[528,256]{1,0:T(8,128)(2,1)S(1)}) custom-call(bf16[2,8,32,256]{3,2,1,0:T(8,128)(2,1)S(1)} %get-tuple-element.30.refs_0_, bf16[2,8,32,256]{3,2,1,0:T(8,128)(2,1)S(1)} %collective-permute-done.refs_1_, s32[128]{0:T(128)S(4)} %get-tuple-element.31.refs_2_, ...), custom_call_target="tpu_custom_call" | custom-call | flops 1 | bytes 1 | tf_op jit(solution)/shard_map/x_products/pallas_call | solution.py:334
  10.5 0.0 collective-permute-done.3.refs_1_
  10.5 1.5 %z_products.2 = (f32[2,8,32,256]{3,2,1,0:T(8,128)S(1)}, s16[528,256]{1,0:T(8,128)(2,1)S(1)}) custom-call(bf16[2,8,32,256]{3,2,1,0:T(8,128)(2,1)S(1)} %get-tuple-element.36.refs_0_, bf16[2,8,32,256]{3,2,1,0:T(8,128)(2,1)S(1)} %collective-permute-done.3.refs_1_, s32[128]{0:T(128)S(4)} %get-tuple-element.31.refs_2_, ...), custom_call_target="tpu_custom_call" | custom-call | flops 1 | bytes 1 | tf_op jit(solution)/shard_map/z_products/pallas_call | solution.py:334
  12.0 0.0 collective-permute-done.2.refs_0_
  12.0 0.1 collective-permute-start.4
  12.1 1.1 %collective-permute-start.9 = (bf16[2,8,32,256]{3,2,1,0:T(8,128)(2,1)S(1)}, bf16[2,8,32,256]{3,2,1,0:T(8,128)(2,1)S(1)}, u32[]{:S(2)}, u32[]{:S(2)}) collective-permute-start(bf16[2,8,32,256]{3,2,1,0:T(8,128)(2,1)S(1)} %get-tuple-element.36.refs_0_), channel_id=1, source_target_pairs={{0,16},{8,24},{16,0},{24,8},{1,17},{9,25},{17,1},{25,9},{2,18},{10... | collective-permute-start | bytes 786440 | tf_op jit(solution)/shard_map/ppermute | solution.py:307
  13.2 1.5 %collective-permute-start.1 = (s16[528,256]{1,0:T(8,128)(2,1)S(1)}, s16[528,256]{1,0:T(8,128)(2,1)S(1)}, u32[]{:S(2)}, u32[]{:S(2)}) collective-permute-start(s16[528,256]{1,0:T(8,128)(2,1)S(1)} %get-tuple-element.34), channel_id=1, source_target_pairs={{0,1},{1,0},{2,3},{3,2},{4,5},{5,4},{6,7},{7,6},{8,9},{9,8},{10,11... | collective-permute-start | bytes 811016 | tf_op jit(solution)/shard_map/ppermute | solution.py:314
  14.7 1.6 %collective-permute-start.8 = (s16[528,256]{1,0:T(8,128)(2,1)S(1)}, s16[528,256]{1,0:T(8,128)(2,1)S(1)}, u32[]{:S(2)}, u32[]{:S(2)}) collective-permute-start(s16[528,256]{1,0:T(8,128)(2,1)S(1)} %get-tuple-element.45), channel_id=1, source_target_pairs={{0,2},{1,3},{2,0},{3,1},{4,6},{5,7},{6,4},{7,5},{8,10},{9,11},{10,... | collective-permute-start | bytes 811016 | tf_op jit(solution)/shard_map/ppermute | solution.py:317
  16.2 0.0 collective-permute-done.4.refs_1_
  16.2 1.5 %x_products.3 = (f32[2,8,32,256]{3,2,1,0:T(8,128)S(1)}, s16[528,256]{1,0:T(8,128)(2,1)S(1)}) custom-call(bf16[2,8,32,256]{3,2,1,0:T(8,128)(2,1)S(1)} %collective-permute-done.2.refs_0_, bf16[2,8,32,256]{3,2,1,0:T(8,128)(2,1)S(1)} %collective-permute-done.4.refs_1_, s32[128]{0:T(128)S(4)} %get-tuple-element.31.refs_2_, ...), custom_call_target="tpu_custom_call" | custom-call | flops 1 | bytes 1 | tf_op jit(solution)/shard_map/x_products/pallas_call | solution.py:334
  17.7 0.6 %collective-permute-start.5 = (s16[528,256]{1,0:T(8,128)(2,1)S(1)}, s16[528,256]{1,0:T(8,128)(2,1)S(1)}, u32[]{:S(2)}, u32[]{:S(2)}) collective-permute-start(s16[528,256]{1,0:T(8,128)(2,1)S(1)} %get-tuple-element.40), channel_id=1, source_target_pairs={{0,1},{1,0},{2,3},{3,2},{4,5},{5,4},{6,7},{7,6},{8,9},{9,8},{10,11... | collective-permute-start | bytes 811016 | tf_op jit(solution)/shard_map/ppermute | solution.py:314
  18.3 2.5 %collective-permute-done.9.refs_0_ = bf16[2,8,32,256]{3,2,1,0:T(8,128)(2,1)S(1)} collective-permute-done((bf16[2,8,32,256]{3,2,1,0:T(8,128)(2,1)S(1)}, bf16[2,8,32,256]{3,2,1,0:T(8,128)(2,1)S(1)}, u32[]{:S(2)}, u32[]{:S(2)}) %collective-permute-start.9) | collective-permute-done | bytes 262176 | tf_op jit(solution)/shard_map/ppermute | solution.py:307
  20.8 0.0 collective-permute-start.10
  20.8 1.7 %collective-permute-done.1.refs_1_ = s16[528,256]{1,0:T(8,128)(2,1)S(1)} collective-permute-done((s16[528,256]{1,0:T(8,128)(2,1)S(1)}, s16[528,256]{1,0:T(8,128)(2,1)S(1)}, u32[]{:S(2)}, u32[]{:S(2)}) %collective-permute-start.1) | collective-permute-done | bytes 270368 | tf_op jit(solution)/shard_map/ppermute | solution.py:314
  22.5 0.5 collective-permute-done.8.near_received
  23.0 0.0 collective-permute-done.10.refs_1_
  23.0 1.5 %z_products.3 = (f32[2,8,32,256]{3,2,1,0:T(8,128)S(1)}, s16[528,256]{1,0:T(8,128)(2,1)S(1)}) custom-call(bf16[2,8,32,256]{3,2,1,0:T(8,128)(2,1)S(1)} %collective-permute-done.9.refs_0_, bf16[2,8,32,256]{3,2,1,0:T(8,128)(2,1)S(1)} %collective-permute-done.10.refs_1_, s32[128]{0:T(128)S(4)} %get-tuple-element.31.refs_2_, ...), custom_call_target="tpu_custom_call" | custom-call | flops 1 | bytes 1 | tf_op jit(solution)/shard_map/z_products/pallas_call | solution.py:334
  24.5 1.6 %collective-permute-start.11 = (s16[528,256]{1,0:T(8,128)(2,1)S(1)}, s16[528,256]{1,0:T(8,128)(2,1)S(1)}, u32[]{:S(2)}, u32[]{:S(2)}) collective-permute-start(s16[528,256]{1,0:T(8,128)(2,1)S(1)} %get-tuple-element.50), channel_id=1, source_target_pairs={{0,2},{1,3},{2,0},{3,1},{4,6},{5,7},{6,4},{7,5},{8,10},{9,11},{10,... | collective-permute-start | bytes 811016 | tf_op jit(solution)/shard_map/ppermute | solution.py:317
  26.1 1.5 %collective-permute-done.5.refs_3_ = s16[528,256]{1,0:T(8,128)(2,1)S(1)} collective-permute-done((s16[528,256]{1,0:T(8,128)(2,1)S(1)}, s16[528,256]{1,0:T(8,128)(2,1)S(1)}, u32[]{:S(2)}, u32[]{:S(2)}) %collective-permute-start.5) | collective-permute-done | bytes 270368 | tf_op jit(solution)/shard_map/ppermute | solution.py:314
  27.6 0.4 x_pairs.1
  28.0 1.6 %collective-permute-start.6 = (s16[528,256]{1,0:T(8,128)(2,1)S(1)}, s16[528,256]{1,0:T(8,128)(2,1)S(1)}, u32[]{:S(2)}, u32[]{:S(2)}) collective-permute-start(s16[528,256]{1,0:T(8,128)(2,1)S(1)} %get-tuple-element.42), channel_id=1, source_target_pairs={{0,2},{1,3},{2,0},{3,1},{4,6},{5,7},{6,4},{7,5},{8,10},{9,11},{10,... | collective-permute-start | bytes 811016 | tf_op jit(solution)/shard_map/ppermute | solution.py:317
  29.6 4.3 %collective-permute-done.11.far_received = s16[528,256]{1,0:T(8,128)(2,1)S(1)} collective-permute-done((s16[528,256]{1,0:T(8,128)(2,1)S(1)}, s16[528,256]{1,0:T(8,128)(2,1)S(1)}, u32[]{:S(2)}, u32[]{:S(2)}) %collective-permute-start.11) | collective-permute-done | bytes 270368 | tf_op jit(solution)/shard_map/ppermute | solution.py:317
  34.0 0.3 z_pairs.1
  34.3 1.0 %collective-permute-start.12 = (s16[528,256]{1,0:T(8,128)(2,1)S(1)}, s16[528,256]{1,0:T(8,128)(2,1)S(1)}, u32[]{:S(2)}, u32[]{:S(2)}) collective-permute-start(s16[528,256]{1,0:T(8,128)(2,1)S(1)} %get-tuple-element.52), channel_id=1, source_target_pairs={{0,1},{1,0},{2,3},{3,2},{4,5},{5,4},{6,7},{7,6},{8,9},{9,8},{10,11... | collective-permute-start | bytes 811016 | tf_op jit(solution)/shard_map/ppermute | solution.py:314
  35.2 3.0 %collective-permute-done.6.received_ref = s16[528,256]{1,0:T(8,128)(2,1)S(1)} collective-permute-done((s16[528,256]{1,0:T(8,128)(2,1)S(1)}, s16[528,256]{1,0:T(8,128)(2,1)S(1)}, u32[]{:S(2)}, u32[]{:S(2)}) %collective-permute-start.6) | collective-permute-done | bytes 270368 | tf_op jit(solution)/shard_map/ppermute | solution.py:317
  38.2 0.2 halve.1
  38.4 2.7 %collective-permute-start.7 = (s16[272,256]{1,0:T(8,128)(2,1)S(1)}, s16[272,256]{1,0:T(8,128)(2,1)S(1)}, u32[]{:S(2)}, u32[]{:S(2)}) collective-permute-start(s16[272,256]{1,0:T(8,128)(2,1)S(1)} %get-tuple-element.44), channel_id=1, source_target_pairs={{0,4},{1,5},{2,6},{3,7},{4,0},{5,1},{6,2},{7,3},{8,12},{9,13},{10,... | collective-permute-start | bytes 417800 | tf_op jit(solution)/shard_map/ppermute | solution.py:317
  41.0 0.0 collective-permute-done.12.refs_0_
  41.0 0.2 zx_pairs.1
  41.3 2.4 %collective-permute-start.13 = (s16[272,256]{1,0:T(8,128)(2,1)S(1)}, s16[272,256]{1,0:T(8,128)(2,1)S(1)}, u32[]{:S(2)}, u32[]{:S(2)}) collective-permute-start(s16[272,256]{1,0:T(8,128)(2,1)S(1)} %get-tuple-element.54), channel_id=1, source_target_pairs={{0,4},{1,5},{2,6},{3,7},{4,0},{5,1},{6,2},{7,3},{8,12},{9,13},{10,... | collective-permute-start | bytes 417800 | tf_op jit(solution)/shard_map/ppermute | solution.py:317
  43.7 6.9 %collective-permute-done.7.refs_1_ = s16[272,256]{1,0:T(8,128)(2,1)S(1)} collective-permute-done((s16[272,256]{1,0:T(8,128)(2,1)S(1)}, s16[272,256]{1,0:T(8,128)(2,1)S(1)}, u32[]{:S(2)}, u32[]{:S(2)}) %collective-permute-start.7) | collective-permute-done | bytes 139296 | tf_op jit(solution)/shard_map/ppermute | solution.py:317
  50.6 0.1 last.2.refs_0_
  50.7 1.7 %collective-permute-done.13.refs_2_ = s16[272,256]{1,0:T(8,128)(2,1)S(1)} collective-permute-done((s16[272,256]{1,0:T(8,128)(2,1)S(1)}, s16[272,256]{1,0:T(8,128)(2,1)S(1)}, u32[]{:S(2)}, u32[]{:S(2)}) %collective-permute-start.13) | collective-permute-done | bytes 139296 | tf_op jit(solution)/shard_map/ppermute | solution.py:317
  52.4 0.8 %last.3 = bf16[64,8,256]{2,1,0:T(8,128)(2,1)} custom-call(bf16[32,8,256]{2,1,0:T(8,128)(2,1)S(1)} %last.2.refs_0_, f32[1,8,32,256]{3,2,1,0:T(8,128)S(1)} %get-tuple-element.53.refs_1_, s16[272,256]{1,0:T(8,128)(2,1)S(1)} %collective-permute-done.13.refs_2_), custom_call_target="tpu_custom_call" | custom-call | flops 1 | bytes 1 | tf_op jit(solution)/shard_map/last/pallas_call | solution.py:391
Async XLA Ops:
  1.3 7.7 %collective-permute-start = (bf16[2,8,32,256]{3,2,1,0:T(8,128)(2,1)S(1)}, bf16[2,8,32,256]{3,2,1,0:T(8,128)(2,1)S(1)}, u32[]{:S(2)}, u32[]{:S(2)}) collective-permute-start(bf16[2,8,32,256]{3,2,1,0:T(8,128)(2,1)S(1)} %get-tuple-element.30.refs_0_), channel_id=1, source_target_pairs={{0,8},{8,0},{16,24},{24,16},{1,9},{9,1},{17,25},{25,17},{2,10},{10... | collective-permute-start | bytes 786440 | tf_op jit(solution)/shard_map/ppermute | solution.py:310
  1.9 8.6 %collective-permute-start.3 = (bf16[2,8,32,256]{3,2,1,0:T(8,128)(2,1)S(1)}, bf16[2,8,32,256]{3,2,1,0:T(8,128)(2,1)S(1)}, u32[]{:S(2)}, u32[]{:S(2)}) collective-permute-start(bf16[2,8,32,256]{3,2,1,0:T(8,128)(2,1)S(1)} %get-tuple-element.36.refs_0_), channel_id=1, source_target_pairs={{0,8},{8,0},{16,24},{24,16},{1,9},{9,1},{17,25},{25,17},{2,10},{10... | collective-permute-start | bytes 786440 | tf_op jit(solution)/shard_map/ppermute | solution.py:310
  1.9 10.1 %collective-permute-start.2 = (bf16[2,8,32,256]{3,2,1,0:T(8,128)(2,1)S(1)}, bf16[2,8,32,256]{3,2,1,0:T(8,128)(2,1)S(1)}, u32[]{:S(2)}, u32[]{:S(2)}) collective-permute-start(bf16[2,8,32,256]{3,2,1,0:T(8,128)(2,1)S(1)} %get-tuple-element.30.refs_0_), channel_id=1, source_target_pairs={{0,16},{8,24},{16,0},{24,8},{1,17},{9,25},{17,1},{25,9},{2,18},{10... | collective-permute-start | bytes 786440 | tf_op jit(solution)/shard_map/ppermute | solution.py:307
  12.0 4.2 %collective-permute-start.4 = (bf16[2,8,32,256]{3,2,1,0:T(8,128)(2,1)S(1)}, bf16[2,8,32,256]{3,2,1,0:T(8,128)(2,1)S(1)}, u32[]{:S(2)}, u32[]{:S(2)}) collective-permute-start(bf16[2,8,32,256]{3,2,1,0:T(8,128)(2,1)S(1)} %collective-permute-done.2.refs_0_), channel_id=1, source_target_pairs={{0,8},{8,0},{16,24},{24,16},{1,9},{9,1},{17,25},{25,17},{2,10},{10... | collective-permute-start | bytes 786440 | tf_op jit(solution)/shard_map/ppermute | solution.py:310
  12.1 8.7 %collective-permute-start.9 = (bf16[2,8,32,256]{3,2,1,0:T(8,128)(2,1)S(1)}, bf16[2,8,32,256]{3,2,1,0:T(8,128)(2,1)S(1)}, u32[]{:S(2)}, u32[]{:S(2)}) collective-permute-start(bf16[2,8,32,256]{3,2,1,0:T(8,128)(2,1)S(1)} %get-tuple-element.36.refs_0_), channel_id=1, source_target_pairs={{0,16},{8,24},{16,0},{24,8},{1,17},{9,25},{17,1},{25,9},{2,18},{10... | collective-permute-start | bytes 786440 | tf_op jit(solution)/shard_map/ppermute | solution.py:307
  13.2 9.3 %collective-permute-start.1 = (s16[528,256]{1,0:T(8,128)(2,1)S(1)}, s16[528,256]{1,0:T(8,128)(2,1)S(1)}, u32[]{:S(2)}, u32[]{:S(2)}) collective-permute-start(s16[528,256]{1,0:T(8,128)(2,1)S(1)} %get-tuple-element.34), channel_id=1, source_target_pairs={{0,1},{1,0},{2,3},{3,2},{4,5},{5,4},{6,7},{7,6},{8,9},{9,8},{10,11... | collective-permute-start | bytes 811016 | tf_op jit(solution)/shard_map/ppermute | solution.py:314
  14.7 8.3 %collective-permute-start.8 = (s16[528,256]{1,0:T(8,128)(2,1)S(1)}, s16[528,256]{1,0:T(8,128)(2,1)S(1)}, u32[]{:S(2)}, u32[]{:S(2)}) collective-permute-start(s16[528,256]{1,0:T(8,128)(2,1)S(1)} %get-tuple-element.45), channel_id=1, source_target_pairs={{0,2},{1,3},{2,0},{3,1},{4,6},{5,7},{6,4},{7,5},{8,10},{9,11},{10,... | collective-permute-start | bytes 811016 | tf_op jit(solution)/shard_map/ppermute | solution.py:317
  17.7 9.9 %collective-permute-start.5 = (s16[528,256]{1,0:T(8,128)(2,1)S(1)}, s16[528,256]{1,0:T(8,128)(2,1)S(1)}, u32[]{:S(2)}, u32[]{:S(2)}) collective-permute-start(s16[528,256]{1,0:T(8,128)(2,1)S(1)} %get-tuple-element.40), channel_id=1, source_target_pairs={{0,1},{1,0},{2,3},{3,2},{4,5},{5,4},{6,7},{7,6},{8,9},{9,8},{10,11... | collective-permute-start | bytes 811016 | tf_op jit(solution)/shard_map/ppermute | solution.py:314
  20.8 2.2 %collective-permute-start.10 = (bf16[2,8,32,256]{3,2,1,0:T(8,128)(2,1)S(1)}, bf16[2,8,32,256]{3,2,1,0:T(8,128)(2,1)S(1)}, u32[]{:S(2)}, u32[]{:S(2)}) collective-permute-start(bf16[2,8,32,256]{3,2,1,0:T(8,128)(2,1)S(1)} %collective-permute-done.9.refs_0_), channel_id=1, source_target_pairs={{0,8},{8,0},{16,24},{24,16},{1,9},{9,1},{17,25},{25,17},{2,10},{10... | collective-permute-start | bytes 786440 | tf_op jit(solution)/shard_map/ppermute | solution.py:310
  24.5 9.5 %collective-permute-start.11 = (s16[528,256]{1,0:T(8,128)(2,1)S(1)}, s16[528,256]{1,0:T(8,128)(2,1)S(1)}, u32[]{:S(2)}, u32[]{:S(2)}) collective-permute-start(s16[528,256]{1,0:T(8,128)(2,1)S(1)} %get-tuple-element.50), channel_id=1, source_target_pairs={{0,2},{1,3},{2,0},{3,1},{4,6},{5,7},{6,4},{7,5},{8,10},{9,11},{10,... | collective-permute-start | bytes 811016 | tf_op jit(solution)/shard_map/ppermute | solution.py:317
  28.0 10.2 %collective-permute-start.6 = (s16[528,256]{1,0:T(8,128)(2,1)S(1)}, s16[528,256]{1,0:T(8,128)(2,1)S(1)}, u32[]{:S(2)}, u32[]{:S(2)}) collective-permute-start(s16[528,256]{1,0:T(8,128)(2,1)S(1)} %get-tuple-element.42), channel_id=1, source_target_pairs={{0,2},{1,3},{2,0},{3,1},{4,6},{5,7},{6,4},{7,5},{8,10},{9,11},{10,... | collective-permute-start | bytes 811016 | tf_op jit(solution)/shard_map/ppermute | solution.py:317
  34.3 6.8 %collective-permute-start.12 = (s16[528,256]{1,0:T(8,128)(2,1)S(1)}, s16[528,256]{1,0:T(8,128)(2,1)S(1)}, u32[]{:S(2)}, u32[]{:S(2)}) collective-permute-start(s16[528,256]{1,0:T(8,128)(2,1)S(1)} %get-tuple-element.52), channel_id=1, source_target_pairs={{0,1},{1,0},{2,3},{3,2},{4,5},{5,4},{6,7},{7,6},{8,9},{9,8},{10,11... | collective-permute-start | bytes 811016 | tf_op jit(solution)/shard_map/ppermute | solution.py:314
  38.4 12.2 %collective-permute-start.7 = (s16[272,256]{1,0:T(8,128)(2,1)S(1)}, s16[272,256]{1,0:T(8,128)(2,1)S(1)}, u32[]{:S(2)}, u32[]{:S(2)}) collective-permute-start(s16[272,256]{1,0:T(8,128)(2,1)S(1)} %get-tuple-element.44), channel_id=1, source_target_pairs={{0,4},{1,5},{2,6},{3,7},{4,0},{5,1},{6,2},{7,3},{8,12},{9,13},{10,... | collective-permute-start | bytes 417800 | tf_op jit(solution)/shard_map/ppermute | solution.py:317
  41.3 11.1 %collective-permute-start.13 = (s16[272,256]{1,0:T(8,128)(2,1)S(1)}, s16[272,256]{1,0:T(8,128)(2,1)S(1)}, u32[]{:S(2)}, u32[]{:S(2)}) collective-permute-start(s16[272,256]{1,0:T(8,128)(2,1)S(1)} %get-tuple-element.54), channel_id=1, source_target_pairs={{0,4},{1,5},{2,6},{3,7},{4,0},{5,1},{6,2},{7,3},{8,12},{9,13},{10,... | collective-permute-start | bytes 417800 | tf_op jit(solution)/shard_map/ppermute | solution.py:317
